TPU v7x, 128 devices: a whole 4x4x4 slice. The times are simulated.
128 devices in a mesh: seq: 32 (over z, x, core), dp: 4 (over y).
Axes of the slice: x: 4, y: 4, z: 4, core: 2. Of those that a mesh axis runs over, the one named last changes fastest.
Arguments:
- latents: bfloat16 [4, 64, 256, 1152], P('dp', 'seq'), may hold values from -24 to 24
- frame_counts: int32 [4], P('dp'), may hold values from 24 to 64, as said below
- mod_table: float32 [3, 1152], replicated, may hold values from -3 to 3
- clip_mod: float32 [4, 3, 1152], P('dp'), may hold values from -3 to 3
- q_gain: float32 [72], replicated, may hold values from 0.5 to 8
- k_gain: float32 [72], replicated, may hold values from 0.5 to 8
- w_qkv: bfloat16 [1152, 3456], replicated, may hold values from -0.1875 to 0.1875
- w_out: bfloat16 [1152, 1152], replicated, may hold values from -0.1875 to 0.1875
- cotangent: bfloat16 [4, 64, 256, 1152], P('dp', 'seq'), may hold values from -12 to 12
Outputs:
- block_out: bfloat16 [4, 64, 256, 1152], P('dp', 'seq')
- input_grad: bfloat16 [4, 64, 256, 1152], P('dp', 'seq')
- clip_mod_grad: float32 [4, 3, 1152], P('dp')
- table_grad: float32 [3, 1152], replicated
- q_gain_grad: float32 [72], replicated
- k_gain_grad: float32 [72], replicated
Inputs may be any that keep to these rules, and one draw needn't show every extreme that they name: `frame_counts`: one clip of every draw fills all 64 frame slots.
All inputs are finite; a program needn't handle non-finite values.
Results may differ from a plain program's by a relative error of at most 0.02.
The roundings to bfloat16 on the way count: a program that leaves them out, or rounds other values in their place, can miss the bound.
Values may be sent and summed in bfloat16 or wider, within the bound.
No kernel may reach another device: no remote copies, remote signals or barrier semaphores. Data moves between devices by JAX's collectives and lax.ppermute only.
A program may use at most 192 MiB of HBM per device.

v0:
```python
import jax
import jax.numpy as jnp
from jax import lax
from jax.sharding import PartitionSpec as P

EPS = 1e-06


def layer_stats(flat_rows):
    row_mean = jnp.mean(flat_rows, -1, keepdims=True)
    centred = flat_rows - row_mean
    inv_std = lax.rsqrt(jnp.mean(centred * centred, -1, keepdims=True) + EPS)
    return (centred * inv_std, inv_std)


def head_norm(shaped, gain):
    inv_rms = lax.rsqrt(jnp.mean(shaped * shaped, -1, keepdims=True) + EPS)
    normal = (shaped * inv_rms * gain).astype(jnp.bfloat16)
    return (normal, inv_rms)


def head_norm_grad(shaped, inv_rms, gain, grad_b16):
    upstream = grad_b16.astype(jnp.float32)
    gain_part = jnp.sum(upstream * shaped * inv_rms, axis=tuple(range(shaped.ndim - 1)))
    scaled = upstream * gain
    inner = jnp.mean(scaled * shaped, -1, keepdims=True)
    result = inv_rms * scaled - shaped * (inv_rms * inv_rms * inv_rms) * inner
    return (result, gain_part)


def attention_forward(query, keys, vals, key_valid, att_scale):
    scores = (
        jnp.einsum("phfd,phgd->phfg", query, keys, preferred_element_type=jnp.float32) * att_scale
    )
    scores = jnp.where(key_valid, scores, jnp.float32(-1e30))
    row_max = jnp.max(scores, -1, keepdims=True)
    raised = jnp.exp(scores - row_max)
    prob_f32 = raised / jnp.sum(raised, -1, keepdims=True)
    prob_b16 = prob_f32.astype(jnp.bfloat16)
    att_out = jnp.einsum("phfg,phgd->phfd", prob_b16, vals, preferred_element_type=jnp.float32)
    return (att_out.astype(jnp.bfloat16), prob_f32, prob_b16)


def attention_backward(query, keys, vals, grad_out, prob_f32, prob_b16, att_scale):
    grad_prob = jnp.einsum("phfd,phgd->phfg", grad_out, vals, preferred_element_type=jnp.float32)
    grad_vals = jnp.einsum(
        "phfg,phfd->phgd", prob_b16, grad_out, preferred_element_type=jnp.float32
    ).astype(jnp.bfloat16)
    delta = jnp.sum(prob_f32 * grad_prob, -1, keepdims=True)
    grad_score = (prob_f32 * (grad_prob - delta) * att_scale).astype(jnp.bfloat16)
    grad_query = jnp.einsum(
        "phfg,phgd->phfd", grad_score, keys, preferred_element_type=jnp.float32
    ).astype(jnp.bfloat16)
    grad_keys = jnp.einsum(
        "phfg,phfd->phgd", grad_score, query, preferred_element_type=jnp.float32
    ).astype(jnp.bfloat16)
    return (grad_query, grad_keys, grad_vals)


def shards(latents, frame_counts, mod_table, clip_mod, q_gain, k_gain, w_qkv, w_out, cotangent):
    local_frames, positions, width = (latents.shape[1], latents.shape[2], latents.shape[3])
    head_dim = q_gain.shape[0]
    heads = width // head_dim
    ranks = lax.axis_size("seq")
    frames = local_frames * ranks
    owned = positions // ranks
    att_scale = head_dim ** (-0.5)
    modulation = mod_table + clip_mod[0]
    mod_shift, mod_scale, mod_gate = (modulation[0], modulation[1], modulation[2])
    out_heads = w_out.reshape(heads, head_dim, width)

    def time_order(flat):
        return flat.reshape(local_frames, ranks, owned, heads, head_dim).transpose(1, 2, 3, 0, 4)

    def time_view(array):
        return array.reshape(owned, heads, frames, head_dim)

    def space_rows(array):
        return array.transpose(3, 0, 1, 2, 4).reshape(local_frames * positions, heads, head_dim)

    flat_rows = latents.reshape(-1, width).astype(jnp.float32)
    unit_rows, inv_std = layer_stats(flat_rows)
    normed = (unit_rows * (1.0 + mod_scale) + mod_shift).astype(jnp.bfloat16)
    grad_rows = cotangent.reshape(-1, width).astype(jnp.float32)
    grad_y = (grad_rows * mod_gate).astype(jnp.bfloat16)
    grad_att = lax.dot_general(
        grad_y, w_out, (((1,), (1,)), ((), ())), preferred_element_type=jnp.float32
    ).astype(jnp.bfloat16)
    key_valid = lax.iota(jnp.int32, frames) < frame_counts[0]
    projected = jnp.dot(normed, w_qkv, preferred_element_type=jnp.float32)
    q_proj = projected[:, :width].reshape(-1, heads, head_dim)
    k_proj = projected[:, width : 2 * width].reshape(-1, heads, head_dim)
    q_norm, q_inv = head_norm(q_proj, q_gain)
    k_norm, k_inv = head_norm(k_proj, k_gain)
    v_norm = projected[:, 2 * width :].astype(jnp.bfloat16)
    time_q, time_k, time_v = (
        lax.all_to_all(time_order(q_norm), "seq", split_axis=0, concat_axis=3, tiled=True),
        lax.all_to_all(time_order(k_norm), "seq", split_axis=0, concat_axis=3, tiled=True),
        lax.all_to_all(time_order(v_norm), "seq", split_axis=0, concat_axis=3, tiled=True),
    )
    head_q = time_view(time_q)
    head_k = time_view(time_k)
    head_v = time_view(time_v)
    att_out, prob_f32, prob_b16 = attention_forward(head_q, head_k, head_v, key_valid, att_scale)
    space_out = lax.all_to_all(att_out[None], "seq", split_axis=3, concat_axis=0, tiled=True)
    proj_y = jnp.einsum(
        "rphld,hdc->lrpc", space_out, out_heads, preferred_element_type=jnp.float32
    ).reshape(-1, width)
    block_out = (flat_rows + mod_gate * proj_y).astype(jnp.bfloat16).reshape(latents.shape)
    time_grad = lax.all_to_all(time_order(grad_att), "seq", split_axis=0, concat_axis=3, tiled=True)
    grad_qn, grad_kn, grad_vals = attention_backward(
        head_q, head_k, head_v, time_view(time_grad), prob_f32, prob_b16, att_scale
    )
    back_q, back_k, back_v = (
        lax.all_to_all(grad_qn[None], "seq", split_axis=3, concat_axis=0, tiled=True),
        lax.all_to_all(grad_kn[None], "seq", split_axis=3, concat_axis=0, tiled=True),
        lax.all_to_all(grad_vals[None], "seq", split_axis=3, concat_axis=0, tiled=True),
    )
    grad_q, q_part = head_norm_grad(q_proj, q_inv, q_gain, space_rows(back_q))
    grad_k, k_part = head_norm_grad(k_proj, k_inv, k_gain, space_rows(back_k))
    grad_qkv = jnp.concatenate(
        [
            grad_q.reshape(-1, width),
            grad_k.reshape(-1, width),
            space_rows(back_v).reshape(-1, width).astype(jnp.float32),
        ],
        1,
    ).astype(jnp.bfloat16)
    grad_normed = lax.dot_general(
        grad_qkv, w_qkv, (((1,), (1,)), ((), ())), preferred_element_type=jnp.float32
    ).astype(jnp.bfloat16)
    grad_h = grad_normed.astype(jnp.float32)
    grad_shift = jnp.sum(grad_h, 0)
    grad_scale = jnp.sum(grad_h * unit_rows, 0)
    grad_gate = jnp.sum(grad_rows * proj_y, 0)
    grad_unit = grad_h * (1.0 + mod_scale)
    grad_x = inv_std * (
        grad_unit
        - jnp.mean(grad_unit, -1, keepdims=True)
        - unit_rows * jnp.mean(grad_unit * unit_rows, -1, keepdims=True)
    )
    input_grad = (grad_rows + grad_x).astype(jnp.bfloat16).reshape(latents.shape)
    mod_part = jnp.stack([grad_shift, grad_scale, grad_gate])
    clip_total = lax.psum(mod_part, "seq")
    table_total, q_total, k_total = lax.psum((mod_part, q_part, k_part), ("seq", "dp"))
    return (block_out, input_grad, clip_total[None], table_total, q_total, k_total)


def solution(mesh):
    return jax.shard_map(
        shards,
        mesh=mesh,
        in_specs=(
            P("dp", "seq", None, None),
            P("dp"),
            P(),
            P("dp", None, None),
            P(),
            P(),
            P(),
            P(),
            P("dp", "seq", None, None),
        ),
        out_specs=(
            P("dp", "seq", None, None),
            P("dp", "seq", None, None),
            P("dp", None, None),
            P(),
            P(),
            P(),
        ),
        check_vma=False,
    )
```

profile of v0, /device:TPU:0, one launch (start us, length us, event | category | flops | bytes accessed | tf_op | source)
XLA Modules:
  0.0 571.6 jit_solution(9891228624355973868)
XLA Ops:
  6.8 7.4 %fusion.66 = f32[512,3456]{1,0:T(8,128)S(1)} fusion(bf16[512,1152]{1,0:T(8,128)(2,1)S(1)} %get-tuple-element.66, bf16[1152,3456]{1,0:T(8,128)(2,1)} %param.15), kind=kOutput, calls=%fused_computation.107 | convolution fusion | flops 4076863488 | bytes 16220160 | tf_op jit(solution)/shard_map/dot_general | solution.py:90
  18.2 5.8 %reshape.227 = bf16[2,32,8,16,72]{4,3,2,1,0:T(8,128)(2,1)} reshape(bf16[512,1152]{1,0:T(8,128)(2,1)} %slice.41) | data formatting | bytes 2359296 | tf_op jit(solution)/shard_map/reshape | solution.py:73
  27.5 8.4 %all-to-all-start.2 = ((bf16[32,8,16,2,72]{4,2,1,3,0:T(8,128)(2,1)}), bf16[32,8,16,2,72]{4,2,1,3,0:T(8,128)(2,1)}, u32[]{:S(2)}, u32[]{:S(2)}) async-start(bf16[32,8,16,2,72]{4,2,1,3,0:T(8,128)(2,1)} %bitcast.163), calls=%async_computation.2 | async-start | bytes 4194304 | tf_op jit(solution)/shard_map/all_to_all | solution.py:99
  40.8 6.1 %reshape.221 = f32[2,32,8,16,72]{4,3,2,1,0:T(8,128)} reshape(f32[512,1152]{1,0:T(8,128)} %get-tuple-element.51) | data formatting | bytes 4718592 | tf_op jit(solution)/shard_map/reshape | solution.py:91
  56.9 8.9 %all-to-all-done.2 = bf16[32,8,16,2,72]{4,2,1,3,0:T(8,128)(2,1)} async-done(((bf16[32,8,16,2,72]{4,2,1,3,0:T(8,128)(2,1)}), bf16[32,8,16,2,72]{4,2,1,3,0:T(8,128)(2,1)}, u32[]{:S(2)}, u32[]{:S(2)}) %all-to-all-start.2) | async-done | bytes 1179680 | tf_op jit(solution)/shard_map/all_to_all | solution.py:99
  70.6 6.2 %reshape.224 = f32[2,32,8,16,72]{4,3,2,1,0:T(8,128)} reshape(f32[512,1152]{1,0:T(8,128)} %get-tuple-element.50) | data formatting | bytes 4718592 | tf_op jit(solution)/shard_map/reshape | solution.py:92
  86.8 13.8 %all-to-all-done = bf16[32,8,16,2,72]{4,2,1,3,0:T(8,128)(2,1)} async-done(((bf16[32,8,16,2,72]{4,2,1,3,0:T(8,128)(2,1)}), bf16[32,8,16,2,72]{4,2,1,3,0:T(8,128)(2,1)}, u32[]{:S(2)}, u32[]{:S(2)}) %all-to-all-start) | async-done | bytes 1179680 | tf_op jit(solution)/shard_map/all_to_all | solution.py:97
  110.5 5.8 %reshape.231 = bf16[2,32,8,16,72]{4,3,2,1,0:T(8,128)(2,1)} reshape(bf16[512,1152]{1,0:T(8,128)(2,1)} %convolution_convert_fusion) | data formatting | bytes 2359296 | tf_op jit(solution)/shard_map/reshape | solution.py:73
  119.8 15.8 %all-to-all-done.1 = bf16[32,8,16,2,72]{4,2,1,3,0:T(8,128)(2,1)} async-done(((bf16[32,8,16,2,72]{4,2,1,3,0:T(8,128)(2,1)}), bf16[32,8,16,2,72]{4,2,1,3,0:T(8,128)(2,1)}, u32[]{:S(2)}, u32[]{:S(2)}) %all-to-all-start.1) | async-done | bytes 1179680 | tf_op jit(solution)/shard_map/all_to_all | solution.py:98
  140.4 5.2 copy.132
  155.7 5.8 %fusion.63 = (f32[8,16,64]{2,1,0:T(8,128)S(1)}, f32[8,16,64,64]{2,3,1,0:T(8,128)}) fusion(pred[64]{0:T(512)(128)(4,1)S(1)} %iota_compare_fusion, bf16[8,16,64,72]{3,2,1,0:T(8,128)(2,1)} %bitcast.171, bf16[8,16,64,72]{3,2,1,0:T(8,128)(2,1)} %bitcast.169), kind=kOutput, calls=%fused_computation.105 | convolution fusion | flops 77594688 | bytes 4489280 | tf_op jit(solution)/shard_map/sub | solution.py:37
  170.4 5.2 all-to-all-start.3
  184.1 9.3 %convert_bitcast_fusion.2 = bf16[1,8,16,64,72]{4,3,2,1,0:T(8,128)(2,1)} fusion(bf16[8,16,64,72]{3,2,1,0:T(8,128)(2,1)} %bitcast.172, f32[8,16,64,64]{2,3,1,0:T(8,128)} %fusion.67, f32[8,16,64,64]{2,3,1,0:T(8,128)} %get-tuple-element.61, f32[8,16,64]{2,1,0:T(8,128)S(1)} %get-tuple-element.60), kind=kOutput, calls=%fused_computation.64 | convolution fusion | flops 79765568 | bytes 6586368 | tf_op jit(solution)/shard_map/phfg,phfd->phgd/dot_general | solution.py:54
  197.8 7.8 %all-to-all-done.3 = bf16[1,8,16,64,72]{4,2,1,0,3:T(8,128)(2,1)} async-done(((bf16[1,8,16,64,72]{4,2,1,0,3:T(8,128)(2,1)}), bf16[1,8,16,64,72]{4,2,1,0,3:T(8,128)(2,1)}, u32[]{:S(2)}, u32[]{:S(2)}) %all-to-all-start.3) | async-done | bytes 1179680 | tf_op jit(solution)/shard_map/all_to_all | solution.py:105
  229.6 9.3 %convert_bitcast_fusion.3 = bf16[1,8,16,64,72]{4,3,2,1,0:T(8,128)(2,1)} fusion(bf16[8,16,64,72]{3,2,1,0:T(8,128)(2,1)} %bitcast.170, f32[8,16,64,64]{2,3,1,0:T(8,128)} %fusion.67, f32[8,16,64,64]{2,3,1,0:T(8,128)} %get-tuple-element.61, f32[8,16,64]{2,1,0:T(8,128)S(1)} %get-tuple-element.60), kind=kOutput, calls=%fused_computation.65 | convolution fusion | flops 79765568 | bytes 6586368 | tf_op jit(solution)/shard_map/phfg,phgd->phfd/dot_general | solution.py:51
  243.3 7.4 %all-to-all-start.5 = ((bf16[1,8,16,64,72]{4,2,1,0,3:T(8,128)(2,1)}), bf16[1,8,16,64,72]{4,2,1,0,3:T(8,128)(2,1)}, u32[]{:S(2)}, u32[]{:S(2)}) async-start(bf16[1,8,16,64,72]{4,2,1,0,3:T(8,128)(2,1)} %copy.140), calls=%async_computation.5 | async-start | bytes 4194304 | tf_op jit(solution)/shard_map/all_to_all | solution.py:115
  262.7 17.9 %all-to-all-done.5 = bf16[1,8,16,64,72]{4,2,1,0,3:T(8,128)(2,1)} async-done(((bf16[1,8,16,64,72]{4,2,1,0,3:T(8,128)(2,1)}), bf16[1,8,16,64,72]{4,2,1,0,3:T(8,128)(2,1)}, u32[]{:S(2)}, u32[]{:S(2)}) %all-to-all-start.5) | async-done | bytes 1179680 | tf_op jit(solution)/shard_map/all_to_all | solution.py:115
  303.7 11.7 %all-to-all-done.7 = bf16[1,8,16,64,72]{4,2,1,0,3:T(8,128)(2,1)} async-done(((bf16[1,8,16,64,72]{4,2,1,0,3:T(8,128)(2,1)}), bf16[1,8,16,64,72]{4,2,1,0,3:T(8,128)(2,1)}, u32[]{:S(2)}, u32[]{:S(2)}) %all-to-all-start.7) | async-done | bytes 1179680 | tf_op jit(solution)/shard_map/all_to_all | solution.py:117
  323.6 5.2 reshape.238
  328.8 5.2 reshape.236
  359.8 8.6 %multiply_reduce_fusion.1 = (f32[1152]{0:T(1024)S(1)}, f32[1152]{0:T(1024)S(1)}, bf16[512,1152]{1,0:T(8,128)(2,1)S(1)}, bf16[512,1152]{1,0:T(8,128)(2,1)S(1)}) fusion(f32[512,1152]{1,0:T(8,128)} %copy.148, f32[512,1152]{1,0:T(8,128)} %reshape.238, f32[512,3456]{1,0:T(8,128)} %copy-done.4, f32[512,1152]{1,0:T(8,128)} %copy.142, f32[512,1152]{1,0:T(8,128)} %reshape.236, ...), kind=kLoop, calls=%fused_computation.46 | loop fusion | flops 10614528 | bytes 25970688 | tf_op jit(solution)/shard_map/reduce_sum | solution.py:24
  368.4 9.3 %fusion.27 = (f32[1152]{0:T(1024)S(1)}, f32[512]{0:T(512)S(1)}, f32[512]{0:T(512)S(1)}, f32[1152]{0:T(1024)S(1)}, bf16[512,1152]{1,0:T(8,128)(2,1)}) fusion(bf16[1,2,256,1152]{3,2,1,0:T(8,128)(2,1)S(1)} %copy-done.3, f32[512]{0:T(512)S(1)} %bitcast.178, f32[512]{0:T(512)S(1)} %bitcast.181, f32[1152]{0:T(1024)S(1)} %get-tuple-element.44, ...), kind=kOutput, calls=%fused_computation.34 | convolution fusion | flops 4094555136 | bytes 13882880 | tf_op jit(solution)/shard_map/dot_general | solution.py:129
  377.8 125.2 %psum.28 = f32[1,3,1152]{2,1,0:T(4,128)S(1)} all-reduce(f32[1,3,1152]{2,1,0:T(4,128)S(1)} %get-tuple-element.57), channel_id=1, replica_groups=mesh['seq'=32,'dp'=4] {'seq'}, use_global_device_ids=true, to_apply=%region_14.15 | all-reduce | flops 3456 | bytes 27648 | tf_op jit(solution)/shard_map/psum | solution.py:144
  508.1 63.0 %all-reduce = (f32[3,1152]{1,0:T(4,128)}, f32[72]{0:T(128)}, f32[72]{0:T(128)}) all-reduce(f32[3,1152]{1,0:T(4,128)S(1)} %get-tuple-element.56, f32[72]{0:T(128)S(1)} %reduce_sum.164, f32[72]{0:T(128)S(1)} %reduce_sum.167), channel_id=1, replica_groups=mesh['seq'=32,'dp'=4] {'seq','dp'}, use_global_device_ids=true, to_apply=%region_15.16 | all-reduce | flops 3600 | bytes 28800 | tf_op jit(solution)/shard_map/psum | solution.py:145
  (111 shorter events, 195.0 us)
Async XLA Ops:
  0.6 105.7 %copy-start = (bf16[1152,1152]{1,0:T(8,128)(2,1)S(1)}, bf16[1152,1152]{1,0:T(8,128)(2,1)}, u32[]{:S(2)}) copy-start(bf16[1152,1152]{1,0:T(8,128)(2,1)} %param.16) | copy-start | bytes 7962628
  0.6 4.4 copy-start.2
  0.7 4.4 copy-start.7
  14.1 2.9 copy-start.4
  27.5 38.4 %all-to-all-start.2 = ((bf16[32,8,16,2,72]{4,2,1,3,0:T(8,128)(2,1)}), bf16[32,8,16,2,72]{4,2,1,3,0:T(8,128)(2,1)}, u32[]{:S(2)}, u32[]{:S(2)}) async-start(bf16[32,8,16,2,72]{4,2,1,3,0:T(8,128)(2,1)} %bitcast.163), calls=%async_computation.2 | async-start | bytes 4194304 | tf_op jit(solution)/shard_map/all_to_all | solution.py:99
  50.0 2.2 copy-start.11
  65.8 34.7 %all-to-all-start = ((bf16[32,8,16,2,72]{4,2,1,3,0:T(8,128)(2,1)}), bf16[32,8,16,2,72]{4,2,1,3,0:T(8,128)(2,1)}, u32[]{:S(2)}, u32[]{:S(2)}) async-start(bf16[32,8,16,2,72]{4,2,1,3,0:T(8,128)(2,1)} %fusion.39), calls=%async_computation | async-start | bytes 4194304 | tf_op jit(solution)/shard_map/all_to_all | solution.py:97
  79.8 2.2 copy-start.12
  100.6 35.1 %all-to-all-start.1 = ((bf16[32,8,16,2,72]{4,2,1,3,0:T(8,128)(2,1)}), bf16[32,8,16,2,72]{4,2,1,3,0:T(8,128)(2,1)}, u32[]{:S(2)}, u32[]{:S(2)}) async-start(bf16[32,8,16,2,72]{4,2,1,3,0:T(8,128)(2,1)} %fusion.40), calls=%async_computation.1 | async-start | bytes 4194304 | tf_op jit(solution)/shard_map/all_to_all | solution.py:98
  135.6 34.7 %all-to-all-start.4 = ((bf16[32,8,16,2,72]{4,2,1,3,0:T(8,128)(2,1)}), bf16[32,8,16,2,72]{4,2,1,3,0:T(8,128)(2,1)}, u32[]{:S(2)}, u32[]{:S(2)}) async-start(bf16[32,8,16,2,72]{4,2,1,3,0:T(8,128)(2,1)} %bitcast.162), calls=%async_computation.4 | async-start | bytes 4194304 | tf_op jit(solution)/shard_map/all_to_all | solution.py:110
  170.4 35.2 %all-to-all-start.3 = ((bf16[1,8,16,64,72]{4,2,1,0,3:T(8,128)(2,1)}), bf16[1,8,16,64,72]{4,2,1,0,3:T(8,128)(2,1)}, u32[]{:S(2)}, u32[]{:S(2)}) async-start(bf16[1,8,16,64,72]{4,2,1,0,3:T(8,128)(2,1)} %copy.134), calls=%async_computation.3 | async-start | bytes 4194304 | tf_op jit(solution)/shard_map/all_to_all | solution.py:105
  175.6 5.2 copy-start.6
  179.5 1.3 copy-start.5
  205.5 37.8 %all-to-all-start.6 = ((bf16[1,8,16,64,72]{4,2,1,0,3:T(8,128)(2,1)}), bf16[1,8,16,64,72]{4,2,1,0,3:T(8,128)(2,1)}, u32[]{:S(2)}, u32[]{:S(2)}) async-start(bf16[1,8,16,64,72]{4,2,1,0,3:T(8,128)(2,1)} %copy.146), calls=%async_computation.6 | async-start | bytes 4194304 | tf_op jit(solution)/shard_map/all_to_all | solution.py:116
  243.3 37.4 %all-to-all-start.5 = ((bf16[1,8,16,64,72]{4,2,1,0,3:T(8,128)(2,1)}), bf16[1,8,16,64,72]{4,2,1,0,3:T(8,128)(2,1)}, u32[]{:S(2)}, u32[]{:S(2)}) async-start(bf16[1,8,16,64,72]{4,2,1,0,3:T(8,128)(2,1)} %copy.140), calls=%async_computation.5 | async-start | bytes 4194304 | tf_op jit(solution)/shard_map/all_to_all | solution.py:115
  257.0 2.2 copy-start.8
  280.7 34.7 %all-to-all-start.7 = ((bf16[1,8,16,64,72]{4,2,1,0,3:T(8,128)(2,1)}), bf16[1,8,16,64,72]{4,2,1,0,3:T(8,128)(2,1)}, u32[]{:S(2)}, u32[]{:S(2)}) async-start(bf16[1,8,16,64,72]{4,2,1,0,3:T(8,128)(2,1)} %copy.152), calls=%async_computation.7 | async-start | bytes 4194304 | tf_op jit(solution)/shard_map/all_to_all | solution.py:117
  298.0 4.3 copy-start.3
  298.0 4.3 copy-start.9
  359.8 8.6 %copy-start.10 = (bf16[512,1152]{1,0:T(8,128)(2,1)S(1)}, bf16[512,1152]{1,0:T(8,128)(2,1)}, u32[]{:S(2)}) copy-start(bf16[512,1152]{1,0:T(8,128)(2,1)} %convert_element_type.170) | copy-start | bytes 3538948
  503.9 67.2 %copy-start.1 = (bf16[1152,1152]{1,0:T(8,128)(2,1)S(1)}, bf16[1152,1152]{1,0:T(8,128)(2,1)}, u32[]{:S(2)}) copy-start(bf16[1152,1152]{1,0:T(8,128)(2,1)} %param.16) | copy-start | bytes 7962628
where the time goes:
time: 583 us; the launch traced here: 572 us
  blocking collectives  188 us (32%)
  local copies, waits for them, and re-layouts  150 us (26%)
  waiting for transfers between devices  78.4 us (13%)
  matrix products  59.5 us (10%)
  other arithmetic  48.3 us (8%)
  starting transfers between devices  45.2 us (8%)
    psum x1, blocking collectives, shards(): clip_total = lax.psum(mod_part, 'seq')  125 us
    psum x1, blocking collectives, shards(): lax.psum((mod_part, q_part, k_part), ('seq', 'dp'))  63 us
    convert_element_type x6, local copies, waits for them, and re-layouts, head_norm_grad(): upstream = grad_b16.astype(jnp.float32)  28.8 us
    mul x8, local copies, waits for them, and re-layouts, head_norm_grad(): result = inv_rms * scaled - shaped * (inv_rms * inv_rms * inv_rms) * inner  19.2 us
    reshape x4, local copies, waits for them, and re-layouts, time_order(): flat.reshape(local_frames, ranks, owned, heads, head_dim)  18.6 us
    all_to_all x1, waiting for transfers between devices, shards(): lax.all_to_all(grad_qn[None], 'seq', split_axis=3, concat_axis=0, tiled=T...  17.9 us
    all_to_all x1, waiting for transfers between devices, shards(): lax.all_to_all(time_order(k_norm), 'seq', split_axis=0, concat_axis=3, ti...  15.8 us
    all_to_all x1, waiting for transfers between devices, shards(): lax.all_to_all(time_order(q_norm), 'seq', split_axis=0, concat_axis=3, ti...  13.8 us
  transfers between devices with their start and end apart: 8, of which 7 were waited for; matrix products, arithmetic and copies ran while one was open for 28% of the time, Pallas kernels for 0%

commit v1 on v0

v1 whole, which is shorter than its diff:
```python
import jax
import jax.numpy as jnp
from jax import lax
from jax.experimental import pallas as pl
from jax.experimental.pallas import tpu as pltpu
from jax.sharding import PartitionSpec as P

EPS = 1e-06
F32 = jnp.float32
BF16 = jnp.bfloat16
HEAD = 72
HEADS = 16
D = HEAD * HEADS
MAIN = 64 * HEADS
REST = 8 * HEADS
TOK = 512
POS = 8
FR = 64
ROWS = 128
PAIRS = TOK // ROWS
VMEM = 56 * 1024 * 1024
NN = (((1,), (0,)), ((), ()))
NT = (((1,), (1,)), ((), ()))
TN = (((0,), (0,)), ((), ()))


def dot(a, b, dims=NN):
    return lax.dot_general(a, b, dims, preferred_element_type=F32)


def iota(shape, dim):
    return lax.broadcasted_iota(jnp.int32, shape, dim)


def one_hot(cond):
    return jnp.where(cond, jnp.float32(1), jnp.float32(0)).astype(BF16)


def source_main(col):
    return col + 8 * (col >> 6)


def source_rest(col):
    return col + 64 + 64 * (col >> 3)


def split_columns(w_ref, o_ref):
    for part in range(3):
        base = part * D
        for j in range(4):
            lo = (288 * j) // 128 * 128
            r, c = iota((384, 256), 0), iota((384, 256), 1)
            pick = one_hot(source_main(c + 256 * j) == r + lo)
            o_ref[:, part * MAIN + 256 * j : part * MAIN + 256 * (j + 1)] = dot(
                w_ref[:, base + lo : base + lo + 384], pick
            ).astype(BF16)
        r, c = iota((D, REST), 0), iota((D, REST), 1)
        pick = one_hot(source_rest(c) == r)
        o_ref[:, 3 * MAIN + part * REST : 3 * MAIN + (part + 1) * REST] = dot(
            w_ref[:, base : base + D], pick
        ).astype(BF16)


def split_rows(w_ref, o_ref):
    for j in range(4):
        lo = (288 * j) // 128 * 128
        r, c = iota((256, 384), 0), iota((256, 384), 1)
        pick = one_hot(source_main(r + 256 * j) == c + lo)
        o_ref[256 * j : 256 * (j + 1), :] = dot(pick, w_ref[lo : lo + 384, :]).astype(BF16)
    r, c = iota((REST, D), 0), iota((REST, D), 1)
    pick = one_hot(source_rest(r) == c)
    o_ref[MAIN:, :] = dot(pick, w_ref[...]).astype(BF16)


def split_weights(w_qkv, w_out):
    steps = 4
    rows = D // steps
    wq = pl.pallas_call(
        split_columns,
        grid=(steps,),
        in_specs=[pl.BlockSpec((rows, 3 * D), lambda i: (i, 0))],
        out_specs=pl.BlockSpec((rows, 3 * D), lambda i: (i, 0)),
        out_shape=jax.ShapeDtypeStruct((D, 3 * D), BF16),
        compiler_params=pltpu.CompilerParams(vmem_limit_bytes=VMEM),
        cost_estimate=pl.CostEstimate(
            flops=2 * D * D * 1200, bytes_accessed=12 * D * D, transcendentals=0
        ),
        name="split_columns",
    )(w_qkv)
    cols = D // 3
    wo = pl.pallas_call(
        split_rows,
        grid=(3,),
        in_specs=[pl.BlockSpec((D, cols), lambda i: (0, i))],
        out_specs=pl.BlockSpec((D, cols), lambda i: (0, i)),
        out_shape=jax.ShapeDtypeStruct((D, D), BF16),
        compiler_params=pltpu.CompilerParams(vmem_limit_bytes=VMEM),
        cost_estimate=pl.CostEstimate(
            flops=2 * D * D * 400, bytes_accessed=4 * D * D, transcendentals=0
        ),
        name="split_rows",
    )(w_out)
    return wq, wo


def to_positions(start):
    r, c = iota((ROWS, TOK), 0) + start, iota((ROWS, TOK), 1)
    return one_hot(c == (r & (FR - 1)) * POS + (r >> 6))


def to_frames(start):
    r, c = iota((ROWS, TOK), 0) + start, iota((ROWS, TOK), 1)
    return one_hot(c == (r & (POS - 1)) * FR + (r >> 3))


def halves(value):
    high = value.astype(BF16)
    return high, (value - high.astype(F32)).astype(BF16)


def init_segments(seg, spread):
    r, c = iota((D, REST), 0), iota((D, REST), 1)
    head = jnp.where(r < MAIN, r >> 6, (r - MAIN) >> 3)
    seg[...] = one_hot(head == (c >> 3))
    r, c = iota((2 * REST, MAIN), 0), iota((2 * REST, MAIN), 1)
    spread[...] = one_hot((r & (REST - 1)) == 8 * (c >> 6))


def head_sums(main, rest, seg):
    mh, ml = halves(main)
    rh, rl = halves(rest)
    return (
        dot(mh, seg[:MAIN, :]) + dot(ml, seg[:MAIN, :]) + dot(rh, seg[MAIN:, :]) + dot(rl, seg[MAIN:, :])
    )


def expand(per_head, spread):
    high, low = halves(per_head)
    return dot(jnp.concatenate([high, low], 1), spread[...])


def head_masks(t):
    c = iota((1, 256), 1)
    head = jnp.where(c < 128, (c >> 6) + 2 * t, (c - 128) >> 3)
    out = [one_hot(head == h) for h in (2 * t, 2 * t + 1)]
    return out


def stacked(block, masks):
    return jnp.concatenate([block * masks[0], block * masks[1]], 0)


def unit_of(ref, rows, t):
    return jnp.concatenate([ref[rows, 128 * t : 128 * (t + 1)], ref[rows, MAIN:]], 1)


def rows_of(i):
    return pl.ds(pl.multiple_of(i * ROWS, ROWS), ROWS)


def over_columns(total, body):
    def step(b, _):
        body(pl.ds(pl.multiple_of(b * 256, 256), 256))
        return 0

    lax.fori_loop(0, total // 256, step, 0)
    if total % 256:
        body(pl.ds(total // 256 * 256, total % 256))


def over_pairs(body):
    def step(i, _):
        body(i)
        return 0

    lax.fori_loop(0, PAIRS, step, 0)


def forward(
    count_ref,
    x_ref,
    mod_ref,
    gain_ref,
    wqkv_ref,
    wout_ref,
    bo_ref,
    unit_ref,
    istd_ref,
    qhat_ref,
    khat_ref,
    rq_ref,
    rk_ref,
    qn_ref,
    kn_ref,
    vn_ref,
    prob_ref,
    y_ref,
    xp,
    normed,
    proj,
    att,
    bo,
    seg,
    spread,
    bias,
):
    init_segments(seg, spread)
    r, c = iota((256, 128), 0), iota((256, 128), 1)
    valid = (((r >> 6) & 1) == (c >> 6)) & ((r & (FR - 1)) < count_ref[0])
    bias[...] = jnp.where(valid, jnp.float32(0), jnp.float32(-1e30))

    def norm(i):
        rows = rows_of(i)
        x = dot(to_positions(i * ROWS), x_ref[...])
        xp[rows, :] = x
        centred = x - jnp.mean(x, -1, keepdims=True)
        inv = lax.rsqrt(jnp.mean(centred * centred, -1, keepdims=True) + EPS)
        unit = centred * inv
        unit_ref[rows, :] = unit
        istd_ref[rows, :] = jnp.broadcast_to(inv, (ROWS, 128))
        normed[rows, :] = (unit * (1.0 + mod_ref[1:2, :]) + mod_ref[0:1, :]).astype(BF16)

    over_pairs(norm)

    def project(cols):
        proj[:, cols] = dot(normed[...], wqkv_ref[:, cols])

    over_columns(3 * D, project)

    def heads(i):
        rows = rows_of(i)
        for part, (n_ref, hat_ref, r_ref) in enumerate(
            ((qn_ref, qhat_ref, rq_ref), (kn_ref, khat_ref, rk_ref))
        ):
            main = proj[rows, part * MAIN : (part + 1) * MAIN]
            rest = proj[rows, 3 * MAIN + part * REST : 3 * MAIN + (part + 1) * REST]
            inv = lax.rsqrt(head_sums(main * main, rest * rest, seg) * (1.0 / HEAD) + EPS)
            r_ref[rows, :] = inv
            main = main * expand(inv, spread)
            rest = rest * inv
            hat_ref[rows, :MAIN] = main
            hat_ref[rows, MAIN:] = rest
            gain = gain_ref[part : part + 1, :]
            n_ref[rows, :MAIN] = (main * gain[:, :MAIN]).astype(BF16)
            n_ref[rows, MAIN:] = (rest * gain[:, MAIN:]).astype(BF16)
        vn_ref[rows, :MAIN] = proj[rows, 2 * MAIN : 3 * MAIN].astype(BF16)
        vn_ref[rows, MAIN:] = proj[rows, 3 * MAIN + 2 * REST :].astype(BF16)

    over_pairs(heads)

    def attend(i):
        rows = rows_of(i)
        total = jnp.zeros((ROWS, REST), F32)
        for t in range(HEADS // 2):
            masks = head_masks(t)
            keys = stacked(unit_of(kn_ref, rows, t), masks)
            s = dot(keys, unit_of(qn_ref, rows, t), NT) * (HEAD**-0.5) + bias[...]
            s = s.reshape(2, 128, 128)
            e = jnp.exp(s - jnp.max(s, 1, keepdims=True))
            prob = (e / jnp.sum(e, 1, keepdims=True)).reshape(256, 128)
            prob_ref[i, t] = prob
            out = dot(prob.astype(BF16), stacked(unit_of(vn_ref, rows, t), masks), TN)
            att[rows, 128 * t : 128 * (t + 1)] = out[:, :128].astype(BF16)
            total = total + out[:, 128:]
        att[rows, MAIN:] = total.astype(BF16)

    over_pairs(attend)

    def out_project(cols):
        y = dot(att[...], wout_ref[:, cols])
        y_ref[:, cols] = y
        bo[:, cols] = (xp[:, cols] + mod_ref[2:3, cols] * y).astype(BF16)

    over_columns(D, out_project)

    def emit(i):
        bo_ref[rows_of(i), :] = dot(to_frames(i * ROWS), bo[...]).astype(BF16)

    over_pairs(emit)


def backward(
    cot_ref,
    mod_ref,
    gain_ref,
    wqkv_ref,
    wout_ref,
    bo_ref,
    unit_ref,
    istd_ref,
    qhat_ref,
    khat_ref,
    rq_ref,
    rk_ref,
    qn_ref,
    kn_ref,
    vn_ref,
    prob_ref,
    y_ref,
    out_ref,
    sum_ref,
    cp,
    gy,
    gatt,
    dq,
    dk,
    dqkv,
    gn,
    ig,
    seg,
    spread,
):
    ranks = TOK // 16
    init_segments(seg, spread)
    out_ref[:, :16, :] = bo_ref[...].reshape(ranks, 16, D)
    sum_ref[...] = jnp.zeros_like(sum_ref)

    def arrive(i):
        rows = rows_of(i)
        cot = dot(to_positions(i * ROWS), cot_ref[...])
        cp[rows, :] = cot
        gy[rows, :] = (cot * mod_ref[2:3, :]).astype(BF16)
        sum_ref[2:3, :] += jnp.sum(cot * y_ref[rows, :], 0, keepdims=True)

    over_pairs(arrive)

    def grad_attention(rows256):
        gatt[:, rows256] = dot(gy[...], wout_ref[rows256, :], NT).astype(BF16)

    over_columns(D, grad_attention)

    def attend(i):
        rows = rows_of(i)
        rest_q = jnp.zeros((ROWS, REST), F32)
        rest_k = jnp.zeros((ROWS, REST), F32)
        rest_v = jnp.zeros((ROWS, REST), F32)
        for t in range(HEADS // 2):
            masks = head_masks(t)
            cols = slice(128 * t, 128 * (t + 1))
            grad = unit_of(gatt, rows, t)
            prob = prob_ref[i, t]
            dp = dot(stacked(unit_of(vn_ref, rows, t), masks), grad, NT)
            w = (prob * dp).reshape(2, 128, 128)
            delta = jnp.broadcast_to(jnp.sum(w, 1, keepdims=True), (2, 128, 128)).reshape(256, 128)
            ds = (prob * (dp - delta) * (HEAD**-0.5)).astype(BF16)
            pb = prob.astype(BF16)
            g = dot(ds, stacked(unit_of(kn_ref, rows, t), masks), TN)
            dq[rows, cols] = g[:, :128].astype(BF16)
            rest_q = rest_q + g[:, 128:]
            side = jnp.concatenate([ds[:128], ds[128:]], 1)
            g = dot(side, stacked(unit_of(qn_ref, rows, t), masks))
            dk[rows, cols] = g[:, :128].astype(BF16)
            rest_k = rest_k + g[:, 128:]
            side = jnp.concatenate([pb[:128], pb[128:]], 1)
            g = dot(side, stacked(grad, masks))
            dqkv[rows, 2 * MAIN + 128 * t : 2 * MAIN + 128 * (t + 1)] = g[:, :128].astype(BF16)
            rest_v = rest_v + g[:, 128:]
        dq[rows, MAIN:] = rest_q.astype(BF16)
        dk[rows, MAIN:] = rest_k.astype(BF16)
        dqkv[rows, 3 * MAIN + 2 * REST :] = rest_v.astype(BF16)

    over_pairs(attend)

    def heads(i):
        rows = rows_of(i)
        for part, (d_ref, hat_ref, r_ref) in enumerate(
            ((dq, qhat_ref, rq_ref), (dk, khat_ref, rk_ref))
        ):
            gain = gain_ref[part : part + 1, :]
            up = d_ref[rows, :].astype(F32)
            hat = hat_ref[rows, :]
            sum_ref[3 + part : 4 + part, :] += jnp.sum(up * hat, 0, keepdims=True)
            a = up * gain
            w = a * hat
            inner = head_sums(w[:, :MAIN], w[:, MAIN:], seg) * (1.0 / HEAD)
            inv = r_ref[rows, :]
            main = expand(inv, spread) * (a[:, :MAIN] - hat[:, :MAIN] * expand(inner, spread))
            rest = inv * (a[:, MAIN:] - hat[:, MAIN:] * inner)
            dqkv[rows, part * MAIN : (part + 1) * MAIN] = main.astype(BF16)
            dqkv[rows, 3 * MAIN + part * REST : 3 * MAIN + (part + 1) * REST] = rest.astype(BF16)

    over_pairs(heads)

    def grad_normed(rows256):
        gn[:, rows256] = dot(dqkv[...], wqkv_ref[rows256, :], NT).astype(BF16)

    over_columns(D, grad_normed)

    def layer(i):
        rows = rows_of(i)
        g = gn[rows, :].astype(F32)
        unit = unit_ref[rows, :]
        sum_ref[0:1, :] += jnp.sum(g, 0, keepdims=True)
        sum_ref[1:2, :] += jnp.sum(g * unit, 0, keepdims=True)
        u = g * (1.0 + mod_ref[1:2, :])
        first = jnp.mean(u, -1, keepdims=True)
        second = jnp.mean(u * unit, -1, keepdims=True)
        grad_x = istd_ref[rows, 0:1] * (u - first - unit * second)
        ig[rows, :] = (cp[rows, :] + grad_x).astype(BF16)

    over_pairs(layer)

    def emit(i):
        value = dot(to_frames(i * ROWS), ig[...]).astype(BF16)
        out_ref[pl.ds(i * 8, 8), 16:, :] = value.reshape(8, 16, D)

    over_pairs(emit)


def vmem_call(kernel, outs, scratch, flops, name, n_in, scalars=0):
    return pl.pallas_call(
        kernel,
        in_specs=[pl.BlockSpec(memory_space=pltpu.SMEM)] * scalars
        + [pl.BlockSpec(memory_space=pltpu.VMEM)] * (n_in - scalars),
        out_specs=[pl.BlockSpec(memory_space=pltpu.VMEM)] * len(outs),
        out_shape=[jax.ShapeDtypeStruct(s, d) for s, d in outs],
        scratch_shapes=[pltpu.VMEM(s, d) for s, d in scratch],
        compiler_params=pltpu.CompilerParams(vmem_limit_bytes=VMEM),
        cost_estimate=pl.CostEstimate(flops=flops, bytes_accessed=30_000_000, transcendentals=0),
        name=name,
    )


def sum_over(value, axis, size):
    step = 1
    while step < size:
        value = value + lax.ppermute(value, axis, [(i, i ^ step) for i in range(size)])
        step *= 2
    return value


def split_gain(gain):
    return jnp.concatenate([jnp.tile(gain[:64], HEADS), jnp.tile(gain[64:], HEADS)])


def join_gain(row):
    return jnp.concatenate(
        [row[:MAIN].reshape(HEADS, 64).sum(0), row[MAIN:].reshape(HEADS, 8).sum(0)]
    )


def shards(latents, frame_counts, mod_table, clip_mod, q_gain, k_gain, w_qkv, w_out, cotangent):
    ranks = lax.axis_size("seq")
    modulation = mod_table + clip_mod[0]
    gains = jnp.stack([split_gain(q_gain), split_gain(k_gain)])

    def exchange(rows):
        return lax.all_to_all(rows, "seq", split_axis=0, concat_axis=0, tiled=True)

    def outgoing(array):
        return array.reshape(2, ranks, POS, D).transpose(1, 0, 2, 3).reshape(ranks, 16, D)

    def incoming(array):
        return array.reshape(ranks, 2, POS, D).transpose(1, 0, 2, 3).reshape(latents.shape)

    x = exchange(outgoing(latents)).reshape(TOK, D)
    cot = exchange(outgoing(cotangent)).reshape(TOK, D)
    wqkv, wout = split_weights(w_qkv, w_out)
    tok = (TOK, D)
    saved = [
        (tok, BF16),
        (tok, F32),
        ((TOK, 128), F32),
        (tok, F32),
        (tok, F32),
        ((TOK, REST), F32),
        ((TOK, REST), F32),
        (tok, BF16),
        (tok, BF16),
        (tok, BF16),
        ((PAIRS, HEADS // 2, 256, 128), F32),
        (tok, F32),
    ]
    helpers = [((D, REST), BF16), ((2 * REST, MAIN), BF16)]
    residuals = vmem_call(
        forward,
        saved,
        [(tok, F32), (tok, BF16), ((TOK, 3 * D), F32), (tok, BF16), (tok, BF16)]
        + helpers
        + [((256, 128), F32)],
        8_000_000_000,
        "attention_forward",
        6,
        1,
    )(frame_counts, x, modulation, gains, wqkv, wout)
    out, sums = vmem_call(
        backward,
        [((ranks, 32, D), BF16), ((8, D), F32)],
        [(tok, F32)] + [(tok, BF16)] * 4 + [((TOK, 3 * D), BF16)] + [(tok, BF16)] * 2 + helpers,
        9_000_000_000,
        "attention_backward",
        5 + len(saved),
    )(cot, modulation, gains, wqkv, wout, *residuals)
    back = exchange(out)
    block_out = incoming(back[:, :16, :])
    input_grad = incoming(back[:, 16:, :])
    clip_total = sum_over(sums, "seq", ranks)
    table_total = sum_over(clip_total, "dp", lax.axis_size("dp"))
    return (
        block_out,
        input_grad,
        clip_total[None, :3],
        table_total[:3],
        join_gain(table_total[3]),
        join_gain(table_total[4]),
    )


def solution(mesh):
    return jax.shard_map(
        shards,
        mesh=mesh,
        in_specs=(
            P("dp", "seq", None, None),
            P("dp"),
            P(),
            P("dp", None, None),
            P(),
            P(),
            P(),
            P(),
            P("dp", "seq", None, None),
        ),
        out_specs=(
            P("dp", "seq", None, None),
            P("dp", "seq", None, None),
            P("dp", None, None),
            P(),
            P(),
            P(),
        ),
        check_vma=False,
    )
```

time: 583 us -> 188 us (0.32); the launches traced: 572 us -> 187 us
  blocking collectives: 188 us -> 0 us
  local copies, waits for them, and re-layouts: 150 us -> 11.3 us
  Pallas kernels: 0 us -> 93.5 us
  matrix products: 59.5 us -> 0 us
  other arithmetic: 48.3 us -> 5.14 us
  waiting for transfers between devices: 78.4 us -> 37.8 us
  starting transfers between devices: 45.2 us -> 37.6 us
    psum x2 -> x0, blocking collectives: 188 us -> none  [the longest x1 125 us: shards(): clip_total = lax.psum(mod_part, 'seq')]
    pallas_call x0 -> x4, Pallas kernels: none -> 93.5 us  [the longest x1 39.4 us: shards(): vmem_call(backward, [((ranks, 32, D), BF16), ((8, D), F32)], [(tok, F32)]...]
    all_to_all x8 -> x3, waiting for transfers between devices: 78.4 us -> 0.63 us  [exchange(): return lax.all_to_all(rows, 'seq', split_axis=0, concat_axis=0, tiled=True)]
    dot_general x9 -> x0, matrix products: 53.7 us -> none  [the longest x1 9.35 us: attention_backward(): jnp.einsum('phfg,phfd->phgd', grad_score, query, preferred_element_type=j...]
    ppermute x0 -> x7, waiting for transfers between devices: none -> 37.2 us  [sum_over(): lax.ppermute(value, axis, [(i, i ^ step) for i in range(size)])]
    convert_element_type x7 -> x0, local copies, waits for them, and re-layouts: 33.4 us -> none  [the longest x6 28.8 us: head_norm_grad(): upstream = grad_b16.astype(jnp.float32)]
    mul x16 -> x0, local copies, waits for them, and re-layouts: 29 us -> none  [the longest x8 19.2 us: head_norm_grad(): result = inv_rms * scaled - shaped * (inv_rms * inv_rms * inv_rms) * inner]
    reshape x6 -> x7, local copies, waits for them, and re-layouts: 30.9 us -> 4.76 us  [the longest x2 2.21 us: outgoing(): array.reshape(2, ranks, POS, D).transpose(1, 0, 2, 3).reshape(ranks, 16, D)]
  transfers between devices with their start and end apart: 8 -> 10, of which waited for: 7 -> 8; matrix products, arithmetic and copies ran while one was open for 28% -> 6% of each run, Pallas kernels for 0% -> 29%
where the time goes in v1:
time: 188 us; the launch traced here: 187 us
  Pallas kernels  93.5 us (50%)
  waiting for transfers between devices  37.8 us (20%)
  starting transfers between devices  37.6 us (20%)
  local copies, waits for them, and re-layouts  11.3 us (6%)
  other arithmetic  5.14 us (3%)
    pallas_call x1, Pallas kernels, shards(): vmem_call(backward, [((ranks, 32, D), BF16), ((8, D), F32)], [(tok, F32)]...  39.4 us
    pallas_call x1, Pallas kernels, shards(): vmem_call(forward, saved, [(tok, F32), (tok, BF16), ((TOK, 3 * D), F32),...  38.6 us
    ppermute x7, waiting for transfers between devices, sum_over(): lax.ppermute(value, axis, [(i, i ^ step) for i in range(size)])  37.2 us
    all_to_all x3, starting transfers between devices, exchange(): return lax.all_to_all(rows, 'seq', split_axis=0, concat_axis=0, tiled=True)  22.5 us
    ppermute x7, starting transfers between devices, sum_over(): lax.ppermute(value, axis, [(i, i ^ step) for i in range(size)])  15 us
    pallas_call x1, Pallas kernels, split_weights(): pl.pallas_call(split_columns, grid=(steps,), in_specs=[pl.BlockSpec((rows...  10.2 us
    pallas_call x1, Pallas kernels, split_weights(): pl.pallas_call(split_rows, grid=(3,), in_specs=[pl.BlockSpec((D, cols), l...  5.25 us
    unnamed x17, local copies, waits for them, and re-layouts  3.92 us
  transfers between devices with their start and end apart: 10, of which 8 were waited for; matrix products, arithmetic and copies ran while one was open for 6% of the time, Pallas kernels for 29%

profile of v1, /device:TPU:0, one launch (start us, length us, event | category | flops | bytes accessed | tf_op | source)
XLA Modules:
  0.0 186.7 jit_solution(12091008417060743108)
XLA Ops:
  0.6 1.3 copy-done
  3.0 8.4 %all-to-all-start.1 = ((bf16[32,16,1152]{2,1,0:T(8,128)(2,1)}), bf16[32,16,1152]{2,1,0:T(8,128)(2,1)S(1)}, u32[]{:S(2)}, u32[]{:S(2)}) async-start(bf16[32,16,1152]{2,1,0:T(8,128)(2,1)} %copy_bitcast_fusion.2), calls=%async_computation.1 | async-start | bytes 2359296 | tf_op jit(solution)/shard_map/all_to_all | solution.py:448
  12.6 5.2 %split_rows.1.wout_ref = bf16[1152,1152]{1,0:T(8,128)(2,1)} custom-call(bf16[1152,1152]{1,0:T(8,128)(2,1)} %w_ref.3), custom_call_target="tpu_custom_call" | custom-call | flops 1061683200 | bytes 5308416 | tf_op jit(solution)/shard_map/split_rows/pallas_call | solution.py:91
  18.4 10.2 %split_columns.1.wqkv_ref = bf16[1152,3456]{1,0:T(8,128)(2,1)} custom-call(bf16[1152,3456]{1,0:T(8,128)(2,1)} %w_ref.2), custom_call_target="tpu_custom_call" | custom-call | flops 3185049600 | bytes 15925248 | tf_op jit(solution)/shard_map/split_columns/pallas_call | solution.py:78
  31.4 6.9 %all-to-all-start = ((bf16[32,16,1152]{2,1,0:T(8,128)(2,1)}), bf16[32,16,1152]{2,1,0:T(8,128)(2,1)S(1)}, u32[]{:S(2)}, u32[]{:S(2)}) async-start(bf16[32,16,1152]{2,1,0:T(8,128)(2,1)} %copy_bitcast_fusion.3), calls=%async_computation | async-start | bytes 2359296 | tf_op jit(solution)/shard_map/all_to_all | solution.py:448
  38.4 1.3 bitcast_add_fusion.mod_ref
  39.7 38.6 %attention_forward.1 = (bf16[512,1152]{1,0:T(8,128)(2,1)}, f32[512,1152]{1,0:T(8,128)}, f32[512,128]{1,0:T(8,128)}, f32[512,1152]{1,0:T(8,128)}, f32[512,1152]{1...) custom-call(s32[1]{0:T(128)S(6)} %copy.31.count_ref, ...), custom_call_target="tpu_custom_call" | custom-call | flops 8000000000 | bytes 30000000 | tf_op jit(solution)/shard_map/attention_forward/pallas_call | solution.py:475
  79.3 39.4 %attention_backward.1 = (bf16[32,32,1152]{2,1,0:T(8,128)(2,1)}, f32[8,1152]{1,0:T(8,128)}) custom-call(bf16[512,1152]{1,0:T(8,128)(2,1)} %bitcast.35, f32[3,1152]{1,0:T(4,128)} %bitcast_add_fusion.mod_ref, f32[2,1152]{1,0:T(2,128)} %pad_maximum_fusion.gain_ref, bf16[1152,3456]{1,0:T(8,128)(2,1)} %split_columns.1.wqkv_ref, ...), custom_call_target="tpu_custom_call" | custom-call | flops 8999999488 | bytes 30000000 | tf_op jit(solution)/shard_map/attention_backward/pallas_call | solution.py:486
  118.7 7.2 %all-to-all-start.2 = ((bf16[32,32,1152]{2,1,0:T(8,128)(2,1)}), bf16[32,32,1152]{2,1,0:T(8,128)(2,1)S(1)}, u32[]{:S(2)}, u32[]{:S(2)}) async-start(bf16[32,32,1152]{2,1,0:T(8,128)(2,1)} %get-tuple-element.32), calls=%async_computation.2 | async-start | bytes 4718592 | tf_op jit(solution)/shard_map/all_to_all | solution.py:448
  126.3 1.1 collective-permute-done
  128.2 1.8 collective-permute-start.1
  130.0 24.9 %collective-permute-done.1 = f32[8,1152]{1,0:T(8,128)S(1)} collective-permute-done((f32[8,1152]{1,0:T(8,128)S(1)}, f32[8,1152]{1,0:T(8,128)S(1)}, u32[]{:S(2)}, u32[]{:S(2)}) %collective-permute-start.1) | collective-permute-done | bytes 36896 | tf_op jit(solution)/shard_map/ppermute | solution.py:427
  155.0 3.1 %collective-permute-start.2 = (f32[8,1152]{1,0:T(8,128)S(1)}, f32[8,1152]{1,0:T(8,128)S(1)}, u32[]{:S(2)}, u32[]{:S(2)}) collective-permute-start(f32[8,1152]{1,0:T(8,128)S(1)} %add.26), channel_id=1, source_target_pairs={{0,16},{4,20},{8,24},{12,28},{16,0},{20,4},{24,8},{28,12},{32,48},... | collective-permute-start | bytes 110600 | tf_op jit(solution)/shard_map/ppermute | solution.py:427
  158.1 2.4 %collective-permute-done.2 = f32[8,1152]{1,0:T(8,128)S(1)} collective-permute-done((f32[8,1152]{1,0:T(8,128)S(1)}, f32[8,1152]{1,0:T(8,128)S(1)}, u32[]{:S(2)}, u32[]{:S(2)}) %collective-permute-start.2) | collective-permute-done | bytes 36896 | tf_op jit(solution)/shard_map/ppermute | solution.py:427
  160.5 2.3 %collective-permute-start.3 = (f32[8,1152]{1,0:T(8,128)S(1)}, f32[8,1152]{1,0:T(8,128)S(1)}, u32[]{:S(2)}, u32[]{:S(2)}) collective-permute-start(f32[8,1152]{1,0:T(8,128)S(1)} %add.27), channel_id=1, source_target_pairs={{0,32},{4,36},{8,40},{12,44},{16,48},{20,52},{24,56},{28,60},{32,0... | collective-permute-start | bytes 110600 | tf_op jit(solution)/shard_map/ppermute | solution.py:427
  162.8 1.9 %collective-permute-done.3 = f32[8,1152]{1,0:T(8,128)S(1)} collective-permute-done((f32[8,1152]{1,0:T(8,128)S(1)}, f32[8,1152]{1,0:T(8,128)S(1)}, u32[]{:S(2)}, u32[]{:S(2)}) %collective-permute-start.3) | collective-permute-done | bytes 36896 | tf_op jit(solution)/shard_map/ppermute | solution.py:427
  164.7 2.7 %collective-permute-start.4 = (f32[8,1152]{1,0:T(8,128)S(1)}, f32[8,1152]{1,0:T(8,128)S(1)}, u32[]{:S(2)}, u32[]{:S(2)}) collective-permute-start(f32[8,1152]{1,0:T(8,128)S(1)} %add.28), channel_id=1, source_target_pairs={{0,64},{4,68},{8,72},{12,76},{16,80},{20,84},{24,88},{28,92},{32,9... | collective-permute-start | bytes 110600 | tf_op jit(solution)/shard_map/ppermute | solution.py:427
  167.4 2.8 %collective-permute-done.4 = f32[8,1152]{1,0:T(8,128)S(1)} collective-permute-done((f32[8,1152]{1,0:T(8,128)S(1)}, f32[8,1152]{1,0:T(8,128)S(1)}, u32[]{:S(2)}, u32[]{:S(2)}) %collective-permute-start.4) | collective-permute-done | bytes 36896 | tf_op jit(solution)/shard_map/ppermute | solution.py:427
  170.2 1.6 collective-permute-start.5
  171.8 2.4 %collective-permute-done.5 = f32[8,1152]{1,0:T(8,128)S(1)} collective-permute-done((f32[8,1152]{1,0:T(8,128)S(1)}, f32[8,1152]{1,0:T(8,128)S(1)}, u32[]{:S(2)}, u32[]{:S(2)}) %collective-permute-start.5) | collective-permute-done | bytes 36896 | tf_op jit(solution)/shard_map/ppermute | solution.py:427
  174.1 3.2 %collective-permute-start.6 = (f32[8,1152]{1,0:T(8,128)S(1)}, f32[8,1152]{1,0:T(8,128)S(1)}, u32[]{:S(2)}, u32[]{:S(2)}) collective-permute-start(f32[8,1152]{1,0:T(8,128)S(1)} %add.30), channel_id=1, source_target_pairs={{0,2},{1,3},{2,0},{3,1},{4,6},{5,7},{6,4},{7,5},{8,10},{9,11},{10,... | collective-permute-start | bytes 110600 | tf_op jit(solution)/shard_map/ppermute | solution.py:427
  178.0 1.6 collective-permute-done.6
  183.7 1.2 pad_maximum_fusion.3
  185.1 1.6 copy_bitcast_fusion
  (57 shorter events, 12.0 us)
Async XLA Ops:
  0.6 1.3 copy-start
  3.0 9.0 %copy-start.7 = (f32[72]{0:T(128)S(1)}, f32[72]{0:T(128)}, u32[]{:S(2)}) copy-start(f32[72]{0:T(128)} %param.13) | copy-start | bytes 868
  3.0 9.1 %copy-start.6 = (f32[72]{0:T(128)S(1)}, f32[72]{0:T(128)}, u32[]{:S(2)}) copy-start(f32[72]{0:T(128)} %param.14) | copy-start | bytes 868
  3.0 27.4 %all-to-all-start.1 = ((bf16[32,16,1152]{2,1,0:T(8,128)(2,1)}), bf16[32,16,1152]{2,1,0:T(8,128)(2,1)S(1)}, u32[]{:S(2)}, u32[]{:S(2)}) async-start(bf16[32,16,1152]{2,1,0:T(8,128)(2,1)} %copy_bitcast_fusion.2), calls=%async_computation.1 | async-start | bytes 2359296 | tf_op jit(solution)/shard_map/all_to_all | solution.py:448
  18.4 10.2 %copy-start.1 = (bf16[1,2,256,1152]{3,2,1,0:T(8,128)(2,1)S(1)}, bf16[1,2,256,1152]{3,2,1,0:T(8,128)(2,1)}, u32[]{:S(2)}) copy-start(bf16[1,2,256,1152]{3,2,1,0:T(8,128)(2,1)} %param.17) | copy-start | bytes 3538948
  29.8 8.6 %copy-start.5 = (f32[1,3,1152]{2,0,1:T(1,128)S(1)}, f32[1,3,1152]{2,0,1:T(1,128)}, u32[]{:S(2)}) copy-start(f32[1,3,1152]{2,0,1:T(1,128)} %param.12) | copy-start | bytes 41476
  30.4 1.0 copy-start.2
  31.4 46.9 %all-to-all-start = ((bf16[32,16,1152]{2,1,0:T(8,128)(2,1)}), bf16[32,16,1152]{2,1,0:T(8,128)(2,1)S(1)}, u32[]{:S(2)}, u32[]{:S(2)}) async-start(bf16[32,16,1152]{2,1,0:T(8,128)(2,1)} %copy_bitcast_fusion.3), calls=%async_computation | async-start | bytes 2359296 | tf_op jit(solution)/shard_map/all_to_all | solution.py:448
  78.3 1.0 copy-start.3
  118.7 66.2 %all-to-all-start.2 = ((bf16[32,32,1152]{2,1,0:T(8,128)(2,1)}), bf16[32,32,1152]{2,1,0:T(8,128)(2,1)S(1)}, u32[]{:S(2)}, u32[]{:S(2)}) async-start(bf16[32,32,1152]{2,1,0:T(8,128)(2,1)} %get-tuple-element.32), calls=%async_computation.2 | async-start | bytes 4718592 | tf_op jit(solution)/shard_map/all_to_all | solution.py:448
  126.0 1.5 collective-permute-start
  128.2 26.7 %collective-permute-start.1 = (f32[8,1152]{1,0:T(8,128)S(1)}, f32[8,1152]{1,0:T(8,128)S(1)}, u32[]{:S(2)}, u32[]{:S(2)}) collective-permute-start(f32[8,1152]{1,0:T(8,128)S(1)} %add.25), channel_id=1, source_target_pairs={{0,8},{4,12},{8,0},{12,4},{16,24},{20,28},{24,16},{28,20},{32,40},... | collective-permute-start | bytes 110600 | tf_op jit(solution)/shard_map/ppermute | solution.py:427
  155.0 5.5 %collective-permute-start.2 = (f32[8,1152]{1,0:T(8,128)S(1)}, f32[8,1152]{1,0:T(8,128)S(1)}, u32[]{:S(2)}, u32[]{:S(2)}) collective-permute-start(f32[8,1152]{1,0:T(8,128)S(1)} %add.26), channel_id=1, source_target_pairs={{0,16},{4,20},{8,24},{12,28},{16,0},{20,4},{24,8},{28,12},{32,48},... | collective-permute-start | bytes 110600 | tf_op jit(solution)/shard_map/ppermute | solution.py:427
  160.5 4.2 %collective-permute-start.3 = (f32[8,1152]{1,0:T(8,128)S(1)}, f32[8,1152]{1,0:T(8,128)S(1)}, u32[]{:S(2)}, u32[]{:S(2)}) collective-permute-start(f32[8,1152]{1,0:T(8,128)S(1)} %add.27), channel_id=1, source_target_pairs={{0,32},{4,36},{8,40},{12,44},{16,48},{20,52},{24,56},{28,60},{32,0... | collective-permute-start | bytes 110600 | tf_op jit(solution)/shard_map/ppermute | solution.py:427
  164.7 5.5 %collective-permute-start.4 = (f32[8,1152]{1,0:T(8,128)S(1)}, f32[8,1152]{1,0:T(8,128)S(1)}, u32[]{:S(2)}, u32[]{:S(2)}) collective-permute-start(f32[8,1152]{1,0:T(8,128)S(1)} %add.28), channel_id=1, source_target_pairs={{0,64},{4,68},{8,72},{12,76},{16,80},{20,84},{24,88},{28,92},{32,9... | collective-permute-start | bytes 110600 | tf_op jit(solution)/shard_map/ppermute | solution.py:427
  170.2 4.0 %collective-permute-start.5 = (f32[8,1152]{1,0:T(8,128)S(1)}, f32[8,1152]{1,0:T(8,128)S(1)}, u32[]{:S(2)}, u32[]{:S(2)}) collective-permute-start(f32[8,1152]{1,0:T(8,128)S(1)} %add.29), channel_id=1, source_target_pairs={{0,1},{1,0},{2,3},{3,2},{4,5},{5,4},{6,7},{7,6},{8,9},{9,8},{10,11... | collective-permute-start | bytes 110600 | tf_op jit(solution)/shard_map/ppermute | solution.py:427
  174.1 5.5 %collective-permute-start.6 = (f32[8,1152]{1,0:T(8,128)S(1)}, f32[8,1152]{1,0:T(8,128)S(1)}, u32[]{:S(2)}, u32[]{:S(2)}) collective-permute-start(f32[8,1152]{1,0:T(8,128)S(1)} %add.30), channel_id=1, source_target_pairs={{0,2},{1,3},{2,0},{3,1},{4,6},{5,7},{6,4},{7,5},{8,10},{9,11},{10,... | collective-permute-start | bytes 110600 | tf_op jit(solution)/shard_map/ppermute | solution.py:427
  179.6 0.6 copy-start.4

commit v2 on v0

v2 whole, which is shorter than its diff:
```python
import jax
import jax.numpy as jnp
from jax import lax
from jax.experimental import pallas as pl
from jax.experimental.pallas import tpu as pltpu
from jax.sharding import PartitionSpec as P

EPS = 1e-06
F32 = jnp.float32
BF16 = jnp.bfloat16
HEAD = 72
HEADS = 16
D = HEAD * HEADS
MAIN = 64 * HEADS
REST = 8 * HEADS
QK = 2 * D
MAIN_AT = (0, MAIN, QK)
REST_AT = (2 * MAIN, 2 * MAIN + REST, QK + MAIN)
TOK = 512
POS = 8
FR = 64
ROWS = 128
PAIRS = TOK // ROWS
BLOCK = 512
LANES = 128
TILES = D // LANES
SUMS = 16
SENT = 32 + SUMS
VMEM = 56 * 1024 * 1024
NN = (((1,), (0,)), ((), ()))
NT = (((1,), (1,)), ((), ()))
TN = (((0,), (0,)), ((), ()))


def dot(a, b, dims=NN):
    return lax.dot_general(a, b, dims, preferred_element_type=F32)


def iota(shape, dim):
    return lax.broadcasted_iota(jnp.int32, shape, dim)


def one_hot(cond):
    return jnp.where(cond, jnp.float32(1), jnp.float32(0)).astype(BF16)


def source_main(col):
    return col + 8 * (col >> 6)


def source_rest(col):
    return col + 64 + 64 * (col >> 3)


def split_columns(w_ref, o_ref):
    for part in range(3):
        base = part * D
        for j in range(4):
            lo = (288 * j) // 128 * 128
            r, c = iota((384, 256), 0), iota((384, 256), 1)
            pick = one_hot(source_main(c + 256 * j) == r + lo)
            o_ref[:, MAIN_AT[part] + 256 * j : MAIN_AT[part] + 256 * (j + 1)] = dot(
                w_ref[:, base + lo : base + lo + 384], pick
            ).astype(BF16)
        r, c = iota((D, REST), 0), iota((D, REST), 1)
        pick = one_hot(source_rest(c) == r)
        o_ref[:, REST_AT[part] : REST_AT[part] + REST] = dot(
            w_ref[:, base : base + D], pick
        ).astype(BF16)


def split_rows(w_ref, o_ref):
    for j in range(4):
        lo = (288 * j) // 128 * 128
        r, c = iota((256, 384), 0), iota((256, 384), 1)
        pick = one_hot(source_main(r + 256 * j) == c + lo)
        o_ref[256 * j : 256 * (j + 1), :] = dot(pick, w_ref[lo : lo + 384, :]).astype(BF16)
    r, c = iota((REST, D), 0), iota((REST, D), 1)
    pick = one_hot(source_rest(r) == c)
    o_ref[MAIN:, :] = dot(pick, w_ref[...]).astype(BF16)


def split_weights(w_qkv, w_out):
    steps = 4
    rows = D // steps
    wq = pl.pallas_call(
        split_columns,
        grid=(steps,),
        in_specs=[pl.BlockSpec((rows, 3 * D), lambda i: (i, 0))],
        out_specs=pl.BlockSpec((rows, 3 * D), lambda i: (i, 0)),
        out_shape=jax.ShapeDtypeStruct((D, 3 * D), BF16),
        compiler_params=pltpu.CompilerParams(vmem_limit_bytes=VMEM),
        cost_estimate=pl.CostEstimate(
            flops=2 * D * D * 1200, bytes_accessed=12 * D * D, transcendentals=0
        ),
        name="split_columns",
    )(w_qkv)
    cols = D // 3
    wo = pl.pallas_call(
        split_rows,
        grid=(3,),
        in_specs=[pl.BlockSpec((D, cols), lambda i: (0, i))],
        out_specs=pl.BlockSpec((D, cols), lambda i: (0, i)),
        out_shape=jax.ShapeDtypeStruct((D, D), BF16),
        compiler_params=pltpu.CompilerParams(vmem_limit_bytes=VMEM),
        cost_estimate=pl.CostEstimate(
            flops=2 * D * D * 400, bytes_accessed=4 * D * D, transcendentals=0
        ),
        name="split_rows",
    )(w_out)
    return wq, wo


def init_segments(seg, spread, fold):
    r, c = iota((D, REST), 0), iota((D, REST), 1)
    head = jnp.where(r < MAIN, r >> 6, (r - MAIN) >> 3)
    seg[...] = one_hot(head == (c >> 3))
    entry = jnp.where(r < MAIN, r & 63, 64 + (r & 7))
    fold[...] = one_hot(entry == c)
    r, c = iota((2 * REST, MAIN), 0), iota((2 * REST, MAIN), 1)
    spread[...] = one_hot((r & (REST - 1)) == 8 * (c >> 6))


def terms(value):
    high = value.astype(BF16)
    left = value - high.astype(F32)
    mid = left.astype(BF16)
    return high, mid, (left - mid.astype(F32)).astype(BF16)


def both(per_head):
    high = per_head.astype(BF16)
    return jnp.concatenate([high, (per_head - high.astype(F32)).astype(BF16)], 1)


def head_masks(t):
    c = iota((1, 256), 1)
    head = jnp.where(c < 128, (c >> 6) + 2 * t, (c - 128) >> 3)
    return [one_hot(head == h) for h in (2 * t, 2 * t + 1)]


def unit_of(ref, rows, t):
    return jnp.concatenate([ref[rows, 128 * t : 128 * (t + 1)], ref[rows, MAIN:]], 1)


def stacked(block, masks):
    return [
        jnp.concatenate([block[:FR] * masks[0], block[:FR] * masks[1]], 0),
        jnp.concatenate([block[FR:] * masks[0], block[FR:] * masks[1]], 0),
    ]


def diagonal(block):
    zero = jnp.zeros((FR, 256), BF16)
    return jnp.concatenate(
        [
            jnp.concatenate([block[:FR], zero], 1),
            jnp.concatenate([zero, block[FR:]], 1),
        ],
        0,
    )


def own_features(product, masks):
    zero, one = masks[0].astype(F32), masks[1].astype(F32)
    return jnp.concatenate(
        [
            product[:FR, :256] * zero + product[FR:, :256] * one,
            product[:FR, 256:] * zero + product[FR:, 256:] * one,
        ],
        0,
    )


def loop(count, body):
    def step(i, _):
        body(i)
        return 0

    lax.fori_loop(0, count, step, 0)


def over_columns(total, body):
    loop(total // BLOCK, lambda b: body(pl.ds(pl.multiple_of(b * BLOCK, BLOCK), BLOCK)))
    if total % BLOCK:
        body(pl.ds(total // BLOCK * BLOCK, total % BLOCK))


def over_rows(size, body):
    loop(TOK // size, lambda i: body(pl.ds(pl.multiple_of(i * size, size), size)))


def lane_tiles():
    return [slice(LANES * c, LANES * (c + 1)) for c in range(TILES)]


def sub_block(
    count_ref,
    in_ref,
    mod_ref,
    gain_ref,
    wqkv_hbm,
    wout_hbm,
    out_ref,
    wqkv,
    wout,
    sems,
    frames,
    xp,
    unit,
    istd,
    cp,
    gy,
    normed,
    proj,
    gatt,
    qn,
    kn,
    vn,
    rq,
    rk,
    dq,
    dk,
    dqkv,
    sums,
    seg,
    spread,
    fold,
    bias,
):
    ranks = in_ref.shape[0]
    att, gn = gy, normed
    load_qkv = pltpu.make_async_copy(wqkv_hbm, wqkv, sems.at[0])
    load_out = pltpu.make_async_copy(wout_hbm, wout, sems.at[1])
    load_out.start()
    load_qkv.start()
    init_segments(seg, spread, fold)
    r = iota((128, 128), 0)
    bias[...] = jnp.where((r & (FR - 1)) < count_ref[0], jnp.float32(0), jnp.float32(-1e30))
    sums[...] = jnp.zeros_like(sums)

    def at_position(p):
        return pl.ds(p, FR, stride=POS)

    def position_rows(p):
        return pl.ds(pl.multiple_of(p * FR, FR), FR)

    def fill(first):
        for c, cols in enumerate(lane_tiles()):
            frames[c] = in_ref[:, first : first + 16, cols].reshape(TOK, LANES).astype(F32)

    def drain(first):
        for c, cols in enumerate(lane_tiles()):
            out_ref[:, first : first + 16, cols] = frames[c].astype(BF16).reshape(ranks, 16, LANES)

    def arrive(p):
        rows = position_rows(p)
        for c, cols in enumerate(lane_tiles()):
            cot = frames[c, at_position(p), :]
            cp[rows, cols] = cot
            gy[rows, cols] = (cot * mod_ref[2:3, cols]).astype(BF16)

    def norm(p):
        rows = position_rows(p)
        parts = [frames[c, at_position(p), :] for c in range(TILES)]
        mean = jnp.sum(sum(parts), -1, keepdims=True) * (1.0 / D)
        centred = [x - mean for x in parts]
        square = jnp.sum(sum(x * x for x in centred), -1, keepdims=True) * (1.0 / D)
        inv = lax.rsqrt(square + EPS)
        istd[rows, :] = jnp.broadcast_to(inv, (FR, LANES))
        for c, cols in enumerate(lane_tiles()):
            xp[rows, cols] = parts[c]
            u = centred[c] * inv
            unit[rows, cols] = u
            normed[rows, cols] = (u * (1.0 + mod_ref[1:2, cols]) + mod_ref[0:1, cols]).astype(BF16)

    fill(16)
    loop(POS, arrive)
    fill(0)
    loop(POS, norm)

    def grad_attention(cols):
        gatt[:, cols] = dot(gy[...], wout[cols, :], NT).astype(BF16)

    load_out.wait()
    over_columns(D, grad_attention)

    def project(cols):
        proj[:, cols] = dot(normed[...], wqkv[:, cols])

    load_qkv.wait()
    over_columns(QK, project)

    def project_values(cols):
        vn[:, cols] = dot(normed[...], wqkv[:, pl.ds(QK + cols.start, cols.size)]).astype(BF16)

    over_columns(D, project_values)

    def heads(rows):
        for part, (n_ref, r_ref) in enumerate(((qn, rq), (kn, rk))):
            main = slice(MAIN_AT[part], MAIN_AT[part] + MAIN)
            rest = slice(REST_AT[part], REST_AT[part] + REST)
            m, t = proj[rows, main], proj[rows, rest]
            total = sum(dot(part, seg[:MAIN, :]) for part in terms(m * m)[:2])
            total = total + sum(dot(part, seg[MAIN:, :]) for part in terms(t * t)[:2])
            inv = lax.rsqrt(total * (1.0 / HEAD) + EPS)
            r_ref[rows, :] = inv
            pair = both(inv)
            for b in range(0, MAIN, 256):
                cols = slice(MAIN_AT[part] + b, MAIN_AT[part] + b + 256)
                hat = proj[rows, cols] * dot(pair, spread[:, b : b + 256])
                proj[rows, cols] = hat
                n_ref[rows, b : b + 256] = (hat * gain_ref[part : part + 1, b : b + 256]).astype(BF16)
            hat = t * inv
            proj[rows, rest] = hat
            n_ref[rows, MAIN:] = (hat * gain_ref[part : part + 1, MAIN:]).astype(BF16)

    over_rows(256, heads)

    def attend(rows):
        rest = [jnp.zeros((ROWS, REST), F32)] * 4
        for t in range(HEADS // 2):
            masks = head_masks(t)
            cols = slice(128 * t, 128 * (t + 1))
            keys = stacked(unit_of(kn, rows, t), masks)
            vals = stacked(unit_of(vn, rows, t), masks)
            query = diagonal(unit_of(qn, rows, t))
            grad = diagonal(unit_of(gatt, rows, t))
            s = dot(jnp.concatenate(keys, 1), query, NT) * (HEAD**-0.5) + bias[...]
            s = s.reshape(2, FR, 128)
            e = jnp.exp(s - jnp.max(s, 1, keepdims=True))
            prob = e * (1.0 / jnp.sum(e, 1, keepdims=True))
            dp = dot(jnp.concatenate(vals, 1), grad, NT).reshape(2, FR, 128)
            delta = jnp.sum(prob * dp, 1, keepdims=True)
            ds = (prob * (dp - delta) * (HEAD**-0.5)).reshape(128, 128)
            prob = prob.reshape(128, 128)
            pb, db = prob.astype(BF16), ds.astype(BF16)
            pt, dt = prob.T.astype(BF16), ds.T.astype(BF16)
            out = jnp.concatenate([dot(pt[:FR], vals[0]), dot(pt[FR:], vals[1])], 0)
            gq = jnp.concatenate([dot(dt[:FR], keys[0]), dot(dt[FR:], keys[1])], 0)
            gk = own_features(dot(db, query), masks)
            gv = own_features(dot(pb, grad), masks)
            att[rows, cols] = out[:, :128].astype(BF16)
            dq[rows, cols] = gq[:, :128].astype(BF16)
            dk[rows, cols] = gk[:, :128].astype(BF16)
            dqkv[rows, QK + 128 * t : QK + 128 * (t + 1)] = gv[:, :128].astype(BF16)
            rest = [a + b[:, 128:] for a, b in zip(rest, (out, gq, gk, gv))]
        att[rows, MAIN:] = rest[0].astype(BF16)
        dq[rows, MAIN:] = rest[1].astype(BF16)
        dk[rows, MAIN:] = rest[2].astype(BF16)
        dqkv[rows, QK + MAIN :] = rest[3].astype(BF16)

    over_rows(ROWS, attend)

    def out_project(first, size):
        cols = slice(first, first + size)
        y = dot(att[...], wout[:, cols])
        sums[2:3, cols] = jnp.sum(cp[:, cols] * y, 0, keepdims=True)
        value = xp[:, cols] + mod_ref[2:3, cols] * y
        for c in range(size // LANES):
            for p in range(POS):
                frames[first // LANES + c, at_position(p), :] = value[
                    p * FR : (p + 1) * FR, c * LANES : (c + 1) * LANES
                ]

    for first in range(0, D, 384):
        out_project(first, 384)
    drain(0)

    def heads_grad(rows):
        for part, (d_ref, r_ref) in enumerate(((dq, rq), (dk, rk))):
            main = slice(MAIN_AT[part], MAIN_AT[part] + MAIN)
            rest = slice(REST_AT[part], REST_AT[part] + REST)
            gain = gain_ref[part : part + 1, :]
            row = slice(3 + part, 4 + part)
            um, ur = d_ref[rows, :MAIN].astype(F32), d_ref[rows, MAIN:].astype(F32)
            wm, wr = um * proj[rows, main], ur * proj[rows, rest]
            sums[row, :MAIN] += jnp.sum(wm, 0, keepdims=True)
            sums[row, MAIN:] += jnp.sum(wr, 0, keepdims=True)
            total = dot((wm * gain[:, :MAIN]).astype(BF16), seg[:MAIN, :]) + dot(
                (wr * gain[:, MAIN:]).astype(BF16), seg[MAIN:, :]
            )
            inner = total * (1.0 / HEAD)
            inv = r_ref[rows, :]
            pair, inner_pair = both(inv), both(inner)
            for b in range(0, MAIN, 256):
                cols = slice(MAIN_AT[part] + b, MAIN_AT[part] + b + 256)
                a = d_ref[rows, b : b + 256].astype(F32) * gain[:, b : b + 256]
                picked = spread[:, b : b + 256]
                value = dot(pair, picked) * (a - proj[rows, cols] * dot(inner_pair, picked))
                dqkv[rows, cols] = value.astype(BF16)
            value = inv * (ur * gain[:, MAIN:] - proj[rows, rest] * inner)
            dqkv[rows, rest] = value.astype(BF16)

    over_rows(256, heads_grad)

    def grad_normed(cols):
        gn[:, cols] = dot(dqkv[...], wqkv[cols, :], NT).astype(BF16)

    over_columns(D, grad_normed)

    def layer(p):
        rows = position_rows(p)
        grads = [gn[rows, cols].astype(F32) for cols in lane_tiles()]
        units = [unit[rows, cols] for cols in lane_tiles()]
        scaled = []
        for g, u, cols in zip(grads, units, lane_tiles()):
            sums[0:1, cols] += jnp.sum(g, 0, keepdims=True)
            sums[1:2, cols] += jnp.sum(g * u, 0, keepdims=True)
            scaled.append(g * (1.0 + mod_ref[1:2, cols]))
        first = jnp.sum(sum(scaled), -1, keepdims=True) * (1.0 / D)
        second = jnp.sum(sum(g * u for g, u in zip(scaled, units)), -1, keepdims=True) * (1.0 / D)
        inv = istd[rows, :]
        for c, cols in enumerate(lane_tiles()):
            frames[c, at_position(p), :] = cp[rows, cols] + inv * (
                scaled[c] - first - units[c] * second
            )

    loop(POS, layer)
    drain(16)

    total = sums[...]
    folded = sum(dot(part, fold[...]) for part in terms(total))
    gains = jnp.concatenate([folded[3:4], folded[4:5], jnp.zeros((1, D - 256), F32)], 1)
    total = jnp.concatenate([total[:3], gains], 0)
    rows = jnp.concatenate([part.astype(F32) for part in terms(total)] + [jnp.zeros((4, D), F32)], 0)
    out_ref[:, 32:, :] = jnp.broadcast_to(rows.astype(BF16)[None], (ranks, SUMS, D))


def run_sub_block(frame_counts, arrived, modulation, gains, wqkv, wout):
    ranks = arrived.shape[0]
    tok = (TOK, D)
    any_space = pl.BlockSpec(memory_space=pl.ANY)
    vmem = pl.BlockSpec(memory_space=pltpu.VMEM)
    scratch = [
        pltpu.VMEM((D, 3 * D), BF16),
        pltpu.VMEM((D, D), BF16),
        pltpu.SemaphoreType.DMA((2,)),
        pltpu.VMEM((TILES, TOK, LANES), F32),
        pltpu.VMEM(tok, F32),
        pltpu.VMEM(tok, F32),
        pltpu.VMEM((TOK, LANES), F32),
        pltpu.VMEM(tok, F32),
        pltpu.VMEM(tok, BF16),
        pltpu.VMEM(tok, BF16),
        pltpu.VMEM((TOK, QK), F32),
        pltpu.VMEM(tok, BF16),
        pltpu.VMEM(tok, BF16),
        pltpu.VMEM(tok, BF16),
        pltpu.VMEM(tok, BF16),
        pltpu.VMEM((TOK, REST), F32),
        pltpu.VMEM((TOK, REST), F32),
        pltpu.VMEM(tok, BF16),
        pltpu.VMEM(tok, BF16),
        pltpu.VMEM((TOK, 3 * D), BF16),
        pltpu.VMEM((8, D), F32),
        pltpu.VMEM((D, REST), BF16),
        pltpu.VMEM((2 * REST, MAIN), BF16),
        pltpu.VMEM((D, REST), BF16),
        pltpu.VMEM((128, 128), F32),
    ]
    return pl.pallas_call(
        sub_block,
        in_specs=[pl.BlockSpec(memory_space=pltpu.SMEM), vmem, vmem, vmem, any_space, any_space],
        out_specs=vmem,
        out_shape=jax.ShapeDtypeStruct((ranks, SENT, D), BF16),
        scratch_shapes=scratch,
        compiler_params=pltpu.CompilerParams(vmem_limit_bytes=VMEM),
        cost_estimate=pl.CostEstimate(
            flops=17_000_000_000, bytes_accessed=20_000_000, transcendentals=0
        ),
        name="sub_block",
    )(frame_counts, arrived, modulation, gains, wqkv, wout)


def sum_over(value, axis, size):
    step = 1
    while step < size:
        value = value + lax.ppermute(value, axis, [(i, i ^ step) for i in range(size)])
        step *= 2
    return value


def split_gain(gain):
    return jnp.concatenate([jnp.tile(gain[:64], HEADS), jnp.tile(gain[64:], HEADS)])


def shards(latents, frame_counts, mod_table, clip_mod, q_gain, k_gain, w_qkv, w_out, cotangent):
    ranks = lax.axis_size("seq")
    modulation = mod_table + clip_mod[0]
    gains = jnp.stack([split_gain(q_gain), split_gain(k_gain)])

    def exchange(rows):
        return lax.all_to_all(rows, "seq", split_axis=0, concat_axis=0, tiled=True)

    def outgoing(array):
        return array.reshape(2, ranks, POS, D).transpose(1, 0, 2, 3).reshape(ranks, 16, D)

    def incoming(array):
        return array.reshape(ranks, 2, POS, D).transpose(1, 0, 2, 3).reshape(latents.shape)

    arrived = exchange(jnp.concatenate([outgoing(latents), outgoing(cotangent)], 1))
    wqkv, wout = split_weights(w_qkv, w_out)
    out = run_sub_block(frame_counts, arrived, modulation, gains, wqkv, wout)
    back = exchange(out)
    pieces = jnp.sum(back[:, 32:, :].astype(F32), 0)
    clip_total = pieces[0:4] + pieces[4:8] + pieces[8:12]
    total = sum_over(clip_total, "dp", lax.axis_size("dp"))
    return (
        incoming(back[:, :16, :]),
        incoming(back[:, 16:32, :]),
        clip_total[None, :3],
        total[:3],
        total[3, :HEAD],
        total[3, 128 : 128 + HEAD],
    )


def solution(mesh):
    return jax.shard_map(
        shards,
        mesh=mesh,
        in_specs=(
            P("dp", "seq", None, None),
            P("dp"),
            P(),
            P("dp", None, None),
            P(),
            P(),
            P(),
            P(),
            P("dp", "seq", None, None),
        ),
        out_specs=(
            P("dp", "seq", None, None),
            P("dp", "seq", None, None),
            P("dp", None, None),
            P(),
            P(),
            P(),
        ),
        check_vma=False,
    )
```

time: 583 us -> 151 us (0.26); the launches traced: 572 us -> 151 us
  blocking collectives: 188 us -> 48.1 us
  local copies, waits for them, and re-layouts: 150 us -> 11.2 us
  waiting for transfers between devices: 78.4 us -> 13.9 us
  matrix products: 59.5 us -> 0 us
  Pallas kernels: 0 us -> 59.4 us
  other arithmetic: 48.3 us -> 3.81 us
  starting transfers between devices: 45.2 us -> 13.3 us
    psum x2 -> x0, blocking collectives: 188 us -> none  [the longest x1 125 us: shards(): clip_total = lax.psum(mod_part, 'seq')]
    all_to_all x8 -> x1, waiting for transfers between devices: 78.4 us -> 11.7 us  [exchange(): return lax.all_to_all(rows, 'seq', split_axis=0, concat_axis=0, tiled=True)]
    pallas_call x0 -> x3, Pallas kernels: none -> 59.4 us  [the longest x1 44 us: run_sub_block(): pl.pallas_call(sub_block, in_specs=[pl.BlockSpec(memory_space=pltpu.SMEM)...]
    dot_general x9 -> x0, matrix products: 53.7 us -> none  [the longest x1 9.35 us: attention_backward(): jnp.einsum('phfg,phfd->phgd', grad_score, query, preferred_element_type=j...]
    all_to_all x0 -> x1, blocking collectives: none -> 48.1 us  [exchange(): return lax.all_to_all(rows, 'seq', split_axis=0, concat_axis=0, tiled=True)]
    all_to_all x8 -> x1, starting transfers between devices: 45.2 us -> 8.38 us  [exchange(): return lax.all_to_all(rows, 'seq', split_axis=0, concat_axis=0, tiled=True)]
    convert_element_type x7 -> x0, local copies, waits for them, and re-layouts: 33.4 us -> none  [the longest x6 28.8 us: head_norm_grad(): upstream = grad_b16.astype(jnp.float32)]
    reshape x6 -> x1, local copies, waits for them, and re-layouts: 30.9 us -> 1.45 us  [outgoing(): array.reshape(2, ranks, POS, D).transpose(1, 0, 2, 3).reshape(ranks, 16, D)]
  transfers between devices with their start and end apart: 8 -> 3, of which waited for: 7 -> 2; matrix products, arithmetic and copies ran while one was open for 28% -> 6% of each run, Pallas kernels for 0% -> 10%
where the time goes in v2:
time: 151 us
  Pallas kernels  59.4 us (39%)
  blocking collectives  48.1 us (32%)
  waiting for transfers between devices  13.9 us (9%)
  starting transfers between devices  13.3 us (9%)
  local copies, waits for them, and re-layouts  11.2 us (7%)
  other arithmetic  3.81 us (3%)
    all_to_all x1, blocking collectives, exchange(): return lax.all_to_all(rows, 'seq', split_axis=0, concat_axis=0, tiled=True)  48.1 us
    pallas_call x1, Pallas kernels, run_sub_block(): pl.pallas_call(sub_block, in_specs=[pl.BlockSpec(memory_space=pltpu.SMEM)...  44 us
    all_to_all x1, waiting for transfers between devices, exchange(): return lax.all_to_all(rows, 'seq', split_axis=0, concat_axis=0, tiled=True)  11.7 us
    pallas_call x1, Pallas kernels, split_weights(): pl.pallas_call(split_columns, grid=(steps,), in_specs=[pl.BlockSpec((rows...  10.1 us
    all_to_all x1, starting transfers between devices, exchange(): return lax.all_to_all(rows, 'seq', split_axis=0, concat_axis=0, tiled=True)  8.38 us
    pallas_call x1, Pallas kernels, split_weights(): pl.pallas_call(split_rows, grid=(3,), in_specs=[pl.BlockSpec((D, cols), l...  5.25 us
    ppermute x2, starting transfers between devices, sum_over(): lax.ppermute(value, axis, [(i, i ^ step) for i in range(size)])  4.93 us
  transfers between devices with their start and end apart: 3, of which 2 were waited for; matrix products, arithmetic and copies ran while one was open for 6% of the time, Pallas kernels for 10%

profile of v2, /device:TPU:0, one launch (start us, length us, event | category | flops | bytes accessed | tf_op | source)
XLA Modules:
  0.0 150.9 jit_solution(15188540456633753548)
XLA Ops:
  0.6 1.3 copy-done
  1.9 1.5 copy_bitcast_fusion.2
  3.4 1.7 %pad_maximum_fusion = bf16[32,32,1152]{2,1,0:T(8,128)(2,1)} fusion(bf16[32,16,1152]{2,1,0:T(8,128)(2,1)S(1)} %get-tuple-element.10, bf16[32,16,1152]{2,1,0:T(8,128)(2,1)S(1)} %get-tuple-element.11), kind=kLoop, calls=%fused_computation | loop fusion | flops 4718592 | bytes 4718592 | tf_op jit(solution)/shard_map/concatenate | solution.py:502
  5.0 8.4 %all-to-all-start = ((bf16[32,32,1152]{2,1,0:T(8,128)(2,1)}), bf16[32,32,1152]{2,1,0:T(8,128)(2,1)S(1)}, u32[]{:S(2)}, u32[]{:S(2)}) async-start(bf16[32,32,1152]{2,1,0:T(8,128)(2,1)} %pad_maximum_fusion), calls=%async_computation | async-start | bytes 4718592 | tf_op jit(solution)/shard_map/all_to_all | solution.py:494
  14.1 0.6 slice.43
  14.8 0.7 tile.18
  15.5 0.6 tile.19
  16.2 0.7 tile.16
  16.9 0.7 tile.17
  17.5 0.7 pad_maximum_fusion.2
  18.2 5.2 %split_rows.1.wout_hbm = bf16[1152,1152]{1,0:T(8,128)(2,1)} custom-call(bf16[1152,1152]{1,0:T(8,128)(2,1)} %w_ref.3), custom_call_target="tpu_custom_call" | custom-call | flops 1061683200 | bytes 5308416 | tf_op jit(solution)/shard_map/split_rows/pallas_call | solution.py:99
  23.5 0.6 pad_maximum_fusion.1.gain_ref
  24.1 10.1 %split_columns.1.wqkv_hbm = bf16[1152,3456]{1,0:T(8,128)(2,1)} custom-call(bf16[1152,3456]{1,0:T(8,128)(2,1)} %w_ref.2), custom_call_target="tpu_custom_call" | custom-call | flops 3185049600 | bytes 15925248 | tf_op jit(solution)/shard_map/split_columns/pallas_call | solution.py:86
  34.2 0.6 bitcast_add_fusion.mod_ref
  34.9 11.7 %all-to-all-done.in_ref = bf16[32,32,1152]{2,1,0:T(8,128)(2,1)S(1)} async-done(((bf16[32,32,1152]{2,1,0:T(8,128)(2,1)}), bf16[32,32,1152]{2,1,0:T(8,128)(2,1)S(1)}, u32[]{:S(2)}, u32[]{:S(2)}) %all-to-all-start) | async-done | bytes 2359328 | tf_op jit(solution)/shard_map/all_to_all | solution.py:494
  46.5 1.4 copy-done.1
  47.9 44.0 %sub_block.1 = bf16[32,48,1152]{2,1,0:T(8,128)(2,1)} custom-call(s32[1]{0:T(128)S(6)} %copy.31.count_ref, bf16[32,32,1152]{2,1,0:T(8,128)(2,1)} %copy-done.1, f32[3,1152]{1,0:T(4,128)} %bitcast_add_fusion.mod_ref, f32[2,1152]{1,0:T(2,128)} %pad_maximum_fusion.1.gain_ref, bf16[1152,3456]{1,0:T(8,128)(2,1)} %split_columns.1.wqkv_hbm, ...), custom_call_target="tpu_custom_call" | custom-call | flops 16999999488 | bytes 20000000 | tf_op jit(solution)/shard_map/sub_block/pallas_call | solution.py:462
  91.9 48.1 %all_to_all.10 = bf16[32,48,1152]{2,1,0:T(8,128)(2,1)S(1)} all-to-all(bf16[32,48,1152]{2,1,0:T(8,128)(2,1)} %sub_block.1), channel_id=1, replica_groups=mesh['seq'=32,'dp'=4] {'seq'}, dimensions={0} | all-to-all | bytes 7077888 | tf_op jit(solution)/shard_map/all_to_all | solution.py:494
  140.2 1.7 %collective-permute-start = (f32[4,1152]{1,0:T(4,128)S(1)}, f32[4,1152]{1,0:T(4,128)S(1)}, u32[]{:S(2)}, u32[]{:S(2)}) collective-permute-start(f32[4,1152]{1,0:T(4,128)S(1)} %slice_add_fusion), channel_id=1, source_target_pairs={{0,1},{1,0},{2,3},{3,2},{4,5},{5,4},{6,7},{7,6},{8,9},{9,8},{10,11... | collective-permute-start | bytes 55304 | tf_op jit(solution)/shard_map/ppermute | solution.py:479
  141.8 2.2 %collective-permute-done = f32[4,1152]{1,0:T(4,128)S(1)} collective-permute-done((f32[4,1152]{1,0:T(4,128)S(1)}, f32[4,1152]{1,0:T(4,128)S(1)}, u32[]{:S(2)}, u32[]{:S(2)}) %collective-permute-start) | collective-permute-done | bytes 18464 | tf_op jit(solution)/shard_map/ppermute | solution.py:479
  144.0 3.3 %collective-permute-start.1 = (f32[4,1152]{1,0:T(4,128)S(1)}, f32[4,1152]{1,0:T(4,128)S(1)}, u32[]{:S(2)}, u32[]{:S(2)}) collective-permute-start(f32[4,1152]{1,0:T(4,128)S(1)} %fusion), channel_id=1, source_target_pairs={{0,2},{1,3},{2,0},{3,1},{4,6},{5,7},{6,4},{7,5},{8,10},{9,11},{10,... | collective-permute-start | bytes 55304 | tf_op jit(solution)/shard_map/ppermute | solution.py:479
  147.5 1.1 copy.29
  148.6 0.6 broadcast_in_dim.3
  149.2 1.1 copy.30
  (27 shorter events, 1.3 us)
Async XLA Ops:
  0.6 1.3 copy-start
  5.0 9.0 %copy-start.6 = (f32[72]{0:T(128)S(1)}, f32[72]{0:T(128)}, u32[]{:S(2)}) copy-start(f32[72]{0:T(128)} %param.13) | copy-start | bytes 868
  5.0 9.6 %copy-start.5 = (f32[72]{0:T(128)S(1)}, f32[72]{0:T(128)}, u32[]{:S(2)}) copy-start(f32[72]{0:T(128)} %param.14) | copy-start | bytes 868
  5.0 41.5 %all-to-all-start = ((bf16[32,32,1152]{2,1,0:T(8,128)(2,1)}), bf16[32,32,1152]{2,1,0:T(8,128)(2,1)S(1)}, u32[]{:S(2)}, u32[]{:S(2)}) async-start(bf16[32,32,1152]{2,1,0:T(8,128)(2,1)} %pad_maximum_fusion), calls=%async_computation | async-start | bytes 4718592 | tf_op jit(solution)/shard_map/all_to_all | solution.py:494
  24.1 10.1 %copy-start.3 = (f32[3,1152]{1,0:T(4,128)S(1)}, f32[3,1152]{1,0:T(4,128)}, u32[]{:S(2)}) copy-start(f32[3,1152]{1,0:T(4,128)} %param.11) | copy-start | bytes 41476
  24.1 10.1 %copy-start.4 = (f32[1,3,1152]{2,0,1:T(1,128)S(1)}, f32[1,3,1152]{2,0,1:T(1,128)}, u32[]{:S(2)}) copy-start(f32[1,3,1152]{2,0,1:T(1,128)} %param.12) | copy-start | bytes 41476
  46.5 1.4 copy-start.1
  140.2 3.8 %collective-permute-start = (f32[4,1152]{1,0:T(4,128)S(1)}, f32[4,1152]{1,0:T(4,128)S(1)}, u32[]{:S(2)}, u32[]{:S(2)}) collective-permute-start(f32[4,1152]{1,0:T(4,128)S(1)} %slice_add_fusion), channel_id=1, source_target_pairs={{0,1},{1,0},{2,3},{3,2},{4,5},{5,4},{6,7},{7,6},{8,9},{9,8},{10,11... | collective-permute-start | bytes 55304 | tf_op jit(solution)/shard_map/ppermute | solution.py:479
  144.0 6.3 %collective-permute-start.1 = (f32[4,1152]{1,0:T(4,128)S(1)}, f32[4,1152]{1,0:T(4,128)S(1)}, u32[]{:S(2)}, u32[]{:S(2)}) collective-permute-start(f32[4,1152]{1,0:T(4,128)S(1)} %fusion), channel_id=1, source_target_pairs={{0,2},{1,3},{2,0},{3,1},{4,6},{5,7},{6,4},{7,5},{8,10},{9,11},{10,... | collective-permute-start | bytes 55304 | tf_op jit(solution)/shard_map/ppermute | solution.py:479
  150.3 0.6 copy-start.2

commit v3 on v2

--- a/solution.py
+++ b/solution.py
@@ -1,3 +1,5 @@
+import functools
+
 import jax
 import jax.numpy as jnp
 from jax import lax
@@ -16,16 +18,17 @@
 QK = 2 * D
 MAIN_AT = (0, MAIN, QK)
 REST_AT = (2 * MAIN, 2 * MAIN + REST, QK + MAIN)
-TOK = 512
-POS = 8
+CHUNKS = 2
+POS = 4
 FR = 64
+TOK = POS * FR
 ROWS = 128
 PAIRS = TOK // ROWS
 BLOCK = 512
 LANES = 128
 TILES = D // LANES
-SUMS = 16
-SENT = 32 + SUMS
+ROWS_IN = 16
+SUMS = 8
 VMEM = 56 * 1024 * 1024
 NN = (((1,), (0,)), ((), ()))
 NT = (((1,), (1,)), ((), ()))
@@ -52,63 +55,145 @@
     return col + 64 + 64 * (col >> 3)
 
 
-def split_columns(w_ref, o_ref):
+def window(j):
+    return 288 * j // 128 * 128
+
+
+def split_weights_kernel(qkv_ref, out_ref, qkv_o, out_o, pick, pick_rest):
+    @pl.when(pl.program_id(0) == 0)
+    def _():
+        for j in range(4):
+            r, c = iota((384, 256), 0), iota((384, 256), 1)
+            pick[j] = one_hot(source_main(c + 256 * j) == r + window(j))
+        r, c = iota((D, REST), 0), iota((D, REST), 1)
+        pick_rest[...] = one_hot(source_rest(c) == r)
+
     for part in range(3):
         base = part * D
         for j in range(4):
-            lo = (288 * j) // 128 * 128
-            r, c = iota((384, 256), 0), iota((384, 256), 1)
-            pick = one_hot(source_main(c + 256 * j) == r + lo)
-            o_ref[:, MAIN_AT[part] + 256 * j : MAIN_AT[part] + 256 * (j + 1)] = dot(
-                w_ref[:, base + lo : base + lo + 384], pick
+            lo = base + window(j)
+            qkv_o[:, MAIN_AT[part] + 256 * j : MAIN_AT[part] + 256 * (j + 1)] = dot(
+                qkv_ref[:, lo : lo + 384], pick[j]
             ).astype(BF16)
-        r, c = iota((D, REST), 0), iota((D, REST), 1)
-        pick = one_hot(source_rest(c) == r)
-        o_ref[:, REST_AT[part] : REST_AT[part] + REST] = dot(
-            w_ref[:, base : base + D], pick
+        qkv_o[:, REST_AT[part] : REST_AT[part] + REST] = dot(
+            qkv_ref[:, base : base + D], pick_rest[...]
         ).astype(BF16)
 
-
-def split_rows(w_ref, o_ref):
     for j in range(4):
-        lo = (288 * j) // 128 * 128
-        r, c = iota((256, 384), 0), iota((256, 384), 1)
-        pick = one_hot(source_main(r + 256 * j) == c + lo)
-        o_ref[256 * j : 256 * (j + 1), :] = dot(pick, w_ref[lo : lo + 384, :]).astype(BF16)
-    r, c = iota((REST, D), 0), iota((REST, D), 1)
-    pick = one_hot(source_rest(r) == c)
-    o_ref[MAIN:, :] = dot(pick, w_ref[...]).astype(BF16)
+        out_o[256 * j : 256 * (j + 1), :] = dot(
+            pick[j], out_ref[window(j) : window(j) + 384, :], TN
+        ).astype(BF16)
+    out_o[MAIN:, :] = dot(pick_rest[...], out_ref[...], TN).astype(BF16)
 
 
 def split_weights(w_qkv, w_out):
-    steps = 4
-    rows = D // steps
-    wq = pl.pallas_call(
-        split_columns,
+    steps = 3
+    part = D // steps
+    return pl.pallas_call(
+        split_weights_kernel,
         grid=(steps,),
-        in_specs=[pl.BlockSpec((rows, 3 * D), lambda i: (i, 0))],
-        out_specs=pl.BlockSpec((rows, 3 * D), lambda i: (i, 0)),
-        out_shape=jax.ShapeDtypeStruct((D, 3 * D), BF16),
+        in_specs=[
+            pl.BlockSpec((part, 3 * D), lambda i: (i, 0)),
+            pl.BlockSpec((D, part), lambda i: (0, i)),
+        ],
+        out_specs=[
+            pl.BlockSpec((part, 3 * D), lambda i: (i, 0)),
+            pl.BlockSpec((D, part), lambda i: (0, i)),
+        ],
+        out_shape=[
+            jax.ShapeDtypeStruct((D, 3 * D), BF16),
+            jax.ShapeDtypeStruct((D, D), BF16),
+        ],
+        scratch_shapes=[pltpu.VMEM((4, 384, 256), BF16), pltpu.VMEM((D, REST), BF16)],
         compiler_params=pltpu.CompilerParams(vmem_limit_bytes=VMEM),
         cost_estimate=pl.CostEstimate(
-            flops=2 * D * D * 1200, bytes_accessed=12 * D * D, transcendentals=0
+            flops=2 * D * D * 1600, bytes_accessed=16 * D * D, transcendentals=0
         ),
-        name="split_columns",
-    )(w_qkv)
-    cols = D // 3
-    wo = pl.pallas_call(
-        split_rows,
-        grid=(3,),
-        in_specs=[pl.BlockSpec((D, cols), lambda i: (0, i))],
-        out_specs=pl.BlockSpec((D, cols), lambda i: (0, i)),
-        out_shape=jax.ShapeDtypeStruct((D, D), BF16),
+        name="split_weights",
+    )(w_qkv, w_out)
+
+
+def trade(first, second, chunk):
+    upper = iota(first.shape, 1) < POS
+    if chunk == 0:
+        return jnp.where(upper, first, pltpu.roll(second, POS, 1))
+    return jnp.where(upper, pltpu.roll(first, POS, 1), second)
+
+
+def pack_kernel(chunk, lat_ref, cot_ref, *refs):
+    o_ref = refs[-1]
+    ranks, _, width = o_ref.shape
+    for c in range(TILES):
+        cols = slice(LANES * c, LANES * (c + 1))
+        halves = []
+        for ref in (lat_ref, cot_ref):
+            tiles = [ref[0, i, :, cols].astype(F32).reshape(ranks, 8, LANES) for i in range(2)]
+            halves.append(trade(*tiles, chunk))
+        o_ref[:, :, cols] = jnp.concatenate(halves, 1).astype(BF16)
+
+
+def pack(latents, cotangent, chunk, after=()):
+    _, frames, positions, width = latents.shape
+    steps = 4
+    ranks = positions // 8
+    spec = pl.BlockSpec((1, frames, positions // steps, width), lambda i: (0, 0, i, 0))
+    return pl.pallas_call(
+        functools.partial(pack_kernel, chunk),
+        grid=(steps,),
+        in_specs=[spec, spec] + [pl.BlockSpec(memory_space=pl.ANY)] * len(after),
+        out_specs=pl.BlockSpec((ranks // steps, ROWS_IN, width), lambda i: (i, 0, 0)),
+        out_shape=jax.ShapeDtypeStruct((ranks, ROWS_IN, width), BF16),
         compiler_params=pltpu.CompilerParams(vmem_limit_bytes=VMEM),
-        cost_estimate=pl.CostEstimate(
-            flops=2 * D * D * 400, bytes_accessed=4 * D * D, transcendentals=0
-        ),
-        name="split_rows",
-    )(w_out)
-    return wq, wo
+        cost_estimate=pl.CostEstimate(flops=4_000_000, bytes_accessed=3_600_000, transcendentals=0),
+        name="pack",
+    )(latents, cotangent, *after)
+
+
+def tie_kernel(value_ref, other_ref, o_ref):
+    del value_ref, other_ref, o_ref
+
+
+def tie(value, other):
+    any_space = pl.BlockSpec(memory_space=pl.ANY)
+    return pl.pallas_call(
+        tie_kernel,
+        in_specs=[any_space, any_space],
+        out_specs=any_space,
+        out_shape=jax.ShapeDtypeStruct(value.shape, value.dtype),
+        input_output_aliases={0: 0},
+        name="tie",
+    )(value, other)
+
+
+def unpack_kernel(first_ref, second_ref, block_ref, grad_ref):
+    ranks = first_ref.shape[0]
+    for c in range(TILES):
+        cols = slice(LANES * c, LANES * (c + 1))
+        first, second = first_ref[:, :, cols].astype(F32), second_ref[:, :, cols].astype(F32)
+        for at, ref in ((0, block_ref), (8, grad_ref)):
+            for i in range(2):
+                tile = trade(first[:, at : at + 8], second[:, at : at + 8], i)
+                ref[0, i, :, cols] = tile.reshape(ranks * 8, LANES).astype(BF16)
+
+
+def unpack(first, second, shape):
+    _, frames, positions, width = shape
+    steps = 4
+    spec = pl.BlockSpec((1, frames, positions // steps, width), lambda i: (0, 0, i, 0))
+    out = jax.ShapeDtypeStruct(shape, BF16)
+    return pl.pallas_call(
+        unpack_kernel,
+        grid=(steps,),
+        in_specs=[
+            pl.BlockSpec((x.shape[0] // steps, *x.shape[1:]), lambda i: (i, 0, 0))
+            for x in (first, second)
+        ],
+        out_specs=[spec, spec],
+        out_shape=[out, out],
+        compiler_params=pltpu.CompilerParams(vmem_limit_bytes=VMEM),
+        cost_estimate=pl.CostEstimate(flops=4_000_000, bytes_accessed=5_000_000, transcendentals=0),
+        name="unpack",
+    )(first, second)
 
 
 def init_segments(seg, spread, fold):
@@ -161,12 +246,20 @@
     )
 
 
-def own_features(product, masks):
+def by_position(block):
+    lane, zero = iota((128, 128), 1), jnp.zeros((128, 128), F32)
+    own = lane < FR
+    return jnp.concatenate(
+        [jnp.where(own, block, zero), jnp.where(own, zero, block)], 0
+    ).astype(BF16)
+
+
+def own_rows(product, masks):
     zero, one = masks[0].astype(F32), masks[1].astype(F32)
     return jnp.concatenate(
         [
-            product[:FR, :256] * zero + product[FR:, :256] * one,
-            product[:FR, 256:] * zero + product[FR:, 256:] * one,
+            product[:64] * zero + product[64:128] * one,
+            product[128:192] * zero + product[192:] * one,
         ],
         0,
     )
@@ -195,13 +288,19 @@
 
 
 def sub_block(
+    last,
     count_ref,
-    in_ref,
-    mod_ref,
-    gain_ref,
+    in_hbm,
+    table_ref,
+    clip_ref,
+    q_gain_ref,
+    k_gain_ref,
     wqkv_hbm,
     wout_hbm,
+    before_ref,
     out_ref,
+    sums,
+    in_ref,
     wqkv,
     wout,
     sems,
@@ -222,47 +321,57 @@
     dq,
     dk,
     dqkv,
-    sums,
     seg,
     spread,
     fold,
     bias,
+    mod_ref,
+    gain_ref,
 ):
     ranks = in_ref.shape[0]
     att, gn = gy, normed
     load_qkv = pltpu.make_async_copy(wqkv_hbm, wqkv, sems.at[0])
     load_out = pltpu.make_async_copy(wout_hbm, wout, sems.at[1])
+    load_in = pltpu.make_async_copy(in_hbm, in_ref, sems.at[2])
+    load_in.start()
     load_out.start()
     load_qkv.start()
     init_segments(seg, spread, fold)
-    r = iota((128, 128), 0)
-    bias[...] = jnp.where((r & (FR - 1)) < count_ref[0], jnp.float32(0), jnp.float32(-1e30))
-    sums[...] = jnp.zeros_like(sums)
-
-    def at_position(p):
-        return pl.ds(p, FR, stride=POS)
+    key = iota((128, 128), 0) & (FR - 1)
+    valid = 2 * (key & 31) + (key >> 5) < count_ref[0]
+    bias[...] = jnp.where(valid, jnp.float32(0), jnp.float32(-1e30))
+    sums[...] = before_ref[...]
+    mod_ref[...] = table_ref[...] + clip_ref[...]
+    for part, ref in enumerate((q_gain_ref, k_gain_ref)):
+        gain_ref[part : part + 1, :] = sum(dot(x, fold[:, :HEAD], NT) for x in terms(ref[...]))
+
+    def strided(p, first, own):
+        return pl.ds(first + own * POS + p, ranks, stride=ROWS_IN)
+
+    def gather(c, p, first):
+        return jnp.concatenate([frames[c, strided(p, first, own), :] for own in range(2)], 0)
+
+    def scatter(c, p, first, value):
+        for own in range(2):
+            frames[c, strided(p, first, own), :] = value[own * ranks : (own + 1) * ranks]
 
     def position_rows(p):
         return pl.ds(pl.multiple_of(p * FR, FR), FR)
 
-    def fill(first):
-        for c, cols in enumerate(lane_tiles()):
-            frames[c] = in_ref[:, first : first + 16, cols].reshape(TOK, LANES).astype(F32)
-
-    def drain(first):
-        for c, cols in enumerate(lane_tiles()):
-            out_ref[:, first : first + 16, cols] = frames[c].astype(BF16).reshape(ranks, 16, LANES)
+    load_in.wait()
+    for c, cols in enumerate(lane_tiles()):
+        frames[c] = in_ref[:, :, cols].reshape(ranks * ROWS_IN, LANES).astype(F32)
 
     def arrive(p):
         rows = position_rows(p)
         for c, cols in enumerate(lane_tiles()):
-            cot = frames[c, at_position(p), :]
+            cot = gather(c, p, 8)
             cp[rows, cols] = cot
             gy[rows, cols] = (cot * mod_ref[2:3, cols]).astype(BF16)
 
     def norm(p):
         rows = position_rows(p)
-        parts = [frames[c, at_position(p), :] for c in range(TILES)]
+        parts = [gather(c, p, 0) for c in range(TILES)]
         mean = jnp.sum(sum(parts), -1, keepdims=True) * (1.0 / D)
         centred = [x - mean for x in parts]
         square = jnp.sum(sum(x * x for x in centred), -1, keepdims=True) * (1.0 / D)
@@ -274,9 +383,7 @@
             unit[rows, cols] = u
             normed[rows, cols] = (u * (1.0 + mod_ref[1:2, cols]) + mod_ref[0:1, cols]).astype(BF16)
 
-    fill(16)
     loop(POS, arrive)
-    fill(0)
     loop(POS, norm)
 
     def grad_attention(cols):
@@ -319,27 +426,31 @@
 
     def attend(rows):
         rest = [jnp.zeros((ROWS, REST), F32)] * 4
+        ops, soft = [], []
         for t in range(HEADS // 2):
             masks = head_masks(t)
-            cols = slice(128 * t, 128 * (t + 1))
             keys = stacked(unit_of(kn, rows, t), masks)
             vals = stacked(unit_of(vn, rows, t), masks)
             query = diagonal(unit_of(qn, rows, t))
             grad = diagonal(unit_of(gatt, rows, t))
             s = dot(jnp.concatenate(keys, 1), query, NT) * (HEAD**-0.5) + bias[...]
-            s = s.reshape(2, FR, 128)
+            dp = dot(jnp.concatenate(vals, 1), grad, NT)
+            ops.append((t, masks, keys, vals, s, dp))
+        for *_, s, dp in ops:
+            s, dp = s.reshape(2, FR, 128), dp.reshape(2, FR, 128)
             e = jnp.exp(s - jnp.max(s, 1, keepdims=True))
             prob = e * (1.0 / jnp.sum(e, 1, keepdims=True))
-            dp = dot(jnp.concatenate(vals, 1), grad, NT).reshape(2, FR, 128)
             delta = jnp.sum(prob * dp, 1, keepdims=True)
             ds = (prob * (dp - delta) * (HEAD**-0.5)).reshape(128, 128)
             prob = prob.reshape(128, 128)
-            pb, db = prob.astype(BF16), ds.astype(BF16)
+            soft.append((prob, ds))
+        for (t, masks, keys, vals, _, _), (prob, ds) in zip(ops, soft):
             pt, dt = prob.T.astype(BF16), ds.T.astype(BF16)
+            cols = slice(128 * t, 128 * (t + 1))
             out = jnp.concatenate([dot(pt[:FR], vals[0]), dot(pt[FR:], vals[1])], 0)
             gq = jnp.concatenate([dot(dt[:FR], keys[0]), dot(dt[FR:], keys[1])], 0)
-            gk = own_features(dot(db, query), masks)
-            gv = own_features(dot(pb, grad), masks)
+            gk = own_rows(dot(by_position(ds), unit_of(qn, rows, t)), masks)
+            gv = own_rows(dot(by_position(prob), unit_of(gatt, rows, t)), masks)
             att[rows, cols] = out[:, :128].astype(BF16)
             dq[rows, cols] = gq[:, :128].astype(BF16)
             dk[rows, cols] = gk[:, :128].astype(BF16)
@@ -355,17 +466,15 @@
     def out_project(first, size):
         cols = slice(first, first + size)
         y = dot(att[...], wout[:, cols])
-        sums[2:3, cols] = jnp.sum(cp[:, cols] * y, 0, keepdims=True)
+        sums[2:3, cols] += jnp.sum(cp[:, cols] * y, 0, keepdims=True)
         value = xp[:, cols] + mod_ref[2:3, cols] * y
         for c in range(size // LANES):
             for p in range(POS):
-                frames[first // LANES + c, at_position(p), :] = value[
-                    p * FR : (p + 1) * FR, c * LANES : (c + 1) * LANES
-                ]
-
-    for first in range(0, D, 384):
-        out_project(first, 384)
-    drain(0)
+                tile = value[p * FR : (p + 1) * FR, c * LANES : (c + 1) * LANES]
+                scatter(first // LANES + c, p, 0, tile)
+
+    for first in range(0, D, BLOCK):
+        out_project(first, min(BLOCK, D - first))
 
     def heads_grad(rows):
         for part, (d_ref, r_ref) in enumerate(((dq, rq), (dk, rk))):
@@ -412,31 +521,36 @@
         second = jnp.sum(sum(g * u for g, u in zip(scaled, units)), -1, keepdims=True) * (1.0 / D)
         inv = istd[rows, :]
         for c, cols in enumerate(lane_tiles()):
-            frames[c, at_position(p), :] = cp[rows, cols] + inv * (
-                scaled[c] - first - units[c] * second
-            )
+            value = cp[rows, cols] + inv * (scaled[c] - first - units[c] * second)
+            scatter(c, p, 8, value)
 
     loop(POS, layer)
-    drain(16)
-
-    total = sums[...]
-    folded = sum(dot(part, fold[...]) for part in terms(total))
-    gains = jnp.concatenate([folded[3:4], folded[4:5], jnp.zeros((1, D - 256), F32)], 1)
-    total = jnp.concatenate([total[:3], gains], 0)
-    rows = jnp.concatenate([part.astype(F32) for part in terms(total)] + [jnp.zeros((4, D), F32)], 0)
-    out_ref[:, 32:, :] = jnp.broadcast_to(rows.astype(BF16)[None], (ranks, SUMS, D))
-
-
-def run_sub_block(frame_counts, arrived, modulation, gains, wqkv, wout):
+
+    if last:
+        total = sums[...]
+        folded = sum(dot(part, fold[...]) for part in terms(total))
+        gains = jnp.concatenate([folded[3:4], folded[4:5], jnp.zeros((1, D - 256), F32)], 1)
+        high, low, _ = terms(jnp.concatenate([total[:3], gains], 0))
+        sent = jnp.concatenate([high.astype(F32), low.astype(F32)], 0)
+    for c, cols in enumerate(lane_tiles()):
+        block = frames[c].reshape(ranks, ROWS_IN, LANES)
+        if last:
+            rows = jnp.broadcast_to(sent[None, :, cols], (ranks, SUMS, LANES))
+            block = jnp.concatenate([block, rows], 1)
+        out_ref[:, :, cols] = block.astype(BF16)
+
+
+def run_sub_block(last, frame_counts, arrived, modulation, gains, weights, before):
     ranks = arrived.shape[0]
     tok = (TOK, D)
     any_space = pl.BlockSpec(memory_space=pl.ANY)
     vmem = pl.BlockSpec(memory_space=pltpu.VMEM)
     scratch = [
+        pltpu.VMEM((ranks, ROWS_IN, D), BF16),
         pltpu.VMEM((D, 3 * D), BF16),
         pltpu.VMEM((D, D), BF16),
-        pltpu.SemaphoreType.DMA((2,)),
-        pltpu.VMEM((TILES, TOK, LANES), F32),
+        pltpu.SemaphoreType.DMA((3,)),
+        pltpu.VMEM((TILES, ranks * ROWS_IN, LANES), F32),
         pltpu.VMEM(tok, F32),
         pltpu.VMEM(tok, F32),
         pltpu.VMEM((TOK, LANES), F32),
@@ -453,62 +567,68 @@
         pltpu.VMEM(tok, BF16),
         pltpu.VMEM(tok, BF16),
         pltpu.VMEM((TOK, 3 * D), BF16),
-        pltpu.VMEM((8, D), F32),
         pltpu.VMEM((D, REST), BF16),
         pltpu.VMEM((2 * REST, MAIN), BF16),
         pltpu.VMEM((D, REST), BF16),
         pltpu.VMEM((128, 128), F32),
+        pltpu.VMEM((3, D), F32),
+        pltpu.VMEM((2, D), F32),
     ]
+    sent = ROWS_IN + SUMS if last else ROWS_IN
     return pl.pallas_call(
-        sub_block,
-        in_specs=[pl.BlockSpec(memory_space=pltpu.SMEM), vmem, vmem, vmem, any_space, any_space],
-        out_specs=vmem,
-        out_shape=jax.ShapeDtypeStruct((ranks, SENT, D), BF16),
+        functools.partial(sub_block, last),
+        in_specs=[pl.BlockSpec(memory_space=pltpu.SMEM)]
+        + [any_space]
+        + [vmem] * 4
+        + [any_space, any_space, vmem],
+        out_specs=[vmem, vmem],
+        out_shape=[
+            jax.ShapeDtypeStruct((ranks, sent, D), BF16),
+            jax.ShapeDtypeStruct((8, D), F32),
+        ],
         scratch_shapes=scratch,
         compiler_params=pltpu.CompilerParams(vmem_limit_bytes=VMEM),
         cost_estimate=pl.CostEstimate(
-            flops=17_000_000_000, bytes_accessed=20_000_000, transcendentals=0
+            flops=12_000_000_000, bytes_accessed=20_000_000, transcendentals=0
         ),
         name="sub_block",
-    )(frame_counts, arrived, modulation, gains, wqkv, wout)
-
-
-def sum_over(value, axis, size):
-    step = 1
-    while step < size:
-        value = value + lax.ppermute(value, axis, [(i, i ^ step) for i in range(size)])
-        step *= 2
-    return value
-
-
-def split_gain(gain):
-    return jnp.concatenate([jnp.tile(gain[:64], HEADS), jnp.tile(gain[64:], HEADS)])
+    )(frame_counts, arrived, *modulation, *gains, *weights, before)
+
+
+def sum_clips(value):
+    clips = lax.axis_size("dp")
+    one, two, three = (
+        lax.ppermute(value, "dp", [(i, i ^ step) for i in range(clips)]) for step in (1, 2, 3)
+    )
+    return (value + one) + (two + three)
 
 
 def shards(latents, frame_counts, mod_table, clip_mod, q_gain, k_gain, w_qkv, w_out, cotangent):
     ranks = lax.axis_size("seq")
-    modulation = mod_table + clip_mod[0]
-    gains = jnp.stack([split_gain(q_gain), split_gain(k_gain)])
+    modulation = (mod_table, clip_mod[0])
+    gains = (q_gain[None], k_gain[None])
 
     def exchange(rows):
         return lax.all_to_all(rows, "seq", split_axis=0, concat_axis=0, tiled=True)
 
-    def outgoing(array):
-        return array.reshape(2, ranks, POS, D).transpose(1, 0, 2, 3).reshape(ranks, 16, D)
-
-    def incoming(array):
-        return array.reshape(ranks, 2, POS, D).transpose(1, 0, 2, 3).reshape(latents.shape)
-
-    arrived = exchange(jnp.concatenate([outgoing(latents), outgoing(cotangent)], 1))
-    wqkv, wout = split_weights(w_qkv, w_out)
-    out = run_sub_block(frame_counts, arrived, modulation, gains, wqkv, wout)
-    back = exchange(out)
-    pieces = jnp.sum(back[:, 32:, :].astype(F32), 0)
-    clip_total = pieces[0:4] + pieces[4:8] + pieces[8:12]
-    total = sum_over(clip_total, "dp", lax.axis_size("dp"))
+    weights = split_weights(w_qkv, w_out)
+    arrived = [
+        exchange(pack(latents, cotangent, 0)),
+        exchange(pack(latents, cotangent, 1, after=weights[1:])),
+    ]
+    sums = jnp.zeros((8, D), F32)
+    back = []
+    for i in range(CHUNKS):
+        last = i == CHUNKS - 1
+        out, sums = run_sub_block(last, frame_counts, arrived[i], modulation, gains, weights, sums)
+        back.append(exchange(tie(out, back[0]) if last else out))
+    pieces = jnp.sum(back[-1][:, ROWS_IN:, :].astype(F32), 0)
+    clip_total = pieces[0:4] + pieces[4:8]
+    total = sum_clips(clip_total)
+    block_out, input_grad = unpack(*back, latents.shape)
     return (
-        incoming(back[:, :16, :]),
-        incoming(back[:, 16:32, :]),
+        block_out,
+        input_grad,
         clip_total[None, :3],
         total[:3],
         total[3, :HEAD],

time: 151 us -> 134 us (0.89)
  blocking collectives: 48.1 us -> 32.3 us
  starting transfers between devices: 13.3 us -> 24.1 us
  waiting for transfers between devices: 13.9 us -> 3.55 us
  Pallas kernels: 59.4 us -> 66.7 us
  local copies, waits for them, and re-layouts: 11.2 us -> 4.47 us
  other arithmetic: 3.81 us -> 0.12 us
    all_to_all x1, blocking collectives: 48.1 us -> 32.3 us  [exchange(): return lax.all_to_all(rows, 'seq', split_axis=0, concat_axis=0, tiled=True)]
    all_to_all x1 -> x3, starting transfers between devices: 8.38 us -> 19.8 us  [exchange(): return lax.all_to_all(rows, 'seq', split_axis=0, concat_axis=0, tiled=True)]
    all_to_all x1 -> x3, waiting for transfers between devices: 11.7 us -> 3.54 us  [exchange(): return lax.all_to_all(rows, 'seq', split_axis=0, concat_axis=0, tiled=True)]
    pallas_call x3 -> x7, Pallas kernels: 59.4 us -> 66.7 us  [the longest x2 43.2 us: run_sub_block(): pl.pallas_call(functools.partial(sub_block, last), in_specs=[pl.BlockSpec...]
    another operation x10 -> x0, local copies, waits for them, and re-layouts: 2.76 us -> none  [the longest x4 1.39 us: split_gain(): jnp.tile(gain[:64], HEADS)]
    concatenate x3 -> x0, other arithmetic: 2.4 us -> none  [the longest x1 1.68 us: shards(): jnp.concatenate([outgoing(latents), outgoing(cotangent)], 1)]
    transpose x3 -> x0, local copies, waits for them, and re-layouts: 2.39 us -> none  [incoming(): array.reshape(ranks, 2, POS, D).transpose(1, 0, 2, 3).reshape(latents.shape)]
    ppermute x2 -> x3, waiting for transfers between devices: 2.18 us -> 0.01 us  [sum_clips(): lax.ppermute(value, 'dp', [(i, i ^ step) for i in range(clips)])]
  transfers between devices with their start and end apart: 3 -> 6, of which waited for: 2 -> 1; matrix products, arithmetic and copies ran while one was open for 6% -> 1% of each run, Pallas kernels for 10% -> 47%
where the time goes in v3:
time: 134 us; the launch traced here: 133 us
  Pallas kernels  66.7 us (50%)
  blocking collectives  32.3 us (24%)
  starting transfers between devices  24.1 us (18%)
  local copies, waits for them, and re-layouts  4.47 us (3%)
  waiting for transfers between devices  3.55 us (3%)
  between operations  1.41 us (1%)
    pallas_call x2, Pallas kernels, run_sub_block(): pl.pallas_call(functools.partial(sub_block, last), in_specs=[pl.BlockSpec...  43.2 us
    all_to_all x1, blocking collectives, exchange(): return lax.all_to_all(rows, 'seq', split_axis=0, concat_axis=0, tiled=True)  32.3 us
    all_to_all x3, starting transfers between devices, exchange(): return lax.all_to_all(rows, 'seq', split_axis=0, concat_axis=0, tiled=True)  19.8 us
    pallas_call x1, Pallas kernels, split_weights(): pl.pallas_call(split_weights_kernel, grid=(steps,), in_specs=[pl.BlockSpe...  11.7 us
    pallas_call x2, Pallas kernels, pack(): pl.pallas_call(functools.partial(pack_kernel, chunk), grid=(steps,), in_s...  7.56 us
    ppermute x3, starting transfers between devices, sum_clips(): lax.ppermute(value, 'dp', [(i, i ^ step) for i in range(clips)])  4.32 us
    pallas_call x1, Pallas kernels, unpack(): pl.pallas_call(unpack_kernel, grid=(steps,), in_specs=[pl.BlockSpec((x.sh...  4.19 us
    all_to_all x3, waiting for transfers between devices, exchange(): return lax.all_to_all(rows, 'seq', split_axis=0, concat_axis=0, tiled=True)  3.54 us
  transfers between devices with their start and end apart: 6, of which 1 were waited for; matrix products, arithmetic and copies ran while one was open for 1% of the time, Pallas kernels for 47%

profile of v3, /device:TPU:0, one launch (start us, length us, event | category | flops | bytes accessed | tf_op | source)
XLA Modules:
  0.0 132.7 jit_solution(11215059480720231754)
XLA Ops:
  0.6 3.8 %pack.2 = bf16[32,16,1152]{2,1,0:T(8,128)(2,1)} custom-call(bf16[1,2,256,1152]{3,2,1,0:T(8,128)(2,1)} %lat_ref.3, bf16[1,2,256,1152]{3,2,1,0:T(8,128)(2,1)} %cot_ref.3), custom_call_target="tpu_custom_call" | custom-call | flops 4000000 | bytes 3600000 | tf_op jit(solution)/shard_map/pack/pallas_call | solution.py:140
  4.4 8.2 %all-to-all-start = ((bf16[32,16,1152]{2,1,0:T(8,128)(2,1)}), bf16[32,16,1152]{2,1,0:T(8,128)(2,1)S(1)}, u32[]{:S(2)}, u32[]{:S(2)}) async-start(bf16[32,16,1152]{2,1,0:T(8,128)(2,1)} %pack.2), calls=%async_computation | async-start | bytes 2359296 | tf_op jit(solution)/shard_map/all_to_all | solution.py:612
  12.7 11.7 %split_weights.1 = (bf16[1152,3456]{1,0:T(8,128)(2,1)}, bf16[1152,1152]{1,0:T(8,128)(2,1)}) custom-call(bf16[1152,3456]{1,0:T(8,128)(2,1)} %qkv_ref.1, bf16[1152,1152]{1,0:T(8,128)(2,1)} %out_ref.1), custom_call_target="tpu_custom_call" | custom-call | flops 4246732800 | bytes 21233664 | tf_op jit(solution)/shard_map/split_weights/pallas_call | solution.py:92
  24.4 3.8 %pack.3 = bf16[32,16,1152]{2,1,0:T(8,128)(2,1)} custom-call(bf16[1,2,256,1152]{3,2,1,0:T(8,128)(2,1)} %lat_ref.3, bf16[1,2,256,1152]{3,2,1,0:T(8,128)(2,1)} %cot_ref.3, bf16[1152,1152]{1,0:T(8,128)(2,1)} %get-tuple-element.14.wout_hbm.refs_0_), custom_call_target="tpu_custom_call" | custom-call | flops 4000000 | bytes 3600000 | tf_op jit(solution)/shard_map/pack/pallas_call | solution.py:140
  28.2 3.5 %all-to-all-done.in_hbm = bf16[32,16,1152]{2,1,0:T(8,128)(2,1)S(1)} async-done(((bf16[32,16,1152]{2,1,0:T(8,128)(2,1)}), bf16[32,16,1152]{2,1,0:T(8,128)(2,1)S(1)}, u32[]{:S(2)}, u32[]{:S(2)}) %all-to-all-start) | async-done | bytes 1179680 | tf_op jit(solution)/shard_map/all_to_all | solution.py:612
  31.7 4.1 %all-to-all-start.2 = ((bf16[32,16,1152]{2,1,0:T(8,128)(2,1)}), bf16[32,16,1152]{2,1,0:T(8,128)(2,1)S(1)}, u32[]{:S(2)}, u32[]{:S(2)}) async-start(bf16[32,16,1152]{2,1,0:T(8,128)(2,1)} %pack.3), calls=%async_computation.2 | async-start | bytes 2359296 | tf_op jit(solution)/shard_map/all_to_all | solution.py:612
  36.5 0.6 copy.18
  37.1 0.6 broadcast_in_dim.14.before_ref
  37.7 21.3 %sub_block.2 = (bf16[32,16,1152]{2,1,0:T(8,128)(2,1)}, f32[8,1152]{1,0:T(8,128)}) custom-call(s32[1]{0:T(128)S(6)} %copy.20.count_ref, bf16[32,16,1152]{2,1,0:T(8,128)(2,1)} %copy-done.3, f32[3,1152]{1,0:T(4,128)} %table_ref.3, f32[3,1152]{1,0:T(4,128)} %bitcast.13, f32[1,72]{1,0:T(1,128)} %bitcast.15, f32[1,72]{1,0:T(1,128)} %bitcast.17, ...), custom_call_target="tpu_custom_call" | custom-call | flops 12000000000 | bytes 20000000 | tf_op jit(solution)/shard_map/sub_block/pallas_call | solution.py:578
  59.0 0.0 copy-start.2
  59.0 1.0 copy-done.2
  60.0 7.4 %all-to-all-start.1 = ((bf16[32,16,1152]{2,1,0:T(8,128)(2,1)}), bf16[32,16,1152]{2,1,0:T(8,128)(2,1)S(1)}, u32[]{:S(2)}, u32[]{:S(2)}) async-start(bf16[32,16,1152]{2,1,0:T(8,128)(2,1)} %get-tuple-element.15), calls=%async_computation.1 | async-start | bytes 2359296 | tf_op jit(solution)/shard_map/all_to_all | solution.py:612
  67.5 21.9 %sub_block.3 = (bf16[32,24,1152]{2,1,0:T(8,128)(2,1)}, f32[8,1152]{1,0:T(8,128)}) custom-call(s32[1]{0:T(128)S(6)} %copy.20.count_ref, bf16[32,16,1152]{2,1,0:T(8,128)(2,1)} %copy-done.2, f32[3,1152]{1,0:T(4,128)} %table_ref.3, f32[3,1152]{1,0:T(4,128)} %bitcast.14, f32[1,72]{1,0:T(1,128)} %bitcast.16, f32[1,72]{1,0:T(1,128)} %bitcast.18, ...), custom_call_target="tpu_custom_call" | custom-call | flops 12000000000 | bytes 20000000 | tf_op jit(solution)/shard_map/sub_block/pallas_call | solution.py:578
  89.4 0.0 all-to-all-done.1.other_ref.first_ref
  89.4 1.0 copy-done
  90.5 32.3 %all_to_all.20.second_ref = bf16[32,24,1152]{2,1,0:T(8,128)(2,1)S(1)} all-to-all(bf16[32,24,1152]{2,1,0:T(8,128)(2,1)} %tie.1), channel_id=1, replica_groups=mesh['seq'=32,'dp'=4] {'seq'}, dimensions={0} | all-to-all | bytes 3538944 | tf_op jit(solution)/shard_map/all_to_all | solution.py:612
  122.8 0.1 convert_reduce_fusion
  122.9 3.3 %collective-permute-start.1 = (f32[4,1152]{1,0:T(4,128)S(1)}, f32[4,1152]{1,0:T(4,128)S(1)}, u32[]{:S(2)}, u32[]{:S(2)}) collective-permute-start(f32[4,1152]{1,0:T(4,128)S(1)} %slice_add_fusion), channel_id=1, source_target_pairs={{0,2},{1,3},{2,0},{3,1},{4,6},{5,7},{6,4},{7,5},{8,10},{9,11},{10,... | collective-permute-start | bytes 55304 | tf_op jit(solution)/shard_map/ppermute | solution.py:601
  126.2 1.1 collective-permute-start.2
  127.2 0.6 broadcast_in_dim.15
  127.8 4.2 %unpack.1 = (bf16[1,2,256,1152]{3,2,1,0:T(8,128)(2,1)}, bf16[1,2,256,1152]{3,2,1,0:T(8,128)(2,1)}) custom-call(bf16[32,16,1152]{2,1,0:T(8,128)(2,1)} %copy-done, bf16[32,24,1152]{2,1,0:T(8,128)(2,1)} %copy-done.1), custom_call_target="tpu_custom_call" | custom-call | flops 4000000 | bytes 5000000 | tf_op jit(solution)/shard_map/unpack/pallas_call | solution.py:184
  132.1 0.0 copy-start.4
  132.1 0.5 slice_bitcast_fusion
  132.6 0.1 copy-done.4
  (15 shorter events, 0.1 us)
Async XLA Ops:
  4.4 27.3 %all-to-all-start = ((bf16[32,16,1152]{2,1,0:T(8,128)(2,1)}), bf16[32,16,1152]{2,1,0:T(8,128)(2,1)S(1)}, u32[]{:S(2)}, u32[]{:S(2)}) async-start(bf16[32,16,1152]{2,1,0:T(8,128)(2,1)} %pack.2), calls=%async_computation | async-start | bytes 2359296 | tf_op jit(solution)/shard_map/all_to_all | solution.py:612
  28.2 8.3 %copy-start.5 = (f32[1,3,1152]{2,0,1:T(1,128)S(1)}, f32[1,3,1152]{2,0,1:T(1,128)}, u32[]{:S(2)}) copy-start(f32[1,3,1152]{2,0,1:T(1,128)} %param.12) | copy-start | bytes 41476
  31.7 4.8 %copy-start.3 = (bf16[32,16,1152]{2,1,0:T(8,128)(2,1)}, bf16[32,16,1152]{2,1,0:T(8,128)(2,1)S(1)}, u32[]{:S(2)}) copy-start(bf16[32,16,1152]{2,1,0:T(8,128)(2,1)S(1)} %all-to-all-done.in_hbm) | copy-start | bytes 3538948
  31.7 27.3 %all-to-all-start.2 = ((bf16[32,16,1152]{2,1,0:T(8,128)(2,1)}), bf16[32,16,1152]{2,1,0:T(8,128)(2,1)S(1)}, u32[]{:S(2)}, u32[]{:S(2)}) async-start(bf16[32,16,1152]{2,1,0:T(8,128)(2,1)} %pack.3), calls=%async_computation.2 | async-start | bytes 2359296 | tf_op jit(solution)/shard_map/all_to_all | solution.py:612
  59.0 1.0 copy-start.2
  60.0 29.4 %all-to-all-start.1 = ((bf16[32,16,1152]{2,1,0:T(8,128)(2,1)}), bf16[32,16,1152]{2,1,0:T(8,128)(2,1)S(1)}, u32[]{:S(2)}, u32[]{:S(2)}) async-start(bf16[32,16,1152]{2,1,0:T(8,128)(2,1)} %get-tuple-element.15), calls=%async_computation.1 | async-start | bytes 2359296 | tf_op jit(solution)/shard_map/all_to_all | solution.py:612
  89.4 1.0 copy-start
  122.8 5.0 %copy-start.1 = (bf16[32,24,1152]{2,1,0:T(8,128)(2,1)}, bf16[32,24,1152]{2,1,0:T(8,128)(2,1)S(1)}, u32[]{:S(2)}) copy-start(bf16[32,24,1152]{2,1,0:T(8,128)(2,1)S(1)} %all_to_all.20.second_ref) | copy-start | bytes 5308420
  122.9 9.1 %collective-permute-start.1 = (f32[4,1152]{1,0:T(4,128)S(1)}, f32[4,1152]{1,0:T(4,128)S(1)}, u32[]{:S(2)}, u32[]{:S(2)}) collective-permute-start(f32[4,1152]{1,0:T(4,128)S(1)} %slice_add_fusion), channel_id=1, source_target_pairs={{0,2},{1,3},{2,0},{3,1},{4,6},{5,7},{6,4},{7,5},{8,10},{9,11},{10,... | collective-permute-start | bytes 55304 | tf_op jit(solution)/shard_map/ppermute | solution.py:601
  126.2 5.9 %collective-permute-start.2 = (f32[4,1152]{1,0:T(4,128)S(1)}, f32[4,1152]{1,0:T(4,128)S(1)}, u32[]{:S(2)}, u32[]{:S(2)}) collective-permute-start(f32[4,1152]{1,0:T(4,128)S(1)} %slice_add_fusion), channel_id=1, source_target_pairs={{0,3},{1,2},{2,1},{3,0},{4,7},{5,6},{6,5},{7,4},{8,11},{9,10},{10,... | collective-permute-start | bytes 55304 | tf_op jit(solution)/shard_map/ppermute | solution.py:601
  127.2 4.8 %collective-permute-start = (f32[4,1152]{1,0:T(4,128)S(1)}, f32[4,1152]{1,0:T(4,128)S(1)}, u32[]{:S(2)}, u32[]{:S(2)}) collective-permute-start(f32[4,1152]{1,0:T(4,128)S(1)} %slice_add_fusion), channel_id=1, source_target_pairs={{0,1},{1,0},{2,3},{3,2},{4,5},{5,4},{6,7},{7,6},{8,9},{9,8},{10,11... | collective-permute-start | bytes 55304 | tf_op jit(solution)/shard_map/ppermute | solution.py:601
  132.1 0.6 copy-start.4

commit v4 on v3

--- a/solution.py
+++ b/solution.py
@@ -134,7 +134,7 @@
 
 def pack(latents, cotangent, chunk, after=()):
     _, frames, positions, width = latents.shape
-    steps = 4
+    steps = 2
     ranks = positions // 8
     spec = pl.BlockSpec((1, frames, positions // steps, width), lambda i: (0, 0, i, 0))
     return pl.pallas_call(
@@ -178,14 +178,14 @@
 
 def unpack(first, second, shape):
     _, frames, positions, width = shape
-    steps = 4
+    steps = 2
     spec = pl.BlockSpec((1, frames, positions // steps, width), lambda i: (0, 0, i, 0))
     out = jax.ShapeDtypeStruct(shape, BF16)
     return pl.pallas_call(
         unpack_kernel,
         grid=(steps,),
         in_specs=[
-            pl.BlockSpec((x.shape[0] // steps, *x.shape[1:]), lambda i: (i, 0, 0))
+            pl.BlockSpec((x.shape[0] // steps, ROWS_IN, width), lambda i: (i, 0, 0))
             for x in (first, second)
         ],
         out_specs=[spec, spec],
@@ -274,13 +274,13 @@
 
 
 def over_columns(total, body):
-    loop(total // BLOCK, lambda b: body(pl.ds(pl.multiple_of(b * BLOCK, BLOCK), BLOCK)))
-    if total % BLOCK:
-        body(pl.ds(total // BLOCK * BLOCK, total % BLOCK))
+    for b in range(0, total, BLOCK):
+        body(slice(b, min(b + BLOCK, total)))
 
 
 def over_rows(size, body):
-    loop(TOK // size, lambda i: body(pl.ds(pl.multiple_of(i * size, size), size)))
+    for i in range(0, TOK, size):
+        body(slice(i, i + size))
 
 
 def lane_tiles():
@@ -291,15 +291,21 @@
     last,
     count_ref,
     in_hbm,
+    table_hbm,
+    clip_hbm,
+    q_gain_hbm,
+    k_gain_hbm,
+    wqkv_hbm,
+    wout_hbm,
+    before_hbm,
+    out_hbm,
+    sums,
+    out_ref,
     table_ref,
     clip_ref,
     q_gain_ref,
     k_gain_ref,
-    wqkv_hbm,
-    wout_hbm,
     before_ref,
-    out_ref,
-    sums,
     in_ref,
     wqkv,
     wout,
@@ -333,13 +339,29 @@
     load_qkv = pltpu.make_async_copy(wqkv_hbm, wqkv, sems.at[0])
     load_out = pltpu.make_async_copy(wout_hbm, wout, sems.at[1])
     load_in = pltpu.make_async_copy(in_hbm, in_ref, sems.at[2])
+    small = [
+        pltpu.make_async_copy(source, target, sems.at[3 + i])
+        for i, (source, target) in enumerate(
+            (
+                (table_hbm, table_ref),
+                (clip_hbm, clip_ref),
+                (q_gain_hbm, q_gain_ref),
+                (k_gain_hbm, k_gain_ref),
+                (before_hbm, before_ref),
+            )
+        )
+    ]
     load_in.start()
+    for copy in small:
+        copy.start()
     load_out.start()
     load_qkv.start()
     init_segments(seg, spread, fold)
     key = iota((128, 128), 0) & (FR - 1)
     valid = 2 * (key & 31) + (key >> 5) < count_ref[0]
     bias[...] = jnp.where(valid, jnp.float32(0), jnp.float32(-1e30))
+    for copy in small:
+        copy.wait()
     sums[...] = before_ref[...]
     mod_ref[...] = table_ref[...] + clip_ref[...]
     for part, ref in enumerate((q_gain_ref, k_gain_ref)):
@@ -356,6 +378,8 @@
             frames[c, strided(p, first, own), :] = value[own * ranks : (own + 1) * ranks]
 
     def position_rows(p):
+        if isinstance(p, int):
+            return slice(p * FR, (p + 1) * FR)
         return pl.ds(pl.multiple_of(p * FR, FR), FR)
 
     load_in.wait()
@@ -384,13 +408,18 @@
             normed[rows, cols] = (u * (1.0 + mod_ref[1:2, cols]) + mod_ref[0:1, cols]).astype(BF16)
 
     loop(POS, arrive)
-    loop(POS, norm)
 
     def grad_attention(cols):
         gatt[:, cols] = dot(gy[...], wout[cols, :], NT).astype(BF16)
 
     load_out.wait()
-    over_columns(D, grad_attention)
+    norm(0)
+    grad_attention(slice(0, BLOCK))
+    norm(1)
+    grad_attention(slice(BLOCK, 2 * BLOCK))
+    norm(2)
+    grad_attention(slice(2 * BLOCK, D))
+    norm(3)
 
     def project(cols):
         proj[:, cols] = dot(normed[...], wqkv[:, cols])
@@ -399,30 +428,34 @@
     over_columns(QK, project)
 
     def project_values(cols):
-        vn[:, cols] = dot(normed[...], wqkv[:, pl.ds(QK + cols.start, cols.size)]).astype(BF16)
-
-    over_columns(D, project_values)
-
-    def heads(rows):
-        for part, (n_ref, r_ref) in enumerate(((qn, rq), (kn, rk))):
-            main = slice(MAIN_AT[part], MAIN_AT[part] + MAIN)
-            rest = slice(REST_AT[part], REST_AT[part] + REST)
-            m, t = proj[rows, main], proj[rows, rest]
-            total = sum(dot(part, seg[:MAIN, :]) for part in terms(m * m)[:2])
-            total = total + sum(dot(part, seg[MAIN:, :]) for part in terms(t * t)[:2])
-            inv = lax.rsqrt(total * (1.0 / HEAD) + EPS)
-            r_ref[rows, :] = inv
-            pair = both(inv)
-            for b in range(0, MAIN, 256):
-                cols = slice(MAIN_AT[part] + b, MAIN_AT[part] + b + 256)
-                hat = proj[rows, cols] * dot(pair, spread[:, b : b + 256])
-                proj[rows, cols] = hat
-                n_ref[rows, b : b + 256] = (hat * gain_ref[part : part + 1, b : b + 256]).astype(BF16)
-            hat = t * inv
-            proj[rows, rest] = hat
-            n_ref[rows, MAIN:] = (hat * gain_ref[part : part + 1, MAIN:]).astype(BF16)
-
-    over_rows(256, heads)
+        vn[:, cols] = dot(normed[...], wqkv[:, QK + cols.start : QK + cols.stop]).astype(BF16)
+
+
+    def heads(part, n_ref, r_ref, rows):
+        main = slice(MAIN_AT[part], MAIN_AT[part] + MAIN)
+        rest = slice(REST_AT[part], REST_AT[part] + REST)
+        m, t = proj[rows, main], proj[rows, rest]
+        total = sum(dot(part, seg[:MAIN, :]) for part in terms(m * m)[:2])
+        total = total + sum(dot(part, seg[MAIN:, :]) for part in terms(t * t)[:2])
+        inv = lax.rsqrt(total * (1.0 / HEAD) + EPS)
+        r_ref[rows, :] = inv
+        pair = both(inv)
+        for b in range(0, MAIN, 256):
+            cols = slice(MAIN_AT[part] + b, MAIN_AT[part] + b + 256)
+            hat = proj[rows, cols] * dot(pair, spread[:, b : b + 256])
+            proj[rows, cols] = hat
+            n_ref[rows, b : b + 256] = (hat * gain_ref[part : part + 1, b : b + 256]).astype(BF16)
+        hat = t * inv
+        proj[rows, rest] = hat
+        n_ref[rows, MAIN:] = (hat * gain_ref[part : part + 1, MAIN:]).astype(BF16)
+
+
+    everything = slice(0, TOK)
+    project_values(slice(0, BLOCK))
+    heads(0, qn, rq, everything)
+    project_values(slice(BLOCK, 2 * BLOCK))
+    heads(1, kn, rk, everything)
+    project_values(slice(2 * BLOCK, D))
 
     def attend(rows):
         rest = [jnp.zeros((ROWS, REST), F32)] * 4
@@ -473,35 +506,37 @@
                 tile = value[p * FR : (p + 1) * FR, c * LANES : (c + 1) * LANES]
                 scatter(first // LANES + c, p, 0, tile)
 
-    for first in range(0, D, BLOCK):
-        out_project(first, min(BLOCK, D - first))
-
-    def heads_grad(rows):
-        for part, (d_ref, r_ref) in enumerate(((dq, rq), (dk, rk))):
-            main = slice(MAIN_AT[part], MAIN_AT[part] + MAIN)
-            rest = slice(REST_AT[part], REST_AT[part] + REST)
-            gain = gain_ref[part : part + 1, :]
-            row = slice(3 + part, 4 + part)
-            um, ur = d_ref[rows, :MAIN].astype(F32), d_ref[rows, MAIN:].astype(F32)
-            wm, wr = um * proj[rows, main], ur * proj[rows, rest]
-            sums[row, :MAIN] += jnp.sum(wm, 0, keepdims=True)
-            sums[row, MAIN:] += jnp.sum(wr, 0, keepdims=True)
-            total = dot((wm * gain[:, :MAIN]).astype(BF16), seg[:MAIN, :]) + dot(
-                (wr * gain[:, MAIN:]).astype(BF16), seg[MAIN:, :]
-            )
-            inner = total * (1.0 / HEAD)
-            inv = r_ref[rows, :]
-            pair, inner_pair = both(inv), both(inner)
-            for b in range(0, MAIN, 256):
-                cols = slice(MAIN_AT[part] + b, MAIN_AT[part] + b + 256)
-                a = d_ref[rows, b : b + 256].astype(F32) * gain[:, b : b + 256]
-                picked = spread[:, b : b + 256]
-                value = dot(pair, picked) * (a - proj[rows, cols] * dot(inner_pair, picked))
-                dqkv[rows, cols] = value.astype(BF16)
-            value = inv * (ur * gain[:, MAIN:] - proj[rows, rest] * inner)
-            dqkv[rows, rest] = value.astype(BF16)
-
-    over_rows(256, heads_grad)
+
+    def heads_grad(part, d_ref, r_ref, rows):
+        main = slice(MAIN_AT[part], MAIN_AT[part] + MAIN)
+        rest = slice(REST_AT[part], REST_AT[part] + REST)
+        gain = gain_ref[part : part + 1, :]
+        row = slice(3 + part, 4 + part)
+        um, ur = d_ref[rows, :MAIN].astype(F32), d_ref[rows, MAIN:].astype(F32)
+        wm, wr = um * proj[rows, main], ur * proj[rows, rest]
+        sums[row, :MAIN] += jnp.sum(wm, 0, keepdims=True)
+        sums[row, MAIN:] += jnp.sum(wr, 0, keepdims=True)
+        total = dot((wm * gain[:, :MAIN]).astype(BF16), seg[:MAIN, :]) + dot(
+            (wr * gain[:, MAIN:]).astype(BF16), seg[MAIN:, :]
+        )
+        inner = total * (1.0 / HEAD)
+        inv = r_ref[rows, :]
+        pair, inner_pair = both(inv), both(inner)
+        for b in range(0, MAIN, 256):
+            cols = slice(MAIN_AT[part] + b, MAIN_AT[part] + b + 256)
+            a = d_ref[rows, b : b + 256].astype(F32) * gain[:, b : b + 256]
+            picked = spread[:, b : b + 256]
+            value = dot(pair, picked) * (a - proj[rows, cols] * dot(inner_pair, picked))
+            dqkv[rows, cols] = value.astype(BF16)
+        value = inv * (ur * gain[:, MAIN:] - proj[rows, rest] * inner)
+        dqkv[rows, rest] = value.astype(BF16)
+
+
+    out_project(0, BLOCK)
+    heads_grad(0, dq, rq, everything)
+    out_project(BLOCK, BLOCK)
+    heads_grad(1, dk, rk, everything)
+    out_project(2 * BLOCK, D - 2 * BLOCK)
 
     def grad_normed(cols):
         gn[:, cols] = dot(dqkv[...], wqkv[cols, :], NT).astype(BF16)
@@ -524,7 +559,8 @@
             value = cp[rows, cols] + inv * (scaled[c] - first - units[c] * second)
             scatter(c, p, 8, value)
 
-    loop(POS, layer)
+    for p in range(POS):
+        layer(p)
 
     if last:
         total = sums[...]
@@ -538,6 +574,9 @@
             rows = jnp.broadcast_to(sent[None, :, cols], (ranks, SUMS, LANES))
             block = jnp.concatenate([block, rows], 1)
         out_ref[:, :, cols] = block.astype(BF16)
+    leave = pltpu.make_async_copy(out_ref, out_hbm, sems.at[8])
+    leave.start()
+    leave.wait()
 
 
 def run_sub_block(last, frame_counts, arrived, modulation, gains, weights, before):
@@ -545,11 +584,18 @@
     tok = (TOK, D)
     any_space = pl.BlockSpec(memory_space=pl.ANY)
     vmem = pl.BlockSpec(memory_space=pltpu.VMEM)
+    sent = ROWS_IN + SUMS if last else ROWS_IN
     scratch = [
+        pltpu.VMEM((ranks, sent, D), BF16),
+        pltpu.VMEM((3, D), F32),
+        pltpu.VMEM((3, D), F32),
+        pltpu.VMEM((1, HEAD), F32),
+        pltpu.VMEM((1, HEAD), F32),
+        pltpu.VMEM((8, D), F32),
         pltpu.VMEM((ranks, ROWS_IN, D), BF16),
         pltpu.VMEM((D, 3 * D), BF16),
         pltpu.VMEM((D, D), BF16),
-        pltpu.SemaphoreType.DMA((3,)),
+        pltpu.SemaphoreType.DMA((9,)),
         pltpu.VMEM((TILES, ranks * ROWS_IN, LANES), F32),
         pltpu.VMEM(tok, F32),
         pltpu.VMEM(tok, F32),
@@ -574,14 +620,11 @@
         pltpu.VMEM((3, D), F32),
         pltpu.VMEM((2, D), F32),
     ]
-    sent = ROWS_IN + SUMS if last else ROWS_IN
     return pl.pallas_call(
         functools.partial(sub_block, last),
         in_specs=[pl.BlockSpec(memory_space=pltpu.SMEM)]
-        + [any_space]
-        + [vmem] * 4
-        + [any_space, any_space, vmem],
-        out_specs=[vmem, vmem],
+        + [any_space] * 8,
+        out_specs=[any_space, vmem],
         out_shape=[
             jax.ShapeDtypeStruct((ranks, sent, D), BF16),
             jax.ShapeDtypeStruct((8, D), F32),

time: 134 us -> 126 us (0.940)
  Pallas kernels: 66.7 us -> 58.1 us
  waiting for transfers between devices: 3.55 us -> 5.05 us
    pallas_call x2, Pallas kernels: 43.2 us -> 38.2 us  [run_sub_block(): pl.pallas_call(functools.partial(sub_block, last), in_specs=[pl.BlockSpec...]
    pallas_call x2, Pallas kernels: 7.56 us -> 5.24 us  [pack(): pl.pallas_call(functools.partial(pack_kernel, chunk), grid=(steps,), in_s...]
  transfers between devices with their start and end apart: 6 -> 6, of which waited for: 1 -> 2; matrix products, arithmetic and copies ran while one was open for 1% -> 1% of each run, Pallas kernels for 47% -> 44%
where the time goes in v4:
time: 126 us
  Pallas kernels  58.1 us (46%)
  blocking collectives  32.5 us (26%)
  starting transfers between devices  23.9 us (19%)
  waiting for transfers between devices  5.05 us (4%)
  local copies, waits for them, and re-layouts  4.47 us (4%)
  between operations  1.4 us (1%)
    pallas_call x2, Pallas kernels, run_sub_block(): pl.pallas_call(functools.partial(sub_block, last), in_specs=[pl.BlockSpec...  38.2 us
    all_to_all x1, blocking collectives, exchange(): return lax.all_to_all(rows, 'seq', split_axis=0, concat_axis=0, tiled=True)  32.5 us
    all_to_all x3, starting transfers between devices, exchange(): return lax.all_to_all(rows, 'seq', split_axis=0, concat_axis=0, tiled=True)  19.6 us
    pallas_call x1, Pallas kernels, split_weights(): pl.pallas_call(split_weights_kernel, grid=(steps,), in_specs=[pl.BlockSpe...  11.7 us
    pallas_call x2, Pallas kernels, pack(): pl.pallas_call(functools.partial(pack_kernel, chunk), grid=(steps,), in_s...  5.24 us
    all_to_all x3, waiting for transfers between devices, exchange(): return lax.all_to_all(rows, 'seq', split_axis=0, concat_axis=0, tiled=True)  4.71 us
    ppermute x3, starting transfers between devices, sum_clips(): lax.ppermute(value, 'dp', [(i, i ^ step) for i in range(clips)])  4.32 us
    pallas_call x1, Pallas kernels, unpack(): pl.pallas_call(unpack_kernel, grid=(steps,), in_specs=[pl.BlockSpec((x.sh...  2.95 us
  transfers between devices with their start and end apart: 6, of which 2 were waited for; matrix products, arithmetic and copies ran while one was open for 1% of the time, Pallas kernels for 44%

profile of v4, /device:TPU:0, one launch (start us, length us, event | category | flops | bytes accessed | tf_op | source)
XLA Modules:
  0.0 125.6 jit_solution(10472111362008555799)
XLA Ops:
  0.6 2.6 %pack.2 = bf16[32,16,1152]{2,1,0:T(8,128)(2,1)} custom-call(bf16[1,2,256,1152]{3,2,1,0:T(8,128)(2,1)} %lat_ref.3, bf16[1,2,256,1152]{3,2,1,0:T(8,128)(2,1)} %cot_ref.3), custom_call_target="tpu_custom_call" | custom-call | flops 4000000 | bytes 3600000 | tf_op jit(solution)/shard_map/pack/pallas_call | solution.py:140
  3.3 8.2 %all-to-all-start = ((bf16[32,16,1152]{2,1,0:T(8,128)(2,1)}), bf16[32,16,1152]{2,1,0:T(8,128)(2,1)S(1)}, u32[]{:S(2)}, u32[]{:S(2)}) async-start(bf16[32,16,1152]{2,1,0:T(8,128)(2,1)} %pack.2), calls=%async_computation | async-start | bytes 2359296 | tf_op jit(solution)/shard_map/all_to_all | solution.py:655
  11.5 11.7 %split_weights.1 = (bf16[1152,3456]{1,0:T(8,128)(2,1)}, bf16[1152,1152]{1,0:T(8,128)(2,1)}) custom-call(bf16[1152,3456]{1,0:T(8,128)(2,1)} %qkv_ref.1, bf16[1152,1152]{1,0:T(8,128)(2,1)} %out_ref.1), custom_call_target="tpu_custom_call" | custom-call | flops 4246732800 | bytes 21233664 | tf_op jit(solution)/shard_map/split_weights/pallas_call | solution.py:92
  23.2 2.6 %pack.3 = bf16[32,16,1152]{2,1,0:T(8,128)(2,1)} custom-call(bf16[1,2,256,1152]{3,2,1,0:T(8,128)(2,1)} %lat_ref.3, bf16[1,2,256,1152]{3,2,1,0:T(8,128)(2,1)} %cot_ref.3, bf16[1152,1152]{1,0:T(8,128)(2,1)} %get-tuple-element.14.wout_hbm.refs_0_), custom_call_target="tpu_custom_call" | custom-call | flops 4000000 | bytes 3600000 | tf_op jit(solution)/shard_map/pack/pallas_call | solution.py:140
  25.8 4.7 %all-to-all-done.in_hbm = bf16[32,16,1152]{2,1,0:T(8,128)(2,1)S(1)} async-done(((bf16[32,16,1152]{2,1,0:T(8,128)(2,1)}), bf16[32,16,1152]{2,1,0:T(8,128)(2,1)S(1)}, u32[]{:S(2)}, u32[]{:S(2)}) %all-to-all-start) | async-done | bytes 1179680 | tf_op jit(solution)/shard_map/all_to_all | solution.py:655
  30.5 3.9 %all-to-all-start.2 = ((bf16[32,16,1152]{2,1,0:T(8,128)(2,1)}), bf16[32,16,1152]{2,1,0:T(8,128)(2,1)S(1)}, u32[]{:S(2)}, u32[]{:S(2)}) async-start(bf16[32,16,1152]{2,1,0:T(8,128)(2,1)} %pack.3), calls=%async_computation.2 | async-start | bytes 2359296 | tf_op jit(solution)/shard_map/all_to_all | solution.py:655
  35.2 0.6 copy.18
  35.8 0.6 broadcast_in_dim.14.before_hbm
  36.4 19.2 %sub_block.2 = (bf16[32,16,1152]{2,1,0:T(8,128)(2,1)}, f32[8,1152]{1,0:T(8,128)}) custom-call(s32[1]{0:T(128)S(6)} %copy.20.count_ref, bf16[32,16,1152]{2,1,0:T(8,128)(2,1)} %copy-done.3, f32[3,1152]{1,0:T(4,128)} %table_hbm.3, f32[3,1152]{1,0:T(4,128)} %bitcast.13, f32[1,72]{1,0:T(1,128)} %bitcast.15, f32[1,72]{1,0:T(1,128)} %bitcast.17, ...), custom_call_target="tpu_custom_call" | custom-call | flops 12000000000 | bytes 20000000 | tf_op jit(solution)/shard_map/sub_block/pallas_call | solution.py:623
  55.6 0.0 copy-start.2
  55.6 1.0 copy-done.2
  56.6 7.4 %all-to-all-start.1 = ((bf16[32,16,1152]{2,1,0:T(8,128)(2,1)}), bf16[32,16,1152]{2,1,0:T(8,128)(2,1)S(1)}, u32[]{:S(2)}, u32[]{:S(2)}) async-start(bf16[32,16,1152]{2,1,0:T(8,128)(2,1)} %get-tuple-element.15), calls=%async_computation.1 | async-start | bytes 2359296 | tf_op jit(solution)/shard_map/all_to_all | solution.py:655
  64.0 19.0 %sub_block.3 = (bf16[32,24,1152]{2,1,0:T(8,128)(2,1)}, f32[8,1152]{1,0:T(8,128)}) custom-call(s32[1]{0:T(128)S(6)} %copy.20.count_ref, bf16[32,16,1152]{2,1,0:T(8,128)(2,1)} %copy-done.2, f32[3,1152]{1,0:T(4,128)} %table_hbm.3, f32[3,1152]{1,0:T(4,128)} %bitcast.14, f32[1,72]{1,0:T(1,128)} %bitcast.16, f32[1,72]{1,0:T(1,128)} %bitcast.18, ...), custom_call_target="tpu_custom_call" | custom-call | flops 12000000000 | bytes 20000000 | tf_op jit(solution)/shard_map/sub_block/pallas_call | solution.py:623
  83.1 1.0 copy-done
  84.1 32.5 %all_to_all.20.second_ref = bf16[32,24,1152]{2,1,0:T(8,128)(2,1)S(1)} all-to-all(bf16[32,24,1152]{2,1,0:T(8,128)(2,1)} %tie.1), channel_id=1, replica_groups=mesh['seq'=32,'dp'=4] {'seq'}, dimensions={0} | all-to-all | bytes 3538944 | tf_op jit(solution)/shard_map/all_to_all | solution.py:655
  116.6 0.1 convert_reduce_fusion
  116.8 3.3 %collective-permute-start.1 = (f32[4,1152]{1,0:T(4,128)S(1)}, f32[4,1152]{1,0:T(4,128)S(1)}, u32[]{:S(2)}, u32[]{:S(2)}) collective-permute-start(f32[4,1152]{1,0:T(4,128)S(1)} %slice_add_fusion), channel_id=1, source_target_pairs={{0,2},{1,3},{2,0},{3,1},{4,6},{5,7},{6,4},{7,5},{8,10},{9,11},{10,... | collective-permute-start | bytes 55304 | tf_op jit(solution)/shard_map/ppermute | solution.py:644
  120.0 1.1 collective-permute-start.2
  121.1 0.6 broadcast_in_dim.15
  121.7 3.0 %unpack.1 = (bf16[1,2,256,1152]{3,2,1,0:T(8,128)(2,1)}, bf16[1,2,256,1152]{3,2,1,0:T(8,128)(2,1)}) custom-call(bf16[32,16,1152]{2,1,0:T(8,128)(2,1)} %copy-done, bf16[32,24,1152]{2,1,0:T(8,128)(2,1)} %copy-done.1), custom_call_target="tpu_custom_call" | custom-call | flops 4000000 | bytes 5000000 | tf_op jit(solution)/shard_map/unpack/pallas_call | solution.py:184
  124.6 0.3 collective-permute-done.2
  125.0 0.0 copy-start.4
  125.0 0.5 slice_bitcast_fusion
  125.5 0.1 copy-done.4
  (15 shorter events, 0.1 us)
Async XLA Ops:
  3.3 27.3 %all-to-all-start = ((bf16[32,16,1152]{2,1,0:T(8,128)(2,1)}), bf16[32,16,1152]{2,1,0:T(8,128)(2,1)S(1)}, u32[]{:S(2)}, u32[]{:S(2)}) async-start(bf16[32,16,1152]{2,1,0:T(8,128)(2,1)} %pack.2), calls=%async_computation | async-start | bytes 2359296 | tf_op jit(solution)/shard_map/all_to_all | solution.py:655
  25.8 9.3 %copy-start.5 = (f32[1,3,1152]{2,0,1:T(1,128)S(1)}, f32[1,3,1152]{2,0,1:T(1,128)}, u32[]{:S(2)}) copy-start(f32[1,3,1152]{2,0,1:T(1,128)} %param.12) | copy-start | bytes 41476
  30.5 4.6 %copy-start.3 = (bf16[32,16,1152]{2,1,0:T(8,128)(2,1)}, bf16[32,16,1152]{2,1,0:T(8,128)(2,1)S(1)}, u32[]{:S(2)}) copy-start(bf16[32,16,1152]{2,1,0:T(8,128)(2,1)S(1)} %all-to-all-done.in_hbm) | copy-start | bytes 3538948
  30.5 25.1 %all-to-all-start.2 = ((bf16[32,16,1152]{2,1,0:T(8,128)(2,1)}), bf16[32,16,1152]{2,1,0:T(8,128)(2,1)S(1)}, u32[]{:S(2)}, u32[]{:S(2)}) async-start(bf16[32,16,1152]{2,1,0:T(8,128)(2,1)} %pack.3), calls=%async_computation.2 | async-start | bytes 2359296 | tf_op jit(solution)/shard_map/all_to_all | solution.py:655
  55.6 1.0 copy-start.2
  56.6 26.4 %all-to-all-start.1 = ((bf16[32,16,1152]{2,1,0:T(8,128)(2,1)}), bf16[32,16,1152]{2,1,0:T(8,128)(2,1)S(1)}, u32[]{:S(2)}, u32[]{:S(2)}) async-start(bf16[32,16,1152]{2,1,0:T(8,128)(2,1)} %get-tuple-element.15), calls=%async_computation.1 | async-start | bytes 2359296 | tf_op jit(solution)/shard_map/all_to_all | solution.py:655
  83.1 1.0 copy-start
  116.6 5.0 %copy-start.1 = (bf16[32,24,1152]{2,1,0:T(8,128)(2,1)}, bf16[32,24,1152]{2,1,0:T(8,128)(2,1)S(1)}, u32[]{:S(2)}) copy-start(bf16[32,24,1152]{2,1,0:T(8,128)(2,1)S(1)} %all_to_all.20.second_ref) | copy-start | bytes 5308420
  116.8 7.9 %collective-permute-start.1 = (f32[4,1152]{1,0:T(4,128)S(1)}, f32[4,1152]{1,0:T(4,128)S(1)}, u32[]{:S(2)}, u32[]{:S(2)}) collective-permute-start(f32[4,1152]{1,0:T(4,128)S(1)} %slice_add_fusion), channel_id=1, source_target_pairs={{0,2},{1,3},{2,0},{3,1},{4,6},{5,7},{6,4},{7,5},{8,10},{9,11},{10,... | collective-permute-start | bytes 55304 | tf_op jit(solution)/shard_map/ppermute | solution.py:644
  120.0 5.0 %collective-permute-start.2 = (f32[4,1152]{1,0:T(4,128)S(1)}, f32[4,1152]{1,0:T(4,128)S(1)}, u32[]{:S(2)}, u32[]{:S(2)}) collective-permute-start(f32[4,1152]{1,0:T(4,128)S(1)} %slice_add_fusion), channel_id=1, source_target_pairs={{0,3},{1,2},{2,1},{3,0},{4,7},{5,6},{6,5},{7,4},{8,11},{9,10},{10,... | collective-permute-start | bytes 55304 | tf_op jit(solution)/shard_map/ppermute | solution.py:644
  121.1 3.9 %collective-permute-start = (f32[4,1152]{1,0:T(4,128)S(1)}, f32[4,1152]{1,0:T(4,128)S(1)}, u32[]{:S(2)}, u32[]{:S(2)}) collective-permute-start(f32[4,1152]{1,0:T(4,128)S(1)} %slice_add_fusion), channel_id=1, source_target_pairs={{0,1},{1,0},{2,3},{3,2},{4,5},{5,4},{6,7},{7,6},{8,9},{9,8},{10,11... | collective-permute-start | bytes 55304 | tf_op jit(solution)/shard_map/ppermute | solution.py:644
  125.0 0.6 copy-start.4

commit v5 on v4

--- a/solution.py
+++ b/solution.py
@@ -29,7 +29,7 @@
 TILES = D // LANES
 ROWS_IN = 16
 SUMS = 8
-VMEM = 56 * 1024 * 1024
+MIB = 1024 * 1024
 NN = (((1,), (0,)), ((), ()))
 NT = (((1,), (1,)), ((), ()))
 TN = (((0,), (0,)), ((), ()))
@@ -105,7 +105,7 @@
             jax.ShapeDtypeStruct((D, D), BF16),
         ],
         scratch_shapes=[pltpu.VMEM((4, 384, 256), BF16), pltpu.VMEM((D, REST), BF16)],
-        compiler_params=pltpu.CompilerParams(vmem_limit_bytes=VMEM),
+        compiler_params=pltpu.CompilerParams(vmem_limit_bytes=60 * MIB),
         cost_estimate=pl.CostEstimate(
             flops=2 * D * D * 1600, bytes_accessed=16 * D * D, transcendentals=0
         ),
@@ -143,7 +143,7 @@
         in_specs=[spec, spec] + [pl.BlockSpec(memory_space=pl.ANY)] * len(after),
         out_specs=pl.BlockSpec((ranks // steps, ROWS_IN, width), lambda i: (i, 0, 0)),
         out_shape=jax.ShapeDtypeStruct((ranks, ROWS_IN, width), BF16),
-        compiler_params=pltpu.CompilerParams(vmem_limit_bytes=VMEM),
+        compiler_params=pltpu.CompilerParams(vmem_limit_bytes=60 * MIB),
         cost_estimate=pl.CostEstimate(flops=4_000_000, bytes_accessed=3_600_000, transcendentals=0),
         name="pack",
     )(latents, cotangent, *after)
@@ -161,6 +161,7 @@
         out_specs=any_space,
         out_shape=jax.ShapeDtypeStruct(value.shape, value.dtype),
         input_output_aliases={0: 0},
+        compiler_params=pltpu.CompilerParams(vmem_limit_bytes=MIB),
         name="tie",
     )(value, other)
 
@@ -190,7 +191,7 @@
         ],
         out_specs=[spec, spec],
         out_shape=[out, out],
-        compiler_params=pltpu.CompilerParams(vmem_limit_bytes=VMEM),
+        compiler_params=pltpu.CompilerParams(vmem_limit_bytes=50 * MIB),
         cost_estimate=pl.CostEstimate(flops=4_000_000, bytes_accessed=5_000_000, transcendentals=0),
         name="unpack",
     )(first, second)
@@ -298,9 +299,8 @@
     wqkv_hbm,
     wout_hbm,
     before_hbm,
-    out_hbm,
+    out_ref,
     sums,
-    out_ref,
     table_ref,
     clip_ref,
     q_gain_ref,
@@ -574,9 +574,6 @@
             rows = jnp.broadcast_to(sent[None, :, cols], (ranks, SUMS, LANES))
             block = jnp.concatenate([block, rows], 1)
         out_ref[:, :, cols] = block.astype(BF16)
-    leave = pltpu.make_async_copy(out_ref, out_hbm, sems.at[8])
-    leave.start()
-    leave.wait()
 
 
 def run_sub_block(last, frame_counts, arrived, modulation, gains, weights, before):
@@ -586,7 +583,6 @@
     vmem = pl.BlockSpec(memory_space=pltpu.VMEM)
     sent = ROWS_IN + SUMS if last else ROWS_IN
     scratch = [
-        pltpu.VMEM((ranks, sent, D), BF16),
         pltpu.VMEM((3, D), F32),
         pltpu.VMEM((3, D), F32),
         pltpu.VMEM((1, HEAD), F32),
@@ -595,7 +591,7 @@
         pltpu.VMEM((ranks, ROWS_IN, D), BF16),
         pltpu.VMEM((D, 3 * D), BF16),
         pltpu.VMEM((D, D), BF16),
-        pltpu.SemaphoreType.DMA((9,)),
+        pltpu.SemaphoreType.DMA((8,)),
         pltpu.VMEM((TILES, ranks * ROWS_IN, LANES), F32),
         pltpu.VMEM(tok, F32),
         pltpu.VMEM(tok, F32),
@@ -624,13 +620,13 @@
         functools.partial(sub_block, last),
         in_specs=[pl.BlockSpec(memory_space=pltpu.SMEM)]
         + [any_space] * 8,
-        out_specs=[any_space, vmem],
+        out_specs=[vmem, vmem],
         out_shape=[
             jax.ShapeDtypeStruct((ranks, sent, D), BF16),
             jax.ShapeDtypeStruct((8, D), F32),
         ],
         scratch_shapes=scratch,
-        compiler_params=pltpu.CompilerParams(vmem_limit_bytes=VMEM),
+        compiler_params=pltpu.CompilerParams(vmem_limit_bytes=50 * MIB),
         cost_estimate=pl.CostEstimate(
             flops=12_000_000_000, bytes_accessed=20_000_000, transcendentals=0
         ),

time: 126 us -> 122 us (0.968)
  Pallas kernels: 58.1 us -> 54.1 us
  waiting for transfers between devices: 5.05 us -> 6.82 us
    pallas_call x2, Pallas kernels: 38.2 us -> 35.4 us  [run_sub_block(): pl.pallas_call(functools.partial(sub_block, last), in_specs=[pl.BlockSpec...]
    unnamed x13 -> x15, local copies, waits for them, and re-layouts: 2.74 us -> 2.38 us
  transfers between devices with their start and end apart: 6 -> 6, of which waited for: 2 -> 3; matrix products, arithmetic and copies ran while one was open for 1% -> 1% of each run, Pallas kernels for 44% -> 42%
where the time goes in v5:
time: 122 us
  Pallas kernels  54.1 us (44%)
  blocking collectives  31.7 us (26%)
  starting transfers between devices  23.9 us (20%)
  waiting for transfers between devices  6.82 us (6%)
  local copies, waits for them, and re-layouts  3.51 us (3%)
  between operations  1.43 us (1%)
    pallas_call x2, Pallas kernels, run_sub_block(): pl.pallas_call(functools.partial(sub_block, last), in_specs=[pl.BlockSpec...  35.4 us
    all_to_all x1, blocking collectives, exchange(): return lax.all_to_all(rows, 'seq', split_axis=0, concat_axis=0, tiled=True)  31.7 us
    all_to_all x3, starting transfers between devices, exchange(): return lax.all_to_all(rows, 'seq', split_axis=0, concat_axis=0, tiled=True)  19.6 us
    pallas_call x1, Pallas kernels, split_weights(): pl.pallas_call(split_weights_kernel, grid=(steps,), in_specs=[pl.BlockSpe...  11.7 us
    all_to_all x3, waiting for transfers between devices, exchange(): return lax.all_to_all(rows, 'seq', split_axis=0, concat_axis=0, tiled=True)  5.34 us
    pallas_call x2, Pallas kernels, pack(): pl.pallas_call(functools.partial(pack_kernel, chunk), grid=(steps,), in_s...  5.25 us
    ppermute x3, starting transfers between devices, sum_clips(): lax.ppermute(value, 'dp', [(i, i ^ step) for i in range(clips)])  4.32 us
  transfers between devices with their start and end apart: 6, of which 3 were waited for; matrix products, arithmetic and copies ran while one was open for 1% of the time, Pallas kernels for 42%

profile of v5, /device:TPU:0, one launch (start us, length us, event | category | flops | bytes accessed | tf_op | source)
XLA Modules:
  0.0 121.6 jit_solution(18350260488207629631)
XLA Ops:
  0.6 2.6 %pack.2 = bf16[32,16,1152]{2,1,0:T(8,128)(2,1)} custom-call(bf16[1,2,256,1152]{3,2,1,0:T(8,128)(2,1)} %lat_ref.3, bf16[1,2,256,1152]{3,2,1,0:T(8,128)(2,1)} %cot_ref.3), custom_call_target="tpu_custom_call" | custom-call | flops 4000000 | bytes 3600000 | tf_op jit(solution)/shard_map/pack/pallas_call | solution.py:140
  3.3 8.2 %all-to-all-start = ((bf16[32,16,1152]{2,1,0:T(8,128)(2,1)}), bf16[32,16,1152]{2,1,0:T(8,128)(2,1)S(1)}, u32[]{:S(2)}, u32[]{:S(2)}) async-start(bf16[32,16,1152]{2,1,0:T(8,128)(2,1)} %pack.2), calls=%async_computation | async-start | bytes 2359296 | tf_op jit(solution)/shard_map/all_to_all | solution.py:651
  11.5 11.7 %split_weights.1 = (bf16[1152,3456]{1,0:T(8,128)(2,1)}, bf16[1152,1152]{1,0:T(8,128)(2,1)}) custom-call(bf16[1152,3456]{1,0:T(8,128)(2,1)} %qkv_ref.1, bf16[1152,1152]{1,0:T(8,128)(2,1)} %out_ref.1), custom_call_target="tpu_custom_call" | custom-call | flops 4246732800 | bytes 21233664 | tf_op jit(solution)/shard_map/split_weights/pallas_call | solution.py:92
  23.2 2.6 %pack.3 = bf16[32,16,1152]{2,1,0:T(8,128)(2,1)} custom-call(bf16[1,2,256,1152]{3,2,1,0:T(8,128)(2,1)} %lat_ref.3, bf16[1,2,256,1152]{3,2,1,0:T(8,128)(2,1)} %cot_ref.3, bf16[1152,1152]{1,0:T(8,128)(2,1)} %get-tuple-element.14.wout_hbm.refs_0_), custom_call_target="tpu_custom_call" | custom-call | flops 4000000 | bytes 3600000 | tf_op jit(solution)/shard_map/pack/pallas_call | solution.py:140
  25.9 0.0 copy-start.4
  25.9 4.7 %all-to-all-done.in_hbm = bf16[32,16,1152]{2,1,0:T(8,128)(2,1)S(1)} async-done(((bf16[32,16,1152]{2,1,0:T(8,128)(2,1)}), bf16[32,16,1152]{2,1,0:T(8,128)(2,1)S(1)}, u32[]{:S(2)}, u32[]{:S(2)}) %all-to-all-start) | async-done | bytes 1179680 | tf_op jit(solution)/shard_map/all_to_all | solution.py:651
  30.5 3.9 %all-to-all-start.2 = ((bf16[32,16,1152]{2,1,0:T(8,128)(2,1)}), bf16[32,16,1152]{2,1,0:T(8,128)(2,1)S(1)}, u32[]{:S(2)}, u32[]{:S(2)}) async-start(bf16[32,16,1152]{2,1,0:T(8,128)(2,1)} %pack.3), calls=%async_computation.2 | async-start | bytes 2359296 | tf_op jit(solution)/shard_map/all_to_all | solution.py:651
  35.2 18.3 %sub_block.2 = (bf16[32,16,1152]{2,1,0:T(8,128)(2,1)}, f32[8,1152]{1,0:T(8,128)S(1)}) custom-call(s32[1]{0:T(128)S(6)} %copy.20.count_ref, bf16[32,16,1152]{2,1,0:T(8,128)(2,1)S(1)} %all-to-all-done.in_hbm, f32[3,1152]{1,0:T(4,128)S(1)} %copy-done.2, f32[3,1152]{1,0:T(4,128)S(1)} %bitcast.11, f32[1,72]{1,0:T(1,128)S(1)} %bitcast.13, f32[1,72]{1,0:T(1,128)S(1)} %bitcast.15, ...), custom_call_target="tpu_custom_call" | custom-call | flops 12000000000 | bytes 20000000 | tf_op jit(solution)/shard_map/sub_block/pallas_call | solution.py:619
  53.5 0.0 copy-start
  53.5 1.0 copy-done
  54.5 7.4 %all-to-all-start.1 = ((bf16[32,16,1152]{2,1,0:T(8,128)(2,1)}), bf16[32,16,1152]{2,1,0:T(8,128)(2,1)S(1)}, u32[]{:S(2)}, u32[]{:S(2)}) async-start(bf16[32,16,1152]{2,1,0:T(8,128)(2,1)} %get-tuple-element.15), calls=%async_computation.1 | async-start | bytes 2359296 | tf_op jit(solution)/shard_map/all_to_all | solution.py:651
  61.9 1.3 %copy-done.1 = bf16[32,16,1152]{2,1,0:T(8,128)(2,1)S(1)} copy-done((bf16[32,16,1152]{2,1,0:T(8,128)(2,1)S(1)}, bf16[32,16,1152]{2,1,0:T(8,128)(2,1)}, u32[]{:S(2)}) %copy-start.1) | copy-done | bytes 1179672
  63.2 17.1 %sub_block.3 = (bf16[32,24,1152]{2,1,0:T(8,128)(2,1)S(1)}, f32[8,1152]{1,0:T(8,128)}) custom-call(s32[1]{0:T(128)S(6)} %copy.20.count_ref, bf16[32,16,1152]{2,1,0:T(8,128)(2,1)S(1)} %copy-done.1, f32[3,1152]{1,0:T(4,128)S(1)} %copy-done.2, f32[3,1152]{1,0:T(4,128)S(1)} %bitcast.12, f32[1,72]{1,0:T(1,128)S(1)} %bitcast.14, f32[1,72]{1,0:T(1,128)S(1)} %bitcast.16, ...), custom_call_target="tpu_custom_call" | custom-call | flops 12000000000 | bytes 20000000 | tf_op jit(solution)/shard_map/sub_block/pallas_call | solution.py:619
  80.3 0.7 all-to-all-done.1.other_ref.first_ref
  80.9 31.7 %all_to_all.20.second_ref = bf16[32,24,1152]{2,1,0:T(8,128)(2,1)S(1)} all-to-all(bf16[32,24,1152]{2,1,0:T(8,128)(2,1)S(1)} %tie.1), channel_id=1, replica_groups=mesh['seq'=32,'dp'=4] {'seq'}, dimensions={0} | all-to-all | bytes 3538944 | tf_op jit(solution)/shard_map/all_to_all | solution.py:651
  112.6 0.1 convert_reduce_fusion
  112.8 3.3 %collective-permute-start.1 = (f32[4,1152]{1,0:T(4,128)S(1)}, f32[4,1152]{1,0:T(4,128)S(1)}, u32[]{:S(2)}, u32[]{:S(2)}) collective-permute-start(f32[4,1152]{1,0:T(4,128)S(1)} %slice_add_fusion), channel_id=1, source_target_pairs={{0,2},{1,3},{2,0},{3,1},{4,6},{5,7},{6,4},{7,5},{8,10},{9,11},{10,... | collective-permute-start | bytes 55304 | tf_op jit(solution)/shard_map/ppermute | solution.py:640
  116.0 1.1 collective-permute-start.2
  117.1 0.6 broadcast_in_dim.15
  117.7 1.8 %unpack.1 = (bf16[1,2,256,1152]{3,2,1,0:T(8,128)(2,1)}, bf16[1,2,256,1152]{3,2,1,0:T(8,128)(2,1)}) custom-call(bf16[32,16,1152]{2,1,0:T(8,128)(2,1)S(1)} %all-to-all-done.1.other_ref.first_ref, bf16[32,24,1152]{2,1,0:T(8,128)(2,1)S(1)} %all_to_all.20.second_ref), custom_call_target="tpu_custom_call" | custom-call | flops 4000000 | bytes 5000000 | tf_op jit(solution)/shard_map/unpack/pallas_call | solution.py:185
  119.5 1.5 %collective-permute-done.2 = f32[4,1152]{1,0:T(4,128)S(1)} collective-permute-done((f32[4,1152]{1,0:T(4,128)S(1)}, f32[4,1152]{1,0:T(4,128)S(1)}, u32[]{:S(2)}, u32[]{:S(2)}) %collective-permute-start.2) | collective-permute-done | bytes 18464 | tf_op jit(solution)/shard_map/ppermute | solution.py:640
  121.0 0.0 copy-start.5
  121.0 0.5 slice_bitcast_fusion
  121.5 0.1 copy-done.5
  (17 shorter events, 0.1 us)
Async XLA Ops:
  3.3 27.3 %all-to-all-start = ((bf16[32,16,1152]{2,1,0:T(8,128)(2,1)}), bf16[32,16,1152]{2,1,0:T(8,128)(2,1)S(1)}, u32[]{:S(2)}, u32[]{:S(2)}) async-start(bf16[32,16,1152]{2,1,0:T(8,128)(2,1)} %pack.2), calls=%async_computation | async-start | bytes 2359296 | tf_op jit(solution)/shard_map/all_to_all | solution.py:651
  25.9 9.3 %copy-start.6 = (f32[1,3,1152]{2,0,1:T(1,128)S(1)}, f32[1,3,1152]{2,0,1:T(1,128)}, u32[]{:S(2)}) copy-start(f32[1,3,1152]{2,0,1:T(1,128)} %param.12) | copy-start | bytes 41476
  25.9 9.3 %copy-start.2 = (f32[3,1152]{1,0:T(4,128)S(1)}, f32[3,1152]{1,0:T(4,128)}, u32[]{:S(2)}) copy-start(f32[3,1152]{1,0:T(4,128)} %table_hbm.3) | copy-start | bytes 41476
  25.9 9.3 %copy-start.3 = (f32[72]{0:T(128)S(1)}, f32[72]{0:T(128)}, u32[]{:S(2)}) copy-start(f32[72]{0:T(128)} %param.13) | copy-start | bytes 868
  25.9 9.3 %copy-start.4 = (f32[72]{0:T(128)S(1)}, f32[72]{0:T(128)}, u32[]{:S(2)}) copy-start(f32[72]{0:T(128)} %param.14) | copy-start | bytes 868
  30.5 23.0 %all-to-all-start.2 = ((bf16[32,16,1152]{2,1,0:T(8,128)(2,1)}), bf16[32,16,1152]{2,1,0:T(8,128)(2,1)S(1)}, u32[]{:S(2)}, u32[]{:S(2)}) async-start(bf16[32,16,1152]{2,1,0:T(8,128)(2,1)} %pack.3), calls=%async_computation.2 | async-start | bytes 2359296 | tf_op jit(solution)/shard_map/all_to_all | solution.py:651
  53.5 1.0 copy-start
  54.5 26.4 %all-to-all-start.1 = ((bf16[32,16,1152]{2,1,0:T(8,128)(2,1)}), bf16[32,16,1152]{2,1,0:T(8,128)(2,1)S(1)}, u32[]{:S(2)}, u32[]{:S(2)}) async-start(bf16[32,16,1152]{2,1,0:T(8,128)(2,1)} %get-tuple-element.15), calls=%async_computation.1 | async-start | bytes 2359296 | tf_op jit(solution)/shard_map/all_to_all | solution.py:651
  61.9 1.3 %copy-start.1 = (bf16[32,16,1152]{2,1,0:T(8,128)(2,1)S(1)}, bf16[32,16,1152]{2,1,0:T(8,128)(2,1)}, u32[]{:S(2)}) copy-start(bf16[32,16,1152]{2,1,0:T(8,128)(2,1)} %copy-done) | copy-start | bytes 3538948
  112.8 6.8 %collective-permute-start.1 = (f32[4,1152]{1,0:T(4,128)S(1)}, f32[4,1152]{1,0:T(4,128)S(1)}, u32[]{:S(2)}, u32[]{:S(2)}) collective-permute-start(f32[4,1152]{1,0:T(4,128)S(1)} %slice_add_fusion), channel_id=1, source_target_pairs={{0,2},{1,3},{2,0},{3,1},{4,6},{5,7},{6,4},{7,5},{8,10},{9,11},{10,... | collective-permute-start | bytes 55304 | tf_op jit(solution)/shard_map/ppermute | solution.py:640
  116.0 5.0 %collective-permute-start.2 = (f32[4,1152]{1,0:T(4,128)S(1)}, f32[4,1152]{1,0:T(4,128)S(1)}, u32[]{:S(2)}, u32[]{:S(2)}) collective-permute-start(f32[4,1152]{1,0:T(4,128)S(1)} %slice_add_fusion), channel_id=1, source_target_pairs={{0,3},{1,2},{2,1},{3,0},{4,7},{5,6},{6,5},{7,4},{8,11},{9,10},{10,... | collective-permute-start | bytes 55304 | tf_op jit(solution)/shard_map/ppermute | solution.py:640
  117.1 3.9 %collective-permute-start = (f32[4,1152]{1,0:T(4,128)S(1)}, f32[4,1152]{1,0:T(4,128)S(1)}, u32[]{:S(2)}, u32[]{:S(2)}) collective-permute-start(f32[4,1152]{1,0:T(4,128)S(1)} %slice_add_fusion), channel_id=1, source_target_pairs={{0,1},{1,0},{2,3},{3,2},{4,5},{5,4},{6,7},{7,6},{8,9},{9,8},{10,11... | collective-permute-start | bytes 55304 | tf_op jit(solution)/shard_map/ppermute | solution.py:640
  121.0 0.6 copy-start.5

commit v6 on v5

--- a/solution.py
+++ b/solution.py
@@ -335,6 +335,7 @@
     gain_ref,
 ):
     ranks = in_ref.shape[0]
+    used = ranks * ROWS_IN
     att, gn = gy, normed
     load_qkv = pltpu.make_async_copy(wqkv_hbm, wqkv, sems.at[0])
     load_out = pltpu.make_async_copy(wout_hbm, wout, sems.at[1])
@@ -384,7 +385,7 @@
 
     load_in.wait()
     for c, cols in enumerate(lane_tiles()):
-        frames[c] = in_ref[:, :, cols].reshape(ranks * ROWS_IN, LANES).astype(F32)
+        frames[c, :used] = in_ref[:, :, cols].reshape(used, LANES).astype(F32)
 
     def arrive(p):
         rows = position_rows(p)
@@ -569,7 +570,7 @@
         high, low, _ = terms(jnp.concatenate([total[:3], gains], 0))
         sent = jnp.concatenate([high.astype(F32), low.astype(F32)], 0)
     for c, cols in enumerate(lane_tiles()):
-        block = frames[c].reshape(ranks, ROWS_IN, LANES)
+        block = frames[c, :used].reshape(ranks, ROWS_IN, LANES)
         if last:
             rows = jnp.broadcast_to(sent[None, :, cols], (ranks, SUMS, LANES))
             block = jnp.concatenate([block, rows], 1)
@@ -592,7 +593,7 @@
         pltpu.VMEM((D, 3 * D), BF16),
         pltpu.VMEM((D, D), BF16),
         pltpu.SemaphoreType.DMA((8,)),
-        pltpu.VMEM((TILES, ranks * ROWS_IN, LANES), F32),
+        pltpu.VMEM((TILES, (ranks + 1) * ROWS_IN, LANES), F32),
         pltpu.VMEM(tok, F32),
         pltpu.VMEM(tok, F32),
         pltpu.VMEM((TOK, LANES), F32),

time: 122 us -> 122 us (level)
  no operation moved by 1% of the time
where the time goes in v6:
time: 122 us
  Pallas kernels  54.2 us (44%)
  blocking collectives  31.7 us (26%)
  starting transfers between devices  23.9 us (20%)
  waiting for transfers between devices  6.8 us (6%)
  local copies, waits for them, and re-layouts  3.51 us (3%)
  between operations  1.42 us (1%)
    pallas_call x2, Pallas kernels, run_sub_block(): pl.pallas_call(functools.partial(sub_block, last), in_specs=[pl.BlockSpec...  35.4 us
    all_to_all x1, blocking collectives, exchange(): return lax.all_to_all(rows, 'seq', split_axis=0, concat_axis=0, tiled=True)  31.7 us
    all_to_all x3, starting transfers between devices, exchange(): return lax.all_to_all(rows, 'seq', split_axis=0, concat_axis=0, tiled=True)  19.6 us
    pallas_call x1, Pallas kernels, split_weights(): pl.pallas_call(split_weights_kernel, grid=(steps,), in_specs=[pl.BlockSpe...  11.7 us
    all_to_all x3, waiting for transfers between devices, exchange(): return lax.all_to_all(rows, 'seq', split_axis=0, concat_axis=0, tiled=True)  5.32 us
    pallas_call x2, Pallas kernels, pack(): pl.pallas_call(functools.partial(pack_kernel, chunk), grid=(steps,), in_s...  5.25 us
    ppermute x3, starting transfers between devices, sum_clips(): lax.ppermute(value, 'dp', [(i, i ^ step) for i in range(clips)])  4.33 us
  transfers between devices with their start and end apart: 6, of which 3 were waited for; matrix products, arithmetic and copies ran while one was open for 1% of the time, Pallas kernels for 42%

profile of v6, /device:TPU:0, one launch (start us, length us, event | category | flops | bytes accessed | tf_op | source)
XLA Modules:
  0.0 121.6 jit_solution(12869527164672804245)
XLA Ops:
  0.6 2.6 %pack.2 = bf16[32,16,1152]{2,1,0:T(8,128)(2,1)} custom-call(bf16[1,2,256,1152]{3,2,1,0:T(8,128)(2,1)} %lat_ref.3, bf16[1,2,256,1152]{3,2,1,0:T(8,128)(2,1)} %cot_ref.3), custom_call_target="tpu_custom_call" | custom-call | flops 4000000 | bytes 3600000 | tf_op jit(solution)/shard_map/pack/pallas_call | solution.py:140
  3.3 8.2 %all-to-all-start = ((bf16[32,16,1152]{2,1,0:T(8,128)(2,1)}), bf16[32,16,1152]{2,1,0:T(8,128)(2,1)S(1)}, u32[]{:S(2)}, u32[]{:S(2)}) async-start(bf16[32,16,1152]{2,1,0:T(8,128)(2,1)} %pack.2), calls=%async_computation | async-start | bytes 2359296 | tf_op jit(solution)/shard_map/all_to_all | solution.py:652
  11.5 11.7 %split_weights.1 = (bf16[1152,3456]{1,0:T(8,128)(2,1)}, bf16[1152,1152]{1,0:T(8,128)(2,1)}) custom-call(bf16[1152,3456]{1,0:T(8,128)(2,1)} %qkv_ref.1, bf16[1152,1152]{1,0:T(8,128)(2,1)} %out_ref.1), custom_call_target="tpu_custom_call" | custom-call | flops 4246732800 | bytes 21233664 | tf_op jit(solution)/shard_map/split_weights/pallas_call | solution.py:92
  23.2 2.6 %pack.3 = bf16[32,16,1152]{2,1,0:T(8,128)(2,1)} custom-call(bf16[1,2,256,1152]{3,2,1,0:T(8,128)(2,1)} %lat_ref.3, bf16[1,2,256,1152]{3,2,1,0:T(8,128)(2,1)} %cot_ref.3, bf16[1152,1152]{1,0:T(8,128)(2,1)} %get-tuple-element.14.wout_hbm.refs_0_), custom_call_target="tpu_custom_call" | custom-call | flops 4000000 | bytes 3600000 | tf_op jit(solution)/shard_map/pack/pallas_call | solution.py:140
  25.9 4.7 %all-to-all-done.in_hbm = bf16[32,16,1152]{2,1,0:T(8,128)(2,1)S(1)} async-done(((bf16[32,16,1152]{2,1,0:T(8,128)(2,1)}), bf16[32,16,1152]{2,1,0:T(8,128)(2,1)S(1)}, u32[]{:S(2)}, u32[]{:S(2)}) %all-to-all-start) | async-done | bytes 1179680 | tf_op jit(solution)/shard_map/all_to_all | solution.py:652
  30.5 3.9 %all-to-all-start.2 = ((bf16[32,16,1152]{2,1,0:T(8,128)(2,1)}), bf16[32,16,1152]{2,1,0:T(8,128)(2,1)S(1)}, u32[]{:S(2)}, u32[]{:S(2)}) async-start(bf16[32,16,1152]{2,1,0:T(8,128)(2,1)} %pack.3), calls=%async_computation.2 | async-start | bytes 2359296 | tf_op jit(solution)/shard_map/all_to_all | solution.py:652
  35.2 18.3 %sub_block.2 = (bf16[32,16,1152]{2,1,0:T(8,128)(2,1)}, f32[8,1152]{1,0:T(8,128)S(1)}) custom-call(s32[1]{0:T(128)S(6)} %copy.20.count_ref, bf16[32,16,1152]{2,1,0:T(8,128)(2,1)S(1)} %all-to-all-done.in_hbm, f32[3,1152]{1,0:T(4,128)S(1)} %copy-done.2, f32[3,1152]{1,0:T(4,128)S(1)} %bitcast.11, f32[1,72]{1,0:T(1,128)S(1)} %bitcast.13, f32[1,72]{1,0:T(1,128)S(1)} %bitcast.15, ...), custom_call_target="tpu_custom_call" | custom-call | flops 12000000000 | bytes 20000000 | tf_op jit(solution)/shard_map/sub_block/pallas_call | solution.py:620
  53.5 0.0 all-to-all-done.2.in_hbm
  53.5 0.0 copy-start
  53.5 1.0 copy-done
  54.5 7.4 %all-to-all-start.1 = ((bf16[32,16,1152]{2,1,0:T(8,128)(2,1)}), bf16[32,16,1152]{2,1,0:T(8,128)(2,1)S(1)}, u32[]{:S(2)}, u32[]{:S(2)}) async-start(bf16[32,16,1152]{2,1,0:T(8,128)(2,1)} %get-tuple-element.15), calls=%async_computation.1 | async-start | bytes 2359296 | tf_op jit(solution)/shard_map/all_to_all | solution.py:652
  61.9 1.3 %copy-done.1 = bf16[32,16,1152]{2,1,0:T(8,128)(2,1)S(1)} copy-done((bf16[32,16,1152]{2,1,0:T(8,128)(2,1)S(1)}, bf16[32,16,1152]{2,1,0:T(8,128)(2,1)}, u32[]{:S(2)}) %copy-start.1) | copy-done | bytes 1179672
  63.2 17.1 %sub_block.3 = (bf16[32,24,1152]{2,1,0:T(8,128)(2,1)S(1)}, f32[8,1152]{1,0:T(8,128)}) custom-call(s32[1]{0:T(128)S(6)} %copy.20.count_ref, bf16[32,16,1152]{2,1,0:T(8,128)(2,1)S(1)} %copy-done.1, f32[3,1152]{1,0:T(4,128)S(1)} %copy-done.2, f32[3,1152]{1,0:T(4,128)S(1)} %bitcast.12, f32[1,72]{1,0:T(1,128)S(1)} %bitcast.14, f32[1,72]{1,0:T(1,128)S(1)} %bitcast.16, ...), custom_call_target="tpu_custom_call" | custom-call | flops 12000000000 | bytes 20000000 | tf_op jit(solution)/shard_map/sub_block/pallas_call | solution.py:620
  80.3 0.6 all-to-all-done.1.other_ref.first_ref
  80.9 31.7 %all_to_all.20.second_ref = bf16[32,24,1152]{2,1,0:T(8,128)(2,1)S(1)} all-to-all(bf16[32,24,1152]{2,1,0:T(8,128)(2,1)S(1)} %tie.1), channel_id=1, replica_groups=mesh['seq'=32,'dp'=4] {'seq'}, dimensions={0} | all-to-all | bytes 3538944 | tf_op jit(solution)/shard_map/all_to_all | solution.py:652
  112.6 0.1 convert_reduce_fusion
  112.7 3.3 %collective-permute-start.1 = (f32[4,1152]{1,0:T(4,128)S(1)}, f32[4,1152]{1,0:T(4,128)S(1)}, u32[]{:S(2)}, u32[]{:S(2)}) collective-permute-start(f32[4,1152]{1,0:T(4,128)S(1)} %slice_add_fusion), channel_id=1, source_target_pairs={{0,2},{1,3},{2,0},{3,1},{4,6},{5,7},{6,4},{7,5},{8,10},{9,11},{10,... | collective-permute-start | bytes 55304 | tf_op jit(solution)/shard_map/ppermute | solution.py:641
  116.0 1.1 collective-permute-start.2
  117.1 0.6 broadcast_in_dim.15
  117.7 1.8 %unpack.1 = (bf16[1,2,256,1152]{3,2,1,0:T(8,128)(2,1)}, bf16[1,2,256,1152]{3,2,1,0:T(8,128)(2,1)}) custom-call(bf16[32,16,1152]{2,1,0:T(8,128)(2,1)S(1)} %all-to-all-done.1.other_ref.first_ref, bf16[32,24,1152]{2,1,0:T(8,128)(2,1)S(1)} %all_to_all.20.second_ref), custom_call_target="tpu_custom_call" | custom-call | flops 4000000 | bytes 5000000 | tf_op jit(solution)/shard_map/unpack/pallas_call | solution.py:185
  119.5 1.5 %collective-permute-done.2 = f32[4,1152]{1,0:T(4,128)S(1)} collective-permute-done((f32[4,1152]{1,0:T(4,128)S(1)}, f32[4,1152]{1,0:T(4,128)S(1)}, u32[]{:S(2)}, u32[]{:S(2)}) %collective-permute-start.2) | collective-permute-done | bytes 18464 | tf_op jit(solution)/shard_map/ppermute | solution.py:641
  121.0 0.0 copy-start.5
  121.0 0.5 slice_bitcast_fusion
  121.5 0.1 copy-done.5
  (17 shorter events, 0.1 us)
Async XLA Ops:
  3.3 27.3 %all-to-all-start = ((bf16[32,16,1152]{2,1,0:T(8,128)(2,1)}), bf16[32,16,1152]{2,1,0:T(8,128)(2,1)S(1)}, u32[]{:S(2)}, u32[]{:S(2)}) async-start(bf16[32,16,1152]{2,1,0:T(8,128)(2,1)} %pack.2), calls=%async_computation | async-start | bytes 2359296 | tf_op jit(solution)/shard_map/all_to_all | solution.py:652
  25.9 9.3 %copy-start.6 = (f32[1,3,1152]{2,0,1:T(1,128)S(1)}, f32[1,3,1152]{2,0,1:T(1,128)}, u32[]{:S(2)}) copy-start(f32[1,3,1152]{2,0,1:T(1,128)} %param.12) | copy-start | bytes 41476
  25.9 9.3 %copy-start.2 = (f32[3,1152]{1,0:T(4,128)S(1)}, f32[3,1152]{1,0:T(4,128)}, u32[]{:S(2)}) copy-start(f32[3,1152]{1,0:T(4,128)} %table_hbm.3) | copy-start | bytes 41476
  25.9 9.3 %copy-start.3 = (f32[72]{0:T(128)S(1)}, f32[72]{0:T(128)}, u32[]{:S(2)}) copy-start(f32[72]{0:T(128)} %param.13) | copy-start | bytes 868
  25.9 9.3 %copy-start.4 = (f32[72]{0:T(128)S(1)}, f32[72]{0:T(128)}, u32[]{:S(2)}) copy-start(f32[72]{0:T(128)} %param.14) | copy-start | bytes 868
  30.5 23.0 %all-to-all-start.2 = ((bf16[32,16,1152]{2,1,0:T(8,128)(2,1)}), bf16[32,16,1152]{2,1,0:T(8,128)(2,1)S(1)}, u32[]{:S(2)}, u32[]{:S(2)}) async-start(bf16[32,16,1152]{2,1,0:T(8,128)(2,1)} %pack.3), calls=%async_computation.2 | async-start | bytes 2359296 | tf_op jit(solution)/shard_map/all_to_all | solution.py:652
  53.5 1.0 copy-start
  54.5 26.4 %all-to-all-start.1 = ((bf16[32,16,1152]{2,1,0:T(8,128)(2,1)}), bf16[32,16,1152]{2,1,0:T(8,128)(2,1)S(1)}, u32[]{:S(2)}, u32[]{:S(2)}) async-start(bf16[32,16,1152]{2,1,0:T(8,128)(2,1)} %get-tuple-element.15), calls=%async_computation.1 | async-start | bytes 2359296 | tf_op jit(solution)/shard_map/all_to_all | solution.py:652
  61.9 1.3 %copy-start.1 = (bf16[32,16,1152]{2,1,0:T(8,128)(2,1)S(1)}, bf16[32,16,1152]{2,1,0:T(8,128)(2,1)}, u32[]{:S(2)}) copy-start(bf16[32,16,1152]{2,1,0:T(8,128)(2,1)} %copy-done) | copy-start | bytes 3538948
  112.7 6.8 %collective-permute-start.1 = (f32[4,1152]{1,0:T(4,128)S(1)}, f32[4,1152]{1,0:T(4,128)S(1)}, u32[]{:S(2)}, u32[]{:S(2)}) collective-permute-start(f32[4,1152]{1,0:T(4,128)S(1)} %slice_add_fusion), channel_id=1, source_target_pairs={{0,2},{1,3},{2,0},{3,1},{4,6},{5,7},{6,4},{7,5},{8,10},{9,11},{10,... | collective-permute-start | bytes 55304 | tf_op jit(solution)/shard_map/ppermute | solution.py:641
  116.0 5.0 %collective-permute-start.2 = (f32[4,1152]{1,0:T(4,128)S(1)}, f32[4,1152]{1,0:T(4,128)S(1)}, u32[]{:S(2)}, u32[]{:S(2)}) collective-permute-start(f32[4,1152]{1,0:T(4,128)S(1)} %slice_add_fusion), channel_id=1, source_target_pairs={{0,3},{1,2},{2,1},{3,0},{4,7},{5,6},{6,5},{7,4},{8,11},{9,10},{10,... | collective-permute-start | bytes 55304 | tf_op jit(solution)/shard_map/ppermute | solution.py:641
  117.1 3.9 %collective-permute-start = (f32[4,1152]{1,0:T(4,128)S(1)}, f32[4,1152]{1,0:T(4,128)S(1)}, u32[]{:S(2)}, u32[]{:S(2)}) collective-permute-start(f32[4,1152]{1,0:T(4,128)S(1)} %slice_add_fusion), channel_id=1, source_target_pairs={{0,1},{1,0},{2,3},{3,2},{4,5},{5,4},{6,7},{7,6},{8,9},{9,8},{10,11... | collective-permute-start | bytes 55304 | tf_op jit(solution)/shard_map/ppermute | solution.py:641
  121.0 0.6 copy-start.5
